TPU v7x, 32 devices: a whole 2x2x4 slice. The times are simulated.
32 devices in a mesh: batch: 4 (over y, core), blk: 8 (over z, x).
Axes of the slice: x: 2, y: 2, z: 4, core: 2. Of those that a mesh axis runs over, the one named last changes fastest.
Arguments:
- inputs: bfloat16 [12, 2048, 1024], P('batch', 'blk'), may hold values from -6 to 6
- ln_attn: float32 [1024], replicated, may hold values from 0.1 to 1.9
- w_query: bfloat16 [1024, 1024], replicated, may hold values from -0.1875 to 0.1875
- w_key: bfloat16 [1024, 1024], replicated, may hold values from -0.1875 to 0.1875
- w_value: bfloat16 [1024, 1024], replicated, may hold values from -0.1875 to 0.1875
- w_out: bfloat16 [1024, 1024], replicated, may hold values from -0.1875 to 0.1875
- head_scale: float32 [16], replicated, may hold values from 0.5 to 2
- ln_post: float32 [1024], replicated, may hold values from 0.1 to 1.9
- ln_ffn: float32 [1024], replicated, may hold values from 0.1 to 1.9
- w_fc1: bfloat16 [1024, 4096], replicated, may hold values from -0.1875 to 0.1875
- ln_mid: float32 [4096], replicated, may hold values from 0.1 to 1.9
- w_fc2: bfloat16 [4096, 1024], replicated, may hold values from -0.09375 to 0.09375
- offsets: int32 [12, 4], P('batch'), may hold values from 0 to 2047, as said below
- cotangent: bfloat16 [12, 2048, 1024], P('batch', 'blk'), may hold values from -6 to 6
Outputs:
- layer_out: bfloat16 [12, 2048, 1024], P('batch', 'blk')
- grad_inputs: float32 [12, 2048, 1024], P('batch', 'blk')
- grad_ln_attn: float32 [1024], P('blk')
- grad_w_query: float32 [1024, 1024], P('blk')
- grad_w_key: float32 [1024, 1024], P('blk')
- grad_w_value: float32 [1024, 1024], P('blk')
- grad_w_out: float32 [1024, 1024], P('blk')
- grad_head_scale: float32 [16], replicated
- grad_ln_post: float32 [1024], P('blk')
- grad_ln_ffn: float32 [1024], P('blk')
- grad_w_fc1: float32 [1024, 4096], P('blk')
- grad_ln_mid: float32 [4096], P('blk')
- grad_w_fc2: float32 [4096, 1024], P('blk')
Inputs may be any that keep to these rules, and one draw needn't show every extreme that they name: In each row offsets rise strictly from offsets[r, 0] = 0. In each aligned block of 3 rows one row has a document that begins within its first 256 positions and ends within its last 256, and its last document is a single position.
All inputs are finite; a program needn't handle non-finite values.
Results may differ from a plain program's by a relative error of at most 0.02.
Values may be sent and summed in bfloat16 or wider, within the bound.
No kernel may reach another device: no remote copies, remote signals or barrier semaphores. Data moves between devices by JAX's collectives and lax.ppermute only.
A program may use at most 256 MiB of HBM per device.

v0:
```python
import jax
import jax.numpy as jnp
from jax import lax
from jax.sharding import PartitionSpec as P

EPSILON = 1e-05
MASKED = -1e30


def from_behind(block, axis, distance):
    devices = range(lax.axis_size(axis))
    route = [(i - distance, i) for i in devices if i - distance in devices]
    return lax.ppermute(block, axis, route)


def for_sending(value):

    def short(part):
        return part.astype(jnp.bfloat16) if part.dtype == jnp.float32 else part

    return jax.tree.map(short, value)


def shifted(value, axis, by):
    peers = lax.axis_size(axis)
    return lax.ppermute(value, axis, [(i, (i + by) % peers) for i in range(peers)])


def layer_norm(rows_in, gain_vec):
    average = jnp.mean(rows_in, axis=-1, keepdims=True)
    centred = rows_in - average
    variance = jnp.mean(centred * centred, axis=-1, keepdims=True)
    return centred * lax.rsqrt(variance + EPSILON) * gain_vec


def mid_block(pre_act, gain_vec):
    return layer_norm(jax.nn.gelu(pre_act, approximate=False), gain_vec)


def row_docs(offsets, positions):
    return jnp.sum((offsets[:, :, None] <= positions[None, None, :]).astype(jnp.int32), axis=1) - 1


def on_device(
    inputs,
    ln_attn,
    w_query,
    w_key,
    w_value,
    w_out,
    head_scale,
    ln_post,
    ln_ffn,
    w_fc1,
    ln_mid,
    w_fc2,
    offsets,
    cotangent,
):
    row_count, block_len, model_width = inputs.shape
    head_count = head_scale.shape[0]
    head_dim = model_width // head_count
    token_count = row_count * block_len
    group_size = lax.axis_size("blk")
    my_index = lax.axis_index("blk")
    score_scale = head_dim ** (-0.5)
    block_range = jnp.arange(block_len, dtype=jnp.int32)
    query_pos = my_index * block_len + block_range
    query_doc = row_docs(offsets, query_pos)
    x_float = inputs.astype(jnp.float32).reshape(token_count, model_width)
    normed = layer_norm(x_float, ln_attn).astype(jnp.bfloat16)

    def project(weight):
        product = jnp.dot(normed, weight, preferred_element_type=jnp.float32)
        return product.astype(jnp.bfloat16).reshape(row_count, block_len, head_count, head_dim)

    query_heads = project(w_query)
    key_heads = project(w_key)
    value_heads = project(w_value)

    def source_pos(turn_index):
        return (my_index - turn_index) % group_size * block_len + block_range

    def visible(key_pos):
        key_doc = row_docs(offsets, key_pos)
        return (key_pos[None, None, :] <= query_pos[None, :, None]) & (
            key_doc[:, None, :] == query_doc[:, :, None]
        )

    def scores_of(key_block, allowed):
        raw_scores = (
            jnp.einsum(
                "rqhe,rkhe->rhqk", query_heads, key_block, preferred_element_type=jnp.float32
            )
            * score_scale
        )
        return jnp.where(allowed[:, None], raw_scores, MASKED)

    def stats_update(stats_now, key_block, key_pos):
        allowed = visible(key_pos)

        def update(stats_in):
            running_max, running_sum = stats_in
            scores = scores_of(key_block, allowed)
            new_max = jnp.maximum(running_max, jnp.max(scores, axis=-1))
            new_sum = running_sum * jnp.exp(running_max - new_max) + jnp.sum(
                jnp.exp(scores - new_max[..., None]), axis=-1
            )
            return (new_max, new_sum)

        def keep_stats(stats_in):
            return stats_in

        return lax.cond(jnp.any(allowed), update, keep_stats, stats_now)

    def value_update(acc_sum, key_block, value_block, key_pos, log_total):
        allowed = visible(key_pos)

        def update(acc_in):
            prob_bf = jnp.exp(scores_of(key_block, allowed) - log_total[..., None]).astype(
                jnp.bfloat16
            )
            return acc_in + jnp.einsum(
                "rhqk,rkhe->rqhe", prob_bf, value_block, preferred_element_type=jnp.float32
            )

        def keep_acc(acc_in):
            return acc_in

        return lax.cond(jnp.any(allowed), update, keep_acc, acc_sum)

    stats_init = (
        jnp.full((row_count, head_count, block_len), MASKED, jnp.float32),
        jnp.zeros((row_count, head_count, block_len), jnp.float32),
    )
    zero_heads = jnp.zeros((row_count, block_len, head_count, head_dim), jnp.float32)
    stats_first = stats_update(stats_init, key_heads, query_pos)

    def stats_turn(turn_index, loop_state):
        key_block, stats_now = loop_state
        key_block = from_behind(key_block, "blk", 1)
        return (key_block, stats_update(stats_now, key_block, source_pos(turn_index)))

    stats_final = lax.fori_loop(1, group_size, stats_turn, (key_heads, stats_first))[1]
    log_total = stats_final[0] + jnp.log(stats_final[1])
    acc_first = value_update(zero_heads, key_heads, value_heads, query_pos, log_total)

    def value_turn(turn_index, loop_state):
        key_block, value_block, acc_sum = loop_state
        key_block, value_block = from_behind((key_block, value_block), "blk", 1)
        return (
            key_block,
            value_block,
            value_update(acc_sum, key_block, value_block, source_pos(turn_index), log_total),
        )

    attn_out = lax.fori_loop(1, group_size, value_turn, (key_heads, value_heads, acc_first))[2]
    scaled = (
        (attn_out * head_scale[None, None, :, None])
        .astype(jnp.bfloat16)
        .reshape(token_count, model_width)
    )
    attn_proj = jnp.dot(scaled, w_out, preferred_element_type=jnp.float32)
    residual = x_float + layer_norm(attn_proj, ln_post)
    ffn_in = layer_norm(residual, ln_ffn).astype(jnp.bfloat16)
    pre_act = jnp.dot(ffn_in, w_fc1, preferred_element_type=jnp.float32)
    mid_act = mid_block(pre_act, ln_mid).astype(jnp.bfloat16)
    layer_out = (residual + jnp.dot(mid_act, w_fc2, preferred_element_type=jnp.float32)).astype(
        jnp.bfloat16
    )
    d_out = cotangent.reshape(token_count, model_width)
    grad_w_fc2 = jnp.einsum("tf,td->fd", mid_act, d_out, preferred_element_type=jnp.float32)
    d_mid = jnp.einsum("td,fd->tf", d_out, w_fc2, preferred_element_type=jnp.float32)
    mid_value, mid_pull = jax.vjp(mid_block, pre_act, ln_mid)
    d_pre, grad_ln_mid = mid_pull(d_mid)
    d_pre = d_pre.astype(jnp.bfloat16)
    grad_w_fc1 = jnp.einsum("td,tf->df", ffn_in, d_pre, preferred_element_type=jnp.float32)
    d_ffn_in = jnp.einsum("tf,df->td", d_pre, w_fc1, preferred_element_type=jnp.float32)
    ffn_value, ffn_pull = jax.vjp(layer_norm, residual, ln_ffn)
    d_resid_ffn, grad_ln_ffn = ffn_pull(d_ffn_in)
    d_residual = d_out.astype(jnp.float32) + d_resid_ffn
    post_value, post_pull = jax.vjp(layer_norm, attn_proj, ln_post)
    d_proj, grad_ln_post = post_pull(d_residual)
    d_proj = d_proj.astype(jnp.bfloat16)
    grad_w_out = jnp.einsum("td,te->de", scaled, d_proj, preferred_element_type=jnp.float32)
    d_scaled = jnp.einsum("te,de->td", d_proj, w_out, preferred_element_type=jnp.float32)
    d_scaled = d_scaled.reshape(row_count, block_len, head_count, head_dim)
    scale_local = jnp.sum(d_scaled * attn_out, axis=(0, 1, 3))
    d_attn = (d_scaled * head_scale[None, None, :, None]).astype(jnp.bfloat16)
    delta_sum = jnp.transpose(jnp.sum(d_attn.astype(jnp.float32) * attn_out, axis=-1), (0, 2, 1))

    def grad_terms(key_block, value_block, key_pos):
        allowed = visible(key_pos)

        def compute(kv_blocks):
            prob_full = jnp.exp(scores_of(kv_blocks[0], allowed) - log_total[..., None])
            d_probs = jnp.einsum(
                "rqhe,rkhe->rhqk", d_attn, kv_blocks[1], preferred_element_type=jnp.float32
            )
            d_scores = (prob_full * (d_probs - delta_sum[..., None])).astype(jnp.bfloat16)
            dq_add = (
                jnp.einsum(
                    "rhqk,rkhe->rqhe", d_scores, kv_blocks[0], preferred_element_type=jnp.float32
                )
                * score_scale
            )
            dk_add = (
                jnp.einsum(
                    "rhqk,rqhe->rkhe", d_scores, query_heads, preferred_element_type=jnp.float32
                )
                * score_scale
            )
            dv_add = jnp.einsum(
                "rhqk,rqhe->rkhe",
                prob_full.astype(jnp.bfloat16),
                d_attn,
                preferred_element_type=jnp.float32,
            )
            return (dq_add, dk_add, dv_add)

        def skip(kv_blocks):
            zero_keys = jnp.zeros(kv_blocks[0].shape, jnp.float32)
            return (zero_heads, zero_keys, zero_keys)

        return lax.cond(jnp.any(allowed), compute, skip, (key_block, value_block))

    def pass_grads(grad_pair):
        return shifted((for_sending(grad_pair[0]), for_sending(grad_pair[1])), "blk", 1)

    dq_first, dk_first, dv_first = grad_terms(key_heads, value_heads, query_pos)
    grads_first = pass_grads((dk_first, dv_first))

    def back_turn(turn_index, loop_state):
        key_block, value_block, d_query, grad_pair = loop_state
        key_block, value_block = from_behind((key_block, value_block), "blk", 1)
        dq_add, dk_add, dv_add = grad_terms(key_block, value_block, source_pos(turn_index))
        grad_pair = pass_grads((grad_pair[0] + dk_add, grad_pair[1] + dv_add))
        return (key_block, value_block, d_query + dq_add, grad_pair)

    loop_state = lax.fori_loop(
        1, group_size, back_turn, (key_heads, value_heads, dq_first, grads_first)
    )
    d_query = loop_state[2].astype(jnp.bfloat16)
    d_key = loop_state[3][0].astype(jnp.bfloat16)
    d_value = loop_state[3][1].astype(jnp.bfloat16)
    d_query = d_query.reshape(token_count, model_width)
    d_key = d_key.reshape(token_count, model_width)
    d_value = d_value.reshape(token_count, model_width)
    grad_w_query = jnp.einsum("td,te->de", normed, d_query, preferred_element_type=jnp.float32)
    grad_w_key = jnp.einsum("td,te->de", normed, d_key, preferred_element_type=jnp.float32)
    grad_w_value = jnp.einsum("td,te->de", normed, d_value, preferred_element_type=jnp.float32)
    d_normed = jnp.einsum("te,de->td", d_query, w_query, preferred_element_type=jnp.float32)
    d_normed = d_normed + jnp.einsum("te,de->td", d_key, w_key, preferred_element_type=jnp.float32)
    d_normed = d_normed + jnp.einsum(
        "te,de->td", d_value, w_value, preferred_element_type=jnp.float32
    )
    attn_value, attn_pull = jax.vjp(layer_norm, x_float, ln_attn)
    d_in_attn, grad_ln_attn = attn_pull(d_normed)
    grad_inputs = (d_residual + d_in_attn).reshape(row_count, block_len, model_width)
    weight_parts = (
        lax.psum_scatter(
            grad_ln_attn.astype(jnp.bfloat16), "blk", scatter_dimension=0, tiled=True
        ).astype(jnp.float32),
        lax.psum_scatter(
            grad_w_query.astype(jnp.bfloat16), "blk", scatter_dimension=0, tiled=True
        ).astype(jnp.float32),
        lax.psum_scatter(
            grad_w_key.astype(jnp.bfloat16), "blk", scatter_dimension=0, tiled=True
        ).astype(jnp.float32),
        lax.psum_scatter(
            grad_w_value.astype(jnp.bfloat16), "blk", scatter_dimension=0, tiled=True
        ).astype(jnp.float32),
        lax.psum_scatter(
            grad_w_out.astype(jnp.bfloat16), "blk", scatter_dimension=0, tiled=True
        ).astype(jnp.float32),
        lax.psum_scatter(
            grad_ln_post.astype(jnp.bfloat16), "blk", scatter_dimension=0, tiled=True
        ).astype(jnp.float32),
        lax.psum_scatter(
            grad_ln_ffn.astype(jnp.bfloat16), "blk", scatter_dimension=0, tiled=True
        ).astype(jnp.float32),
        lax.psum_scatter(
            grad_w_fc1.astype(jnp.bfloat16), "blk", scatter_dimension=0, tiled=True
        ).astype(jnp.float32),
        lax.psum_scatter(
            grad_ln_mid.astype(jnp.bfloat16), "blk", scatter_dimension=0, tiled=True
        ).astype(jnp.float32),
        lax.psum_scatter(
            grad_w_fc2.astype(jnp.bfloat16), "blk", scatter_dimension=0, tiled=True
        ).astype(jnp.float32),
    )
    weight_sums = (
        lax.psum(weight_parts[0].astype(jnp.bfloat16), "batch").astype(jnp.float32),
        lax.psum(weight_parts[1].astype(jnp.bfloat16), "batch").astype(jnp.float32),
        lax.psum(weight_parts[2].astype(jnp.bfloat16), "batch").astype(jnp.float32),
        lax.psum(weight_parts[3].astype(jnp.bfloat16), "batch").astype(jnp.float32),
        lax.psum(weight_parts[4].astype(jnp.bfloat16), "batch").astype(jnp.float32),
        lax.psum(weight_parts[5].astype(jnp.bfloat16), "batch").astype(jnp.float32),
        lax.psum(weight_parts[6].astype(jnp.bfloat16), "batch").astype(jnp.float32),
        lax.psum(weight_parts[7].astype(jnp.bfloat16), "batch").astype(jnp.float32),
        lax.psum(weight_parts[8].astype(jnp.bfloat16), "batch").astype(jnp.float32),
        lax.psum(weight_parts[9].astype(jnp.bfloat16), "batch").astype(jnp.float32),
    )
    grad_head_scale = lax.psum(scale_local, ("batch", "blk"))
    return (
        layer_out.reshape(row_count, block_len, model_width),
        grad_inputs,
        weight_sums[0],
        weight_sums[1],
        weight_sums[2],
        weight_sums[3],
        weight_sums[4],
        grad_head_scale,
        weight_sums[5],
        weight_sums[6],
        weight_sums[7],
        weight_sums[8],
        weight_sums[9],
    )


def solution(mesh):
    placed = (
        P("batch", "blk", None),
        P(),
        P(),
        P(),
        P(),
        P(),
        P(),
        P(),
        P(),
        P(),
        P(),
        P(),
        P("batch", None),
        P("batch", "blk", None),
    )
    return jax.shard_map(
        on_device,
        mesh=mesh,
        in_specs=placed,
        out_specs=(
            P("batch", "blk", None),
            P("batch", "blk", None),
            P("blk"),
            P("blk", None),
            P("blk", None),
            P("blk", None),
            P("blk", None),
            P(),
            P("blk"),
            P("blk"),
            P("blk", None),
            P("blk"),
            P("blk", None),
        ),
        check_vma=False,
    )
```

profile of v0, /device:TPU:0, one launch (start us, length us, event | category | flops | bytes accessed | tf_op | source)
XLA Modules:
  0.0 2893.7 jit_solution(6441731187925492096)
XLA Ops:
  74.0 297.4 %while.67 = (s32[]{:T(128)}, bf16[3,256,16,64]{1,3,2,0:T(8,128)(2,1)}, f32[3,16,256]{2,1,0:T(8,128)}, f32[3,16,256]{2,1,0:T(8,128)S(1)}, s32[]{:T(128)}, /*index...) while((s32[]{:T(128)}, ...), condition=%wide.region_15.16_spmd.clone, body=%wide.region_8.15_spmd.clone.sunk | while | flops 425362944 | bytes 39129536 | solution.py:144
  81.7 31.1 %collective-permute-done = bf16[3,256,16,64]{1,3,2,0:T(8,128)(2,1)} collective-permute-done((bf16[3,256,16,64]{1,3,2,0:T(8,128)(2,1)}, bf16[3,256,16,64]{1,3,2,0:T(8,128)(2,1)}, u32[]{:S(2)}, u32[]{:S(2)}) %collective-permute-start) | collective-permute-done | bytes 1572896 | tf_op jit(solution)/shard_map/while/body/eval_jaxpr/ppermute | solution.py:13
  132.3 30.2 %collective-permute-done = bf16[3,256,16,64]{1,3,2,0:T(8,128)(2,1)} collective-permute-done((bf16[3,256,16,64]{1,3,2,0:T(8,128)(2,1)}, bf16[3,256,16,64]{1,3,2,0:T(8,128)(2,1)}, u32[]{:S(2)}, u32[]{:S(2)}) %collective-permute-start) | collective-permute-done | bytes 1572896 | tf_op jit(solution)/shard_map/while/body/eval_jaxpr/ppermute | solution.py:13
  172.5 29.3 %collective-permute-done = bf16[3,256,16,64]{1,3,2,0:T(8,128)(2,1)} collective-permute-done((bf16[3,256,16,64]{1,3,2,0:T(8,128)(2,1)}, bf16[3,256,16,64]{1,3,2,0:T(8,128)(2,1)}, u32[]{:S(2)}, u32[]{:S(2)}) %collective-permute-start) | collective-permute-done | bytes 1572896 | tf_op jit(solution)/shard_map/while/body/eval_jaxpr/ppermute | solution.py:13
  383.8 542.9 %while.68 = (s32[]{:T(128)}, bf16[3,256,16,64]{1,3,2,0:T(8,128)(2,1)}, bf16[3,256,16,64]{1,3,2,0:T(8,128)(2,1)}, f32[3,256,16,64]{1,3,2,0:T(8,128)}, s32[]{:T(12...) while((s32[]{:T(128)}, ...), condition=%wide.region_23.24_spmd.clone, body=%wide.region_18.23_spmd.clone.sunk | while | flops 819340800 | bytes 30478800 | solution.py:157
  936.7 38.8 %fusion.109 = (f32[768]{0:T(1024)S(1)}, f32[768,4096]{1,0:T(8,128)}, f32[768,4096]{1,0:T(8,128)}, f32[768,4096]{1,0:T(8,128)}) fusion(bf16[1024,4096]{1,0:T(8,128)(2,1)S(1)} %bitcast.155, f32[768,1024]{1,0:T(8,128)S(1)} %get-tuple-element.1410, f32[1024]{0:T(1024)S(1)} %copy-done.69, f32[768]{0:T(1024)S(1)} %fusion.97, f32[768]{0:T(1024)S(1)} %broadcast_multiply_fusion.1), kind=kOutput, calls=%fused_computation.201 | convolution fusion | flops 6650067968 | bytes 49296384 | tf_op jit(solution)/shard_map/dot_general | solution.py:166
  1117.5 73.7 %collective-permute-done.7 = bf16[3,256,16,64]{1,3,2,0:T(8,128)(2,1)} collective-permute-done((bf16[3,256,16,64]{1,3,2,0:T(8,128)(2,1)}, bf16[3,256,16,64]{1,3,2,0:T(8,128)(2,1)}, u32[]{:S(2)}, u32[]{:S(2)}) %collective-permute-start.7) | collective-permute-done | bytes 1572896 | tf_op jit(solution)/shard_map/ppermute | solution.py:26
  1211.7 1075.0 %while.69 = (s32[]{:T(128)}, bf16[3,256,16,64]{1,3,2,0:T(8,128)(2,1)}, bf16[3,256,16,64]{1,3,2,0:T(8,128)(2,1)}, f32[3,256,16,64]{1,3,2,0:T(8,128)}, bf16[3,256,...) while((s32[]{:T(128)}, ...), condition=%wide.region_44.45_spmd.clone, body=%wide.region_39.44_spmd.clone.sunk | while | flops 2052466176 | bytes 137728656 | solution.py:240
  1218.7 32.6 %collective-permute-done.3 = bf16[3,256,16,64]{1,3,2,0:T(8,128)(2,1)} collective-permute-done((bf16[3,256,16,64]{1,3,2,0:T(8,128)(2,1)}, bf16[3,256,16,64]{1,3,2,0:T(8,128)(2,1)}, u32[]{:S(2)}, u32[]{:S(2)}) %collective-permute-start.3) | collective-permute-done | bytes 1572896 | tf_op jit(solution)/shard_map/while/body/eval_jaxpr/ppermute | solution.py:13
  1437.9 29.6 %collective-permute-start.6 = (bf16[3,256,16,64]{1,3,2,0:T(8,128)(2,1)S(1)}, bf16[3,256,16,64]{1,3,2,0:T(8,128)(2,1)}, u32[]{:S(2)}, u32[]{:S(2)}) collective-permute-start(bf16[3,256,16,64]{1,3,2,0:T(8,128)(2,1)S(1)} %add_convert_fusion.10), channel_id=1, source_target_pairs={{0,1},{1,2},{2,3},{3,4},{4,5},{5,6},{6,7},{7,0},{8,9},{9,10},{10,1... | collective-permute-start | bytes 4718600 | tf_op jit(solution)/shard_map/while/body/eval_jaxpr/ppermute | solution.py:26
  1613.6 43.5 %collective-permute-done.5 = bf16[3,256,16,64]{1,3,2,0:T(8,128)(2,1)} collective-permute-done((bf16[3,256,16,64]{1,3,2,0:T(8,128)(2,1)S(1)}, bf16[3,256,16,64]{1,3,2,0:T(8,128)(2,1)}, u32[]{:S(2)}, u32[]{:S(2)}) %collective-permute-start.5) | collective-permute-done | bytes 1572896 | tf_op jit(solution)/shard_map/while/body/eval_jaxpr/ppermute | solution.py:26
  1768.7 44.8 %collective-permute-done.5 = bf16[3,256,16,64]{1,3,2,0:T(8,128)(2,1)} collective-permute-done((bf16[3,256,16,64]{1,3,2,0:T(8,128)(2,1)S(1)}, bf16[3,256,16,64]{1,3,2,0:T(8,128)(2,1)}, u32[]{:S(2)}, u32[]{:S(2)}) %collective-permute-start.5) | collective-permute-done | bytes 1572896 | tf_op jit(solution)/shard_map/while/body/eval_jaxpr/ppermute | solution.py:26
  1840.2 29.8 %collective-permute-done.3 = bf16[3,256,16,64]{1,3,2,0:T(8,128)(2,1)} collective-permute-done((bf16[3,256,16,64]{1,3,2,0:T(8,128)(2,1)}, bf16[3,256,16,64]{1,3,2,0:T(8,128)(2,1)}, u32[]{:S(2)}, u32[]{:S(2)}) %collective-permute-start.3) | collective-permute-done | bytes 1572896 | tf_op jit(solution)/shard_map/while/body/eval_jaxpr/ppermute | solution.py:13
  1914.9 53.1 %collective-permute-done.5 = bf16[3,256,16,64]{1,3,2,0:T(8,128)(2,1)} collective-permute-done((bf16[3,256,16,64]{1,3,2,0:T(8,128)(2,1)S(1)}, bf16[3,256,16,64]{1,3,2,0:T(8,128)(2,1)}, u32[]{:S(2)}, u32[]{:S(2)}) %collective-permute-start.5) | collective-permute-done | bytes 1572896 | tf_op jit(solution)/shard_map/while/body/eval_jaxpr/ppermute | solution.py:26
  1992.9 29.8 %collective-permute-done.3 = bf16[3,256,16,64]{1,3,2,0:T(8,128)(2,1)} collective-permute-done((bf16[3,256,16,64]{1,3,2,0:T(8,128)(2,1)}, bf16[3,256,16,64]{1,3,2,0:T(8,128)(2,1)}, u32[]{:S(2)}, u32[]{:S(2)}) %collective-permute-start.3) | collective-permute-done | bytes 1572896 | tf_op jit(solution)/shard_map/while/body/eval_jaxpr/ppermute | solution.py:13
  2067.7 52.8 %collective-permute-done.5 = bf16[3,256,16,64]{1,3,2,0:T(8,128)(2,1)} collective-permute-done((bf16[3,256,16,64]{1,3,2,0:T(8,128)(2,1)S(1)}, bf16[3,256,16,64]{1,3,2,0:T(8,128)(2,1)}, u32[]{:S(2)}, u32[]{:S(2)}) %collective-permute-start.5) | collective-permute-done | bytes 1572896 | tf_op jit(solution)/shard_map/while/body/eval_jaxpr/ppermute | solution.py:26
  2143.9 28.9 collective-permute-done.3
  2218.7 51.0 %collective-permute-done.5 = bf16[3,256,16,64]{1,3,2,0:T(8,128)(2,1)} collective-permute-done((bf16[3,256,16,64]{1,3,2,0:T(8,128)(2,1)S(1)}, bf16[3,256,16,64]{1,3,2,0:T(8,128)(2,1)}, u32[]{:S(2)}, u32[]{:S(2)}) %collective-permute-start.5) | collective-permute-done | bytes 1572896 | tf_op jit(solution)/shard_map/while/body/eval_jaxpr/ppermute | solution.py:26
  2337.1 39.2 %psum.82 = f32[16]{0:T(128)} all-reduce(f32[16]{0:T(128)S(1)} %copy-done.74), channel_id=1, replica_groups=mesh['batch'=4,'blk'=8] {'batch','blk'}, use_global_device_ids=true, to_apply=%region_59.60 | all-reduce | flops 16 | bytes 128 | tf_op jit(solution)/shard_map/psum | solution.py:304
  2398.2 35.0 %reduce-scatter.11.cloned.1.call-done = bf16[128,1024]{1,0:T(8,128)(2,1)} async-done(((bf16[1024,1024]{1,0:T(8,128)(2,1)}), bf16[128,1024]{1,0:T(8,128)(2,1)}) %reduce-scatter.11.cloned.1.call-update) | async-done | bytes 262160 | tf_op jit(solution)/shard_map/reduce_scatter | solution.py:270
  2433.1 70.6 %reduce-scatter.9.cloned.1.call-done = bf16[128,1024]{1,0:T(8,128)(2,1)} async-done(((bf16[1024,1024]{1,0:T(8,128)(2,1)}), bf16[128,1024]{1,0:T(8,128)(2,1)}) %reduce-scatter.9.cloned.1.call-update) | async-done | bytes 262160 | tf_op jit(solution)/shard_map/reduce_scatter | solution.py:267
  2503.7 151.6 %reduce-scatter.15.cloned.1.call-done = bf16[128,4096]{1,0:T(8,128)(2,1)} async-done(((bf16[1024,4096]{1,0:T(8,128)(2,1)}), bf16[128,4096]{1,0:T(8,128)(2,1)}) %reduce-scatter.15.cloned.1.call-update) | async-done | bytes 1048592 | tf_op jit(solution)/shard_map/reduce_scatter | solution.py:282
  2655.3 152.0 %reduce-scatter.17.cloned.1.call-done = bf16[512,1024]{1,0:T(8,128)(2,1)} async-done(((bf16[4096,1024]{1,0:T(8,128)(2,1)}), bf16[512,1024]{1,0:T(8,128)(2,1)}) %reduce-scatter.17.cloned.1.call-update) | async-done | bytes 1048592 | tf_op jit(solution)/shard_map/reduce_scatter | solution.py:288
  2816.9 35.2 %all-reduce.4 = (bf16[1024]{0:T(1024)(128)(2,1)S(1)}, bf16[1024]{0:T(1024)(128)(2,1)S(1)}, bf16[1024]{0:T(1024)(128)(2,1)S(1)}, bf16[4096]{0:T(1024)(128)(2,1)S(1)}) all-reduce(bf16[1024]{0:T(1024)(128)(2,1)S(1)} %get-tuple-element.1311, bf16[1024]{0:T(1024)(128)(2,1)S(1)} %copy-done.68, ...), channel_id=2, replica_groups=mesh['batch'=4,'blk'=8] {'blk'}, use_global_device_ids=true, to_apply=%region_48.49.clone | all-reduce | flops 7168 | bytes 28672
  (603 shorter events, 1828.9 us)
Async XLA Ops:
  7.2 2390.9 %reduce-scatter.13.cloned.1.call-start = ((), (), s32[]{:S(2)}) async-start(), calls=%async_computation.9 | async-start | bytes 2359296 | tf_op jit(solution)/shard_map/reduce_scatter | solution.py:273
  1090.3 100.8 %collective-permute-start.7 = (bf16[3,256,16,64]{1,3,2,0:T(8,128)(2,1)}, bf16[3,256,16,64]{1,3,2,0:T(8,128)(2,1)}, u32[]{:S(2)}, u32[]{:S(2)}) collective-permute-start(bf16[3,256,16,64]{1,3,2,0:T(8,128)(2,1)} %convert_element_type.283), channel_id=1, source_target_pairs={{0,1},{1,2},{2,3},{3,4},{4,5},{5,6},{6,7},{7,0},{8,9},{9,10},{10,1... | collective-permute-start | bytes 4718600 | tf_op jit(solution)/shard_map/ppermute | solution.py:26
  1103.8 107.9 %collective-permute-start.8 = (bf16[3,256,16,64]{1,3,2,0:T(8,128)(2,1)}, bf16[3,256,16,64]{1,3,2,0:T(8,128)(2,1)}, u32[]{:S(2)}, u32[]{:S(2)}) collective-permute-start(bf16[3,256,16,64]{1,3,2,0:T(8,128)(2,1)} %convert_element_type.284), channel_id=1, source_target_pairs={{0,1},{1,2},{2,3},{3,4},{4,5},{5,6},{6,7},{7,0},{8,9},{9,10},{10,1... | collective-permute-start | bytes 4718600 | tf_op jit(solution)/shard_map/ppermute | solution.py:26
  1111.1 1287.0 %reduce-scatter.7.cloned.1.call-start = ((), (), s32[]{:S(2)}) async-start(), calls=%async_computation.6 | async-start | bytes 2359296 | tf_op jit(solution)/shard_map/reduce_scatter | solution.py:264
  1274.2 66.8 %collective-permute-start.5 = (bf16[3,256,16,64]{1,3,2,0:T(8,128)(2,1)S(1)}, bf16[3,256,16,64]{1,3,2,0:T(8,128)(2,1)}, u32[]{:S(2)}, u32[]{:S(2)}) collective-permute-start(bf16[3,256,16,64]{1,3,2,0:T(8,128)(2,1)S(1)} %add_convert_fusion.9), channel_id=1, source_target_pairs={{0,1},{1,2},{2,3},{3,4},{4,5},{5,6},{6,7},{7,0},{8,9},{9,10},{10,1... | collective-permute-start | bytes 4718600 | tf_op jit(solution)/shard_map/while/body/eval_jaxpr/ppermute | solution.py:26
  1430.1 65.8 %collective-permute-start.5 = (bf16[3,256,16,64]{1,3,2,0:T(8,128)(2,1)S(1)}, bf16[3,256,16,64]{1,3,2,0:T(8,128)(2,1)}, u32[]{:S(2)}, u32[]{:S(2)}) collective-permute-start(bf16[3,256,16,64]{1,3,2,0:T(8,128)(2,1)S(1)} %add_convert_fusion.9), channel_id=1, source_target_pairs={{0,1},{1,2},{2,3},{3,4},{4,5},{5,6},{6,7},{7,0},{8,9},{9,10},{10,1... | collective-permute-start | bytes 4718600 | tf_op jit(solution)/shard_map/while/body/eval_jaxpr/ppermute | solution.py:26
  1437.9 78.7 %collective-permute-start.6 = (bf16[3,256,16,64]{1,3,2,0:T(8,128)(2,1)S(1)}, bf16[3,256,16,64]{1,3,2,0:T(8,128)(2,1)}, u32[]{:S(2)}, u32[]{:S(2)}) collective-permute-start(bf16[3,256,16,64]{1,3,2,0:T(8,128)(2,1)S(1)} %add_convert_fusion.10), channel_id=1, source_target_pairs={{0,1},{1,2},{2,3},{3,4},{4,5},{5,6},{6,7},{7,0},{8,9},{9,10},{10,1... | collective-permute-start | bytes 4718600 | tf_op jit(solution)/shard_map/while/body/eval_jaxpr/ppermute | solution.py:26
  1585.9 71.1 %collective-permute-start.5 = (bf16[3,256,16,64]{1,3,2,0:T(8,128)(2,1)S(1)}, bf16[3,256,16,64]{1,3,2,0:T(8,128)(2,1)}, u32[]{:S(2)}, u32[]{:S(2)}) collective-permute-start(bf16[3,256,16,64]{1,3,2,0:T(8,128)(2,1)S(1)} %add_convert_fusion.9), channel_id=1, source_target_pairs={{0,1},{1,2},{2,3},{3,4},{4,5},{5,6},{6,7},{7,0},{8,9},{9,10},{10,1... | collective-permute-start | bytes 4718600 | tf_op jit(solution)/shard_map/while/body/eval_jaxpr/ppermute | solution.py:26
  1600.6 78.4 %collective-permute-start.6 = (bf16[3,256,16,64]{1,3,2,0:T(8,128)(2,1)S(1)}, bf16[3,256,16,64]{1,3,2,0:T(8,128)(2,1)}, u32[]{:S(2)}, u32[]{:S(2)}) collective-permute-start(bf16[3,256,16,64]{1,3,2,0:T(8,128)(2,1)S(1)} %add_convert_fusion.10), channel_id=1, source_target_pairs={{0,1},{1,2},{2,3},{3,4},{4,5},{5,6},{6,7},{7,0},{8,9},{9,10},{10,1... | collective-permute-start | bytes 4718600 | tf_op jit(solution)/shard_map/while/body/eval_jaxpr/ppermute | solution.py:26
  1681.5 61.7 %collective-permute-start.4 = (bf16[3,256,16,64]{1,3,2,0:T(8,128)(2,1)}, bf16[3,256,16,64]{1,3,2,0:T(8,128)(2,1)}, u32[]{:S(2)}, u32[]{:S(2)}) collective-permute-start(bf16[3,256,16,64]{1,3,2,0:T(8,128)(2,1)} %get-tuple-element.1781), channel_id=1, source_target_pairs={{0,1},{1,2},{2,3},{3,4},{4,5},{5,6},{6,7},{8,9},{9,10},{10,11},{11... | collective-permute-start | bytes 4718600 | tf_op jit(solution)/shard_map/while/body/eval_jaxpr/ppermute | solution.py:13
  1746.2 67.2 %collective-permute-start.5 = (bf16[3,256,16,64]{1,3,2,0:T(8,128)(2,1)S(1)}, bf16[3,256,16,64]{1,3,2,0:T(8,128)(2,1)}, u32[]{:S(2)}, u32[]{:S(2)}) collective-permute-start(bf16[3,256,16,64]{1,3,2,0:T(8,128)(2,1)S(1)} %add_convert_fusion.9), channel_id=1, source_target_pairs={{0,1},{1,2},{2,3},{3,4},{4,5},{5,6},{6,7},{7,0},{8,9},{9,10},{10,1... | collective-permute-start | bytes 4718600 | tf_op jit(solution)/shard_map/while/body/eval_jaxpr/ppermute | solution.py:26
  1750.7 82.8 %collective-permute-start.6 = (bf16[3,256,16,64]{1,3,2,0:T(8,128)(2,1)S(1)}, bf16[3,256,16,64]{1,3,2,0:T(8,128)(2,1)}, u32[]{:S(2)}, u32[]{:S(2)}) collective-permute-start(bf16[3,256,16,64]{1,3,2,0:T(8,128)(2,1)S(1)} %add_convert_fusion.10), channel_id=1, source_target_pairs={{0,1},{1,2},{2,3},{3,4},{4,5},{5,6},{6,7},{7,0},{8,9},{9,10},{10,1... | collective-permute-start | bytes 4718600 | tf_op jit(solution)/shard_map/while/body/eval_jaxpr/ppermute | solution.py:26
  1836.0 61.7 %collective-permute-start.4 = (bf16[3,256,16,64]{1,3,2,0:T(8,128)(2,1)}, bf16[3,256,16,64]{1,3,2,0:T(8,128)(2,1)}, u32[]{:S(2)}, u32[]{:S(2)}) collective-permute-start(bf16[3,256,16,64]{1,3,2,0:T(8,128)(2,1)} %get-tuple-element.1781), channel_id=1, source_target_pairs={{0,1},{1,2},{2,3},{3,4},{4,5},{5,6},{6,7},{8,9},{9,10},{10,11},{11... | collective-permute-start | bytes 4718600 | tf_op jit(solution)/shard_map/while/body/eval_jaxpr/ppermute | solution.py:13
  1900.8 67.2 %collective-permute-start.5 = (bf16[3,256,16,64]{1,3,2,0:T(8,128)(2,1)S(1)}, bf16[3,256,16,64]{1,3,2,0:T(8,128)(2,1)}, u32[]{:S(2)}, u32[]{:S(2)}) collective-permute-start(bf16[3,256,16,64]{1,3,2,0:T(8,128)(2,1)S(1)} %add_convert_fusion.9), channel_id=1, source_target_pairs={{0,1},{1,2},{2,3},{3,4},{4,5},{5,6},{6,7},{7,0},{8,9},{9,10},{10,1... | collective-permute-start | bytes 4718600 | tf_op jit(solution)/shard_map/while/body/eval_jaxpr/ppermute | solution.py:26
  1905.3 81.1 %collective-permute-start.6 = (bf16[3,256,16,64]{1,3,2,0:T(8,128)(2,1)S(1)}, bf16[3,256,16,64]{1,3,2,0:T(8,128)(2,1)}, u32[]{:S(2)}, u32[]{:S(2)}) collective-permute-start(bf16[3,256,16,64]{1,3,2,0:T(8,128)(2,1)S(1)} %add_convert_fusion.10), channel_id=1, source_target_pairs={{0,1},{1,2},{2,3},{3,4},{4,5},{5,6},{6,7},{7,0},{8,9},{9,10},{10,1... | collective-permute-start | bytes 4718600 | tf_op jit(solution)/shard_map/while/body/eval_jaxpr/ppermute | solution.py:26
  2053.5 66.9 %collective-permute-start.5 = (bf16[3,256,16,64]{1,3,2,0:T(8,128)(2,1)S(1)}, bf16[3,256,16,64]{1,3,2,0:T(8,128)(2,1)}, u32[]{:S(2)}, u32[]{:S(2)}) collective-permute-start(bf16[3,256,16,64]{1,3,2,0:T(8,128)(2,1)S(1)} %add_convert_fusion.9), channel_id=1, source_target_pairs={{0,1},{1,2},{2,3},{3,4},{4,5},{5,6},{6,7},{7,0},{8,9},{9,10},{10,1... | collective-permute-start | bytes 4718600 | tf_op jit(solution)/shard_map/while/body/eval_jaxpr/ppermute | solution.py:26
  2058.0 79.3 %collective-permute-start.6 = (bf16[3,256,16,64]{1,3,2,0:T(8,128)(2,1)S(1)}, bf16[3,256,16,64]{1,3,2,0:T(8,128)(2,1)}, u32[]{:S(2)}, u32[]{:S(2)}) collective-permute-start(bf16[3,256,16,64]{1,3,2,0:T(8,128)(2,1)S(1)} %add_convert_fusion.10), channel_id=1, source_target_pairs={{0,1},{1,2},{2,3},{3,4},{4,5},{5,6},{6,7},{7,0},{8,9},{9,10},{10,1... | collective-permute-start | bytes 4718600 | tf_op jit(solution)/shard_map/while/body/eval_jaxpr/ppermute | solution.py:26
  2204.5 65.1 %collective-permute-start.5 = (bf16[3,256,16,64]{1,3,2,0:T(8,128)(2,1)S(1)}, bf16[3,256,16,64]{1,3,2,0:T(8,128)(2,1)}, u32[]{:S(2)}, u32[]{:S(2)}) collective-permute-start(bf16[3,256,16,64]{1,3,2,0:T(8,128)(2,1)S(1)} %add_convert_fusion.9), channel_id=1, source_target_pairs={{0,1},{1,2},{2,3},{3,4},{4,5},{5,6},{6,7},{7,0},{8,9},{9,10},{10,1... | collective-permute-start | bytes 4718600 | tf_op jit(solution)/shard_map/while/body/eval_jaxpr/ppermute | solution.py:26
  2209.0 77.5 %collective-permute-start.6 = (bf16[3,256,16,64]{1,3,2,0:T(8,128)(2,1)S(1)}, bf16[3,256,16,64]{1,3,2,0:T(8,128)(2,1)}, u32[]{:S(2)}, u32[]{:S(2)}) collective-permute-start(bf16[3,256,16,64]{1,3,2,0:T(8,128)(2,1)S(1)} %add_convert_fusion.10), channel_id=1, source_target_pairs={{0,1},{1,2},{2,3},{3,4},{4,5},{5,6},{6,7},{7,0},{8,9},{9,10},{10,1... | collective-permute-start | bytes 4718600 | tf_op jit(solution)/shard_map/while/body/eval_jaxpr/ppermute | solution.py:26
  2294.9 138.2 %reduce-scatter.11.cloned.1.call-start = ((), (), s32[]{:S(2)}) async-start(), calls=%async_computation.8 | async-start | bytes 2359296 | tf_op jit(solution)/shard_map/reduce_scatter | solution.py:270
  2302.6 201.1 %reduce-scatter.9.cloned.1.call-start = ((), (), s32[]{:S(2)}) async-start(), calls=%async_computation.7 | async-start | bytes 2359296 | tf_op jit(solution)/shard_map/reduce_scatter | solution.py:267
  2310.3 345.0 %reduce-scatter.15.cloned.1.call-start = ((), (), s32[]{:S(2)}) async-start(), calls=%async_computation.10 | async-start | bytes 9437184 | tf_op jit(solution)/shard_map/reduce_scatter | solution.py:282
  2323.2 484.0 %reduce-scatter.17.cloned.1.call-start = ((), (), s32[]{:S(2)}) async-start(), calls=%async_computation.11 | async-start | bytes 9437184 | tf_op jit(solution)/shard_map/reduce_scatter | solution.py:288
  2336.5 542.1 %all-reduce.9.cloned.1.call-start = ((), (), s32[]{:S(2)}) async-start(), calls=%async_computation.12 | async-start | bytes 6291456 | tf_op jit(solution)/shard_map/psum | solution.py:294
  (114 other events, 5724.8 us)
Sparse Core Ops, SparseCore 0:
  1111.2 197.3 reduce-scatter.12
  2295.0 68.0 reduce-scatter.6
  2366.6 66.4 reduce-scatter.10
  2437.1 66.6 reduce-scatter.8
  2507.2 148.0 reduce-scatter.14
  2659.2 147.9 reduce-scatter.16
  2810.1 68.4 all-reduce.8
where the time goes:
time: 2910 us; the launch traced here: 2890 us
  waiting for transfers between devices  1810 us (62%)
  starting transfers between devices  437 us (15%)
  matrix products  182 us (6%)
  local copies, waits for them, and re-layouts  177 us (6%)
  other arithmetic  172 us (6%)
  blocking collectives  80.5 us (3%)
    ppermute x35, waiting for transfers between devices, from_behind(): return lax.ppermute(block, axis, route)  870 us
    ppermute x16, waiting for transfers between devices, shifted(): lax.ppermute(value, axis, [(i, (i + by) % peers) for i in range(peers)])  522 us
    ppermute x35, starting transfers between devices, from_behind(): return lax.ppermute(block, axis, route)  321 us
    reduce_scatter x1, waiting for transfers between devices, on_device(): lax.psum_scatter(grad_w_fc2.astype(jnp.bfloat16), 'blk', scatter_dimensio...  152 us
    reduce_scatter x1, waiting for transfers between devices, on_device(): lax.psum_scatter(grad_w_fc1.astype(jnp.bfloat16), 'blk', scatter_dimensio...  152 us
    ppermute x16, starting transfers between devices, shifted(): lax.ppermute(value, axis, [(i, (i + by) % peers) for i in range(peers)])  115 us
    while x35, local copies, waits for them, and re-layouts  95.9 us
    reduce_scatter x1, waiting for transfers between devices, on_device(): lax.psum_scatter(grad_w_key.astype(jnp.bfloat16), 'blk', scatter_dimensio...  70.6 us
  transfers between devices with their start and end apart: 58, of which 56 were waited for; matrix products, arithmetic and copies ran while one was open for 7% of the time, Pallas kernels for 0%

commit v1 on v0

v1 whole, which is shorter than its diff:
```python
import functools

import jax
import jax.numpy as jnp
from jax import lax
from jax.experimental import pallas as pl
from jax.experimental.pallas import tpu as pltpu
from jax.sharding import PartitionSpec as P

EPSILON = 1e-05
MASKED = -1e30
VMEM_BYTES = 56 * 1024 * 1024
F32 = jnp.float32
BF16 = jnp.bfloat16
LAST = (((1,), (1,)), ((), ()))
FIRST = (((0,), (0,)), ((), ()))


def dot_last(left, right):
    return lax.dot_general(left, right, LAST, preferred_element_type=F32)


def dot_first(left, right):
    return lax.dot_general(left, right, FIRST, preferred_element_type=F32)


def doc_start(offs_ref, row, pos):
    start = jnp.zeros_like(pos)
    for d in range(offs_ref.shape[1]):
        first = offs_ref[row, d]
        start = jnp.where(pos >= first, first, start)
    return start


def doc_end(offs_ref, row, pos, length):
    end = jnp.int32(length)
    for d in reversed(range(offs_ref.shape[1])):
        first = offs_ref[row, d]
        end = jnp.where(first > pos, first, end)
    return end


def head_lanes(shape, head, head_dim):
    lane = lax.broadcasted_iota(jnp.int32, shape, 1)
    return (lane >= head * head_dim) & (lane < (head + 1) * head_dim)


def attend_kernel(heads, head_dim, offs_ref, qkv_ref, scale_ref, out_ref, lse_ref, score_ref):
    blocks, _, _, span, width = qkv_ref.shape
    wide = score_ref.shape[-1]
    per = wide // span
    row = pl.program_id(0)
    lanes = min(128, wide)
    score_scale = head_dim ** (-0.5)

    def query_block(i, carry):
        first_pos = i * span
        queries = qkv_ref[i, 0, 0] * jnp.asarray(score_scale, BF16)
        query_head = [
            jnp.where(head_lanes((span, width), h, head_dim), queries, 0).astype(BF16)
            for h in range(heads)
        ]
        query_pos = first_pos + lax.broadcasted_iota(jnp.int32, (span, 1), 0)
        query_start = doc_start(offs_ref, row, query_pos)
        low = doc_start(offs_ref, row, first_pos) // wide
        high = (first_pos + span - 1) // wide + 1

        def score_step(j, tops):
            keys = qkv_ref[pl.ds(j * per, per), 0, 1].reshape(wide, width)
            key_pos = j * wide + lax.broadcasted_iota(jnp.int32, (span, wide), 1)
            allowed = (key_pos >= query_start) & (key_pos <= query_pos)
            new = []
            for h in range(heads):
                scores = jnp.where(allowed, dot_last(query_head[h], keys), MASKED)
                score_ref[h, j] = scores
                top = tops[h]
                for c in range(0, wide, lanes):
                    top = jnp.maximum(top, scores[:, c : c + lanes])
                new.append(top)
            return tuple(new)

        tops = lax.fori_loop(
            low, high, score_step, tuple(jnp.full((span, lanes), MASKED, F32) for h in range(heads))
        )
        tops = [jnp.max(top, axis=1, keepdims=True) for top in tops]

        def value_step(j, state):
            values = qkv_ref[pl.ds(j * per, per), 0, 2].reshape(wide, width)
            new = []
            for h in range(heads):
                total, acc = state[h]
                probs = jnp.exp(score_ref[h, j] - tops[h])
                for c in range(0, wide, lanes):
                    total = total + probs[:, c : c + lanes]
                acc = acc + jnp.dot(probs.astype(BF16), values, preferred_element_type=F32)
                new.append((total, acc))
            return tuple(new)

        state = lax.fori_loop(
            low,
            high,
            value_step,
            tuple(
                (jnp.zeros((span, lanes), F32), jnp.zeros((span, width), F32)) for h in range(heads)
            ),
        )
        result = jnp.zeros((span, width), F32)
        for h in range(heads):
            total = jnp.sum(state[h][0], axis=1, keepdims=True)
            result = jnp.where(head_lanes((span, width), h, head_dim), state[h][1] / total, result)
            log_total = tops[h] + jnp.log(total)
            lse_ref[0, i, h : h + 1, :] = jnp.transpose(jnp.broadcast_to(log_total, (span, 128)))[
                0:1, :
            ]
        out_ref[i, 0] = (result * scale_ref[...]).astype(BF16)
        return carry

    lax.fori_loop(0, blocks, query_block, 0)


def attend(offsets, qkv, scale_lanes, heads, head_dim):
    blocks, rows, _, span, width = qkv.shape
    wide = max(span, min(512, blocks * span))
    grid_spec = pltpu.PrefetchScalarGridSpec(
        num_scalar_prefetch=1,
        grid=(rows,),
        in_specs=[
            pl.BlockSpec((blocks, 1, 3, span, width), lambda r, o: (0, r, 0, 0, 0)),
            pl.BlockSpec((1, width), lambda r, o: (0, 0)),
        ],
        out_specs=[
            pl.BlockSpec((blocks, 1, span, width), lambda r, o: (0, r, 0, 0)),
            pl.BlockSpec((1, blocks, heads, span), lambda r, o: (r, 0, 0, 0)),
        ],
        scratch_shapes=[pltpu.VMEM((heads, blocks * span // wide, span, wide), F32)],
    )
    return pl.pallas_call(
        functools.partial(attend_kernel, heads, head_dim),
        grid_spec=grid_spec,
        out_shape=[
            jax.ShapeDtypeStruct((blocks, rows, span, width), BF16),
            jax.ShapeDtypeStruct((rows, blocks, heads, span), F32),
        ],
        compiler_params=pltpu.CompilerParams(vmem_limit_bytes=VMEM_BYTES),
        name="attend",
    )(offsets, qkv, scale_lanes)


def attend_back_kernel(
    heads,
    head_dim,
    offs_ref,
    qkv_ref,
    grad_ref,
    out_ref,
    inv_ref,
    lse_ref,
    dqkv_ref,
    total_ref,
    q_ref,
    k_ref,
    g_ref,
    delta_ref,
    dq_ref,
):
    blocks, _, _, span, width = qkv_ref.shape
    row = pl.program_id(0)
    score_scale = head_dim ** (-0.5)
    picks = lax.broadcasted_iota(jnp.int32, (8, width), 0)
    lane = lax.broadcasted_iota(jnp.int32, (8, width), 1)
    ones = jnp.where(lane // head_dim == picks, 1.0, 0.0).astype(F32)

    def prepare(i, carry):
        queries = qkv_ref[i, 0, 0] * jnp.asarray(score_scale, BF16)
        keys = qkv_ref[i, 0, 1]
        grads = grad_ref[i, 0]
        for h in range(heads):
            mine = head_lanes((span, width), h, head_dim)
            q_ref[h, i] = jnp.where(mine, queries, 0).astype(BF16)
            k_ref[h, i] = jnp.where(mine, keys, 0).astype(BF16)
            g_ref[h, i] = jnp.where(mine, grads, 0).astype(BF16)
        product = grads.astype(F32) * out_ref[i, 0].astype(F32) * inv_ref[...]
        delta_ref[i] = lax.dot_general(
            ones, product, LAST, precision=lax.Precision.HIGHEST, preferred_element_type=F32
        )
        dq_ref[i] = jnp.zeros((span, width), F32)
        return carry + delta_ref[i]

    total_ref[0] = lax.fori_loop(0, blocks, prepare, jnp.zeros((8, span), F32))

    def key_block(j, carry):
        keys = qkv_ref[j, 0, 1]
        values = qkv_ref[j, 0, 2]
        key_pos = j * span + lax.broadcasted_iota(jnp.int32, (span, 1), 0)
        last = (doc_end(offs_ref, row, (j + 1) * span - 1, blocks * span) - 1) // span + 1

        def query_step(i, state):
            dk, dv = state
            query_pos = i * span + lax.broadcasted_iota(jnp.int32, (1, span), 1)
            query_start = doc_start(offs_ref, row, query_pos)
            allowed = (key_pos >= query_start) & (key_pos <= query_pos)
            dq = dq_ref[i]
            for h in range(heads):
                scores = dot_last(keys, q_ref[h, i])
                scores = jnp.where(allowed, scores - lse_ref[0, i, h : h + 1, :], MASKED)
                probs = jnp.exp(scores)
                d_probs = dot_last(values, g_ref[h, i])
                d_scores = (probs * (d_probs - delta_ref[i, h : h + 1, :])).astype(BF16)
                dv = dv + jnp.dot(probs.astype(BF16), g_ref[h, i], preferred_element_type=F32)
                dk = dk + jnp.dot(d_scores, q_ref[h, i], preferred_element_type=F32)
                dq = dq + dot_first(d_scores, k_ref[h, j])
            dq_ref[i] = dq
            return (dk, dv)

        zero = jnp.zeros((span, width), F32)
        dk, dv = lax.fori_loop(j, last, query_step, (zero, zero))
        dqkv_ref[j, 0, 1] = dk.astype(BF16)
        dqkv_ref[j, 0, 2] = dv.astype(BF16)
        dqkv_ref[j, 0, 0] = (dq_ref[j] * score_scale).astype(BF16)
        return carry

    lax.fori_loop(0, blocks, key_block, 0)


def attend_back(offsets, qkv, grads, scaled, inverse_lanes, lse, heads, head_dim):
    blocks, rows, _, span, width = qkv.shape
    block_spec = pl.BlockSpec((blocks, 1, span, width), lambda r, o: (0, r, 0, 0))
    wide_spec = pl.BlockSpec((blocks, 1, 3, span, width), lambda r, o: (0, r, 0, 0, 0))
    grid_spec = pltpu.PrefetchScalarGridSpec(
        num_scalar_prefetch=1,
        grid=(rows,),
        in_specs=[
            wide_spec,
            block_spec,
            block_spec,
            pl.BlockSpec((1, width), lambda r, o: (0, 0)),
            pl.BlockSpec((1, blocks, heads, span), lambda r, o: (r, 0, 0, 0)),
        ],
        out_specs=[wide_spec, pl.BlockSpec((1, 8, span), lambda r, o: (r, 0, 0))],
        scratch_shapes=[pltpu.VMEM((heads, blocks, span, width), BF16)] * 3
        + [pltpu.VMEM((blocks, 8, span), F32), pltpu.VMEM((blocks, span, width), F32)],
    )
    return pl.pallas_call(
        functools.partial(attend_back_kernel, heads, head_dim),
        grid_spec=grid_spec,
        out_shape=[
            jax.ShapeDtypeStruct(qkv.shape, BF16),
            jax.ShapeDtypeStruct((rows, 8, span), F32),
        ],
        compiler_params=pltpu.CompilerParams(vmem_limit_bytes=VMEM_BYTES),
        name="attend_back",
    )(offsets, qkv, grads, scaled, inverse_lanes, lse)


def exchange(parts):
    return lax.all_to_all(parts, "blk", 0, 0, tiled=True)


def norm_parts(rows_in):
    average = jnp.mean(rows_in, axis=-1, keepdims=True)
    centred = rows_in - average
    spread = lax.rsqrt(jnp.mean(centred * centred, axis=-1, keepdims=True) + EPSILON)
    return centred * spread, spread


def norm_back(hat, spread, gain, grad):
    weighted = grad * gain
    return spread * (
        weighted
        - jnp.mean(weighted, axis=-1, keepdims=True)
        - hat * jnp.mean(weighted * hat, axis=-1, keepdims=True)
    )


def on_device(
    inputs,
    ln_attn,
    w_query,
    w_key,
    w_value,
    w_out,
    head_scale,
    ln_post,
    ln_ffn,
    w_fc1,
    ln_mid,
    w_fc2,
    offsets,
    cotangent,
):
    row_count, span, model_width = inputs.shape
    head_count = head_scale.shape[0]
    head_dim = model_width // head_count
    token_count = row_count * span
    group = lax.axis_size("blk")
    heads = head_count // group
    width = heads * head_dim
    me = lax.axis_index("blk")

    x = inputs.astype(F32).reshape(token_count, model_width)
    x_hat, x_spread = norm_parts(x)
    normed = (x_hat * ln_attn).astype(BF16)

    def project(weight):
        product = jnp.dot(normed, weight, preferred_element_type=F32).astype(BF16)
        return product.reshape(row_count, span, group, width)

    qkv = jnp.stack([project(w_query), project(w_key), project(w_value)], axis=1)
    qkv = exchange(jnp.transpose(qkv, (3, 0, 1, 2, 4)))

    my_scale = lax.dynamic_slice(head_scale, (me * heads,), (heads,))
    scale_lanes = jnp.repeat(my_scale, head_dim).reshape(1, width)
    scaled_mine, lse = attend(offsets, qkv, scale_lanes, heads, head_dim)
    scaled = jnp.transpose(exchange(scaled_mine), (1, 2, 0, 3)).reshape(token_count, model_width)

    d_out = cotangent.reshape(token_count, model_width)
    d_mid = jnp.einsum("td,fd->tf", d_out, w_fc2, preferred_element_type=F32)

    proj = jnp.dot(scaled, w_out, preferred_element_type=F32)
    proj_hat, proj_spread = norm_parts(proj)
    residual = x + proj_hat * ln_post
    res_hat, res_spread = norm_parts(residual)
    ffn_in = (res_hat * ln_ffn).astype(BF16)
    pre = jnp.dot(ffn_in, w_fc1, preferred_element_type=F32)
    phi = 0.5 + 0.5 * lax.erf(pre * (0.5**0.5))
    act = pre * phi
    act_slope = phi + pre * jnp.exp(-0.5 * pre * pre) * 0.3989422804014327
    act_hat, act_spread = norm_parts(act)
    mid = (act_hat * ln_mid).astype(BF16)
    layer_out = (residual + jnp.dot(mid, w_fc2, preferred_element_type=F32)).astype(BF16)

    grad_fc2 = jnp.einsum("tf,td->fd", mid, d_out, preferred_element_type=F32).astype(BF16)
    grad_ln_mid = jnp.sum(d_mid * act_hat, axis=0)
    d_pre = (norm_back(act_hat, act_spread, ln_mid, d_mid) * act_slope).astype(BF16)
    grad_fc1 = jnp.einsum("td,tf->df", ffn_in, d_pre, preferred_element_type=F32).astype(BF16)
    d_ffn = jnp.einsum("tf,df->td", d_pre, w_fc1, preferred_element_type=F32)
    grad_ln_ffn = jnp.sum(d_ffn * res_hat, axis=0)
    d_residual = d_out.astype(F32) + norm_back(res_hat, res_spread, ln_ffn, d_ffn)
    grad_ln_post = jnp.sum(d_residual * proj_hat, axis=0)
    d_proj = norm_back(proj_hat, proj_spread, ln_post, d_residual).astype(BF16)
    grad_out = jnp.einsum("td,te->de", scaled, d_proj, preferred_element_type=F32).astype(BF16)
    d_scaled = jnp.einsum("te,de->td", d_proj, w_out, preferred_element_type=F32)
    d_attn = (d_scaled * jnp.repeat(head_scale, head_dim)).astype(BF16)
    d_attn = jnp.transpose(d_attn.reshape(row_count, span, group, width), (2, 0, 1, 3))
    d_attn = exchange(d_attn)

    dqkv, delta_sums = attend_back(
        offsets, qkv, d_attn, scaled_mine, 1.0 / scale_lanes, lse, heads, head_dim
    )
    my_grad = jnp.sum(delta_sums, axis=(0, 2))[:heads] / my_scale
    grad_scale = lax.dynamic_update_slice(jnp.zeros((head_count,), F32), my_grad, (me * heads,))
    dqkv = exchange(dqkv)
    dqkv = jnp.transpose(dqkv, (2, 1, 3, 0, 4)).reshape(3, token_count, model_width)

    def weight_grad(d_part):
        return jnp.einsum("td,te->de", normed, d_part, preferred_element_type=F32).astype(BF16)

    grads_qkv = [weight_grad(dqkv[n]) for n in range(3)]
    d_normed = sum(
        jnp.einsum("te,de->td", dqkv[n], weight, preferred_element_type=F32)
        for n, weight in enumerate((w_query, w_key, w_value))
    )
    grad_ln_attn = jnp.sum(d_normed * x_hat, axis=0)
    grad_inputs = d_residual + norm_back(x_hat, x_spread, ln_attn, d_normed)

    def reduced(part):
        return lax.psum_scatter(part.astype(BF16), "blk", scatter_dimension=0, tiled=True)

    sums = lax.psum(
        tuple(
            reduced(part)
            for part in (
                grad_ln_attn,
                grads_qkv[0],
                grads_qkv[1],
                grads_qkv[2],
                grad_out,
                grad_ln_post,
                grad_ln_ffn,
                grad_fc1,
                grad_ln_mid,
                grad_fc2,
            )
        ),
        "batch",
    )
    sums = [part.astype(F32) for part in sums]
    grad_scale = lax.psum(grad_scale, ("batch", "blk"))
    return (
        layer_out.reshape(row_count, span, model_width),
        grad_inputs.reshape(row_count, span, model_width),
        sums[0],
        sums[1],
        sums[2],
        sums[3],
        sums[4],
        grad_scale,
        sums[5],
        sums[6],
        sums[7],
        sums[8],
        sums[9],
    )


def solution(mesh):
    rows = P("batch", "blk", None)
    shard = P("blk", None)
    return jax.shard_map(
        on_device,
        mesh=mesh,
        in_specs=(rows,) + (P(),) * 11 + (P("batch", None), rows),
        out_specs=(
            rows,
            rows,
            P("blk"),
            shard,
            shard,
            shard,
            shard,
            P(),
            P("blk"),
            P("blk"),
            shard,
            P("blk"),
            shard,
        ),
        check_vma=False,
    )
```

time: 2910 us -> 1190 us (0.41)
  waiting for transfers between devices: 1810 us -> 731 us
  starting transfers between devices: 437 us -> 21.5 us
  local copies, waits for them, and re-layouts: 177 us -> 27.3 us
  Pallas kernels: 0 us -> 121 us
  other arithmetic: 172 us -> 59.9 us
  matrix products: 182 us -> 120 us
    ppermute x51 -> x0, waiting for transfers between devices: 1390 us -> none  [the longest x35 870 us: from_behind(): return lax.ppermute(block, axis, route)]
    ppermute x51 -> x0, starting transfers between devices: 436 us -> none  [the longest x35 321 us: from_behind(): return lax.ppermute(block, axis, route)]
    all_to_all x0 -> x4, waiting for transfers between devices: none -> 291 us  [exchange(): return lax.all_to_all(parts, 'blk', 0, 0, tiled=True)]
    pallas_call x0 -> x2, Pallas kernels: none -> 121 us  [the longest x1 73.8 us: attend_back(): pl.pallas_call(functools.partial(attend_back_kernel, heads, head_dim), gr...]
    while x37 -> x0, local copies, waits for them, and re-layouts: 102 us -> none
    dot_general x25 -> x18, matrix products: 182 us -> 120 us  [the longest x3 17.1 us: on_device(): jnp.einsum('te,de->td', dqkv[n], weight, preferred_element_type=F32)]
    convert_element_type x31 -> x14, other arithmetic: 75.7 us -> 34.4 us  [the longest x1 18.2 us: on_device(): (norm_back(act_hat, act_spread, ln_mid, d_mid) * act_slope).astype(BF16)]
    add x53 -> x1, other arithmetic: 35.7 us -> 6.06 us  [on_device(): grad_inputs = d_residual + norm_back(x_hat, x_spread, ln_attn, d_normed)]
  transfers between devices with their start and end apart: 58 -> 11, of which waited for: 56 -> 9; matrix products, arithmetic and copies ran while one was open for 7% -> 8% of each run, Pallas kernels for 0% -> 0%
where the time goes in v1:
time: 1190 us; the launch traced here: 1180 us
  waiting for transfers between devices  731 us (61%)
  Pallas kernels  121 us (10%)
  matrix products  120 us (10%)
  blocking collectives  84.3 us (7%)
  other arithmetic  59.9 us (5%)
  local copies, waits for them, and re-layouts  27.3 us (2%)
  starting transfers between devices  21.5 us (2%)
  between operations  16.4 us (1%)
    reduce_scatter x6, waiting for transfers between devices, reduced(): lax.psum_scatter(part.astype(BF16), 'blk', scatter_dimension=0, tiled=True)  426 us
    all_to_all x4, waiting for transfers between devices, exchange(): return lax.all_to_all(parts, 'blk', 0, 0, tiled=True)  291 us
    pallas_call x1, Pallas kernels, attend_back(): pl.pallas_call(functools.partial(attend_back_kernel, heads, head_dim), gr...  73.8 us
    pallas_call x1, Pallas kernels, attend(): pl.pallas_call(functools.partial(attend_kernel, heads, head_dim), grid_sp...  47.1 us
    psum x1, blocking collectives, on_device(): grad_scale = lax.psum(grad_scale, ('batch', 'blk'))  42.9 us
    unnamed x1, blocking collectives  35.2 us
  transfers between devices with their start and end apart: 11, of which 9 were waited for; matrix products, arithmetic and copies ran while one was open for 8% of the time, Pallas kernels for 0%

profile of v1, /device:TPU:0, one launch (start us, length us, event | category | flops | bytes accessed | tf_op | source)
XLA Modules:
  0.0 1180.8 jit_solution(16014260263790924690)
XLA Ops:
  24.2 7.4 all-to-all-start
  32.4 103.8 %all-to-all-done.qkv_ref = bf16[8,3,3,256,128]{4,3,2,1,0:T(8,128)(2,1)} async-done(((bf16[8,3,3,256,128]{4,3,2,1,0:T(8,128)(2,1)}), bf16[8,3,3,256,128]{4,3,2,1,0:T(8,128)(2,1)}, u32[]{:S(2)}, u32[]{:S(2)}) %all-to-all-start) | async-done | bytes 4718624 | tf_op jit(solution)/shard_map/all_to_all | solution.py:256
  136.1 47.1 %attend.1 = (bf16[8,3,256,128]{3,2,1,0:T(8,128)(2,1)}, f32[3,8,2,256]{3,2,1,0:T(2,128)}) custom-call(s32[3,4]{1,0:T(4,128)} %offs_ref.3, bf16[8,3,3,256,128]{4,3,2,1,0:T(8,128)(2,1)} %all-to-all-done.qkv_ref, f32[1,128]{1,0:T(1,128)} %reshape_reshape.3.scale_ref), custom_call_target="tpu_custom_call" | custom-call | tf_op jit(solution)/shard_map/attend/pallas_call | solution.py:137
  187.9 37.7 %all-to-all-done.1 = bf16[8,3,256,128]{3,2,1,0:T(8,128)(2,1)} async-done(((bf16[8,3,256,128]{3,2,1,0:T(8,128)(2,1)}), bf16[8,3,256,128]{3,2,1,0:T(8,128)(2,1)}, u32[]{:S(2)}, u32[]{:S(2)}) %all-to-all-start.1) | async-done | bytes 1572896 | tf_op jit(solution)/shard_map/all_to_all | solution.py:256
  233.3 12.9 %fusion.47 = (f32[768]{0:T(1024)S(1)}, f32[768,4096]{1,0:T(8,128)}, f32[768,4096]{1,0:T(8,128)}) fusion(bf16[1024,4096]{1,0:T(8,128)(2,1)S(1)} %bitcast.137, f32[768,1024]{1,0:T(8,128)S(1)} %get-tuple-element.51, f32[1024]{0:T(1024)S(1)} %copy-done.28, f32[768]{0:T(1024)S(1)} %add_rsqrt_fusion.1, f32[768]{0:T(1024)S(1)} %broadcast_multiply_fusion.9), kind=kOutput, calls=%fused_computation.105 | convolution fusion | flops 6461324288 | bytes 36713472 | tf_op jit(solution)/shard_map/dot_general | solution.py:324
  246.2 6.1 multiply_reduce_fusion.2
  252.3 16.6 %multiply_reduce_fusion = (bf16[4096]{0:T(1024)(128)(2,1)S(1)}, f32[768]{0:T(1024)S(1)}, f32[768]{0:T(1024)S(1)}, f32[768,4096]{1,0:T(8,128)}) fusion(f32[768,4096]{1,0:T(8,128)} %get-tuple-element.49, f32[768]{0:T(1024)S(1)} %add_rsqrt_fusion, f32[768]{0:T(1024)S(1)} %broadcast_multiply_fusion.2, f32[4096]{0:T(1024)S(1)} %copy-done.27, ...), kind=kOutput, calls=%fused_computation.7 | convolution fusion | flops 6467610624 | bytes 35164160 | tf_op jit(solution)/shard_map/td,fd->tf/dot_general | solution.py:317
  268.9 18.2 %fusion.5 = (bf16[768,4096]{1,0:T(8,128)(2,1)S(1)}, bf16[768,4096]{1,0:T(8,128)(2,1)}) fusion(f32[768,4096]{1,0:T(8,128)} %get-tuple-element.59, f32[768,4096]{1,0:T(8,128)} %get-tuple-element.60, f32[768,4096]{1,0:T(8,128)} %get-tuple-element.49, f32[768]{0:T(1024)S(1)} %get-tuple-element.63, f32[768]{0:T(1024)S(1)} %get-tuple-element.64, ...), kind=kLoop, calls=%fused_computation.6 | loop fusion | flops 59768832 | bytes 50360320 | tf_op jit(solution)/shard_map/convert_element_type | solution.py:334
  287.1 13.2 %multiply_reduce_fusion.4 = (bf16[1024]{0:T(1024)(128)(2,1)S(1)}, f32[768]{0:T(1024)S(1)}, f32[768]{0:T(1024)S(1)}, f32[768,1024]{1,0:T(8,128)}) fusion(f32[768,1024]{1,0:T(8,128)S(1)} %get-tuple-element.51, f32[768]{0:T(1024)S(1)} %add_rsqrt_fusion.1, f32[768]{0:T(1024)S(1)} %broadcast_multiply_fusion.9, f32[1024]{0:T(1024)S(1)} %copy-done.28, ...), kind=kOutput, calls=%fused_computation.37 | convolution fusion | flops 6448739328 | bytes 20989952 | tf_op jit(solution)/shard_map/tf,df->td/dot_general | solution.py:336
  316.2 37.8 %all-to-all-done.2.grad_ref = bf16[8,3,256,128]{3,2,1,0:T(8,128)(2,1)} async-done(((bf16[8,3,256,128]{3,2,1,0:T(8,128)(2,1)}), bf16[8,3,256,128]{3,2,1,0:T(8,128)(2,1)}, u32[]{:S(2)}, u32[]{:S(2)}) %all-to-all-start.2) | async-done | bytes 1572896 | tf_op jit(solution)/shard_map/all_to_all | solution.py:256
  354.0 73.8 %attend_back.1 = (bf16[8,3,3,256,128]{4,3,2,1,0:T(8,128)(2,1)}, f32[3,8,256]{2,1,0:T(8,128)}) custom-call(s32[3,4]{1,0:T(4,128)} %offs_ref.3, bf16[8,3,3,256,128]{4,3,2,1,0:T(8,128)(2,1)} %all-to-all-done.qkv_ref, bf16[8,3,256,128]{3,2,1,0:T(8,128)(2,1)} %all-to-all-done.2.grad_ref, bf16[8,3,256,128]{3,2,1,0:T(8,128)(2,1)} %get-tuple-element.17.out_ref, ...), custom_call_target="tpu_custom_call" | custom-call | tf_op jit(solution)/shard_map/attend_back/pallas_call | solution.py:243
  440.9 111.7 %all-to-all-done.3 = bf16[8,3,3,256,128]{4,3,2,1,0:T(8,128)(2,1)} async-done(((bf16[8,3,3,256,128]{4,3,2,1,0:T(8,128)(2,1)}), bf16[8,3,3,256,128]{4,3,2,1,0:T(8,128)(2,1)}, u32[]{:S(2)}, u32[]{:S(2)}) %all-to-all-start.3) | async-done | bytes 4718624 | tf_op jit(solution)/shard_map/all_to_all | solution.py:256
  576.9 12.4 %convolution_convert_fusion.1 = bf16[1024,4096]{1,0:T(8,128)(2,1)} fusion(bf16[768,4096]{1,0:T(8,128)(2,1)} %copy-done.4, f32[768,1024]{1,0:T(8,128)} %copy-done.3, f32[1024]{0:T(1024)S(1)} %copy-done.28, f32[768]{0:T(1024)S(1)} %add_rsqrt_fusion.1, f32[768]{0:T(1024)S(1)} %broadcast_multiply_fusion.9), kind=kOutput, calls=%fused_computation.15 | convolution fusion | flops 6449790976 | bytes 17836032 | tf_op jit(solution)/shard_map/td,tf->df/dot_general | solution.py:335
  589.4 11.3 convolution_convert_fusion
  603.5 12.6 %add_convert_fusion = bf16[768,1024]{1,0:T(8,128)(2,1)} fusion(f32[768,1024]{1,0:T(8,128)} %copy-done.3, bf16[768,4096]{1,0:T(8,128)(2,1)} %get-tuple-element.53, bf16[4096,1024]{1,0:T(8,128)(2,1)} %param.25), kind=kOutput, calls=%fused_computation.45 | convolution fusion | flops 6444023808 | bytes 19398656 | tf_op jit(solution)/shard_map/dot_general | solution.py:330
  616.1 42.9 %psum.82 = f32[16]{0:T(128)} all-reduce(f32[16]{0:T(128)S(1)} %divide_dynamic-update-slice_fusion), channel_id=1, replica_groups=mesh['batch'=4,'blk'=8] {'batch','blk'}, use_global_device_ids=true, to_apply=%region_28.0 | all-reduce | flops 16 | bytes 128 | tf_op jit(solution)/shard_map/psum | solution.py:388
  668.3 51.5 %reduce-scatter.7.cloned.1.call-done = bf16[128,1024]{1,0:T(8,128)(2,1)} async-done(((bf16[1024,1024]{1,0:T(8,128)(2,1)}), bf16[128,1024]{1,0:T(8,128)(2,1)}) %reduce-scatter.7.cloned.1.call-update) | async-done | bytes 262160 | tf_op jit(solution)/shard_map/reduce_scatter | solution.py:367
  719.8 70.9 %reduce-scatter.9.cloned.1.call-done = bf16[128,1024]{1,0:T(8,128)(2,1)} async-done(((bf16[1024,1024]{1,0:T(8,128)(2,1)}), bf16[128,1024]{1,0:T(8,128)(2,1)}) %reduce-scatter.9.cloned.1.call-update) | async-done | bytes 262160 | tf_op jit(solution)/shard_map/reduce_scatter | solution.py:367
  790.7 151.6 %reduce-scatter.15.cloned.1.call-done = bf16[128,4096]{1,0:T(8,128)(2,1)} async-done(((bf16[1024,4096]{1,0:T(8,128)(2,1)}), bf16[128,4096]{1,0:T(8,128)(2,1)}) %reduce-scatter.15.cloned.1.call-update) | async-done | bytes 1048592 | tf_op jit(solution)/shard_map/reduce_scatter | solution.py:367
  942.3 152.0 %reduce-scatter.17.cloned.1.call-done = bf16[512,1024]{1,0:T(8,128)(2,1)} async-done(((bf16[4096,1024]{1,0:T(8,128)(2,1)}), bf16[512,1024]{1,0:T(8,128)(2,1)}) %reduce-scatter.17.cloned.1.call-update) | async-done | bytes 1048592 | tf_op jit(solution)/shard_map/reduce_scatter | solution.py:367
  1094.4 7.8 fusion.21
  1102.2 35.2 %all-reduce.4 = (bf16[1024]{0:T(1024)(128)(2,1)S(1)}, bf16[1024]{0:T(1024)(128)(2,1)S(1)}, bf16[1024]{0:T(1024)(128)(2,1)S(1)}, bf16[4096]{0:T(1024)(128)(2,1)S(1)}) all-reduce(bf16[1024]{0:T(1024)(128)(2,1)S(1)} %get-tuple-element.28, bf16[1024]{0:T(1024)(128)(2,1)S(1)} %get-tuple-element.26, ...), channel_id=2, replica_groups=mesh['batch'=4,'blk'=8] {'blk'}, use_global_device_ids=true, to_apply=%region_17.0.clone | all-reduce | flops 7168 | bytes 28672
  1137.7 6.2 all-reduce.5
  1152.0 13.6 %all-reduce.9.cloned.1.call-done = (bf16[128,1024]{1,0:T(8,128)(2,1)}, bf16[128,1024]{1,0:T(8,128)(2,1)}, bf16[128,1024]{1,0:T(8,128)(2,1)}, bf16[128,1024]{1,0:...) async-done(((bf16[128,1024]{1,0:T(8,128)(2,1)}, bf16[128,1024]{1,0:T(8,128)(2,1)}, bf16[128,1024]{1,0:T(8,128)(2,1)}, bf16[128,1024]{1,0:T(8,128)(2,1)}, ...) | async-done | bytes 3145744 | tf_op jit(solution)/shard_map/psum | solution.py:369
  (174 shorter events, 110.1 us)
Async XLA Ops:
  7.2 12.1 %copy-start = (bf16[1024,1024]{1,0:T(8,128)(2,1)S(1)}, bf16[1024,1024]{1,0:T(8,128)(2,1)}, u32[]{:S(2)}) copy-start(bf16[1024,1024]{1,0:T(8,128)(2,1)} %param.18) | copy-start | bytes 6291460
  24.2 7.4 copy-start.29
  24.2 111.9 %all-to-all-start = ((bf16[8,3,3,256,128]{4,3,2,1,0:T(8,128)(2,1)}), bf16[8,3,3,256,128]{4,3,2,1,0:T(8,128)(2,1)}, u32[]{:S(2)}, u32[]{:S(2)}) async-start(bf16[8,3,3,256,128]{4,3,2,1,0:T(8,128)(2,1)} %maximum_bitcast_fusion), calls=%async_computation | async-start | bytes 9437184 | tf_op jit(solution)/shard_map/all_to_all | solution.py:256
  183.3 42.3 %all-to-all-start.1 = ((bf16[8,3,256,128]{3,2,1,0:T(8,128)(2,1)}), bf16[8,3,256,128]{3,2,1,0:T(8,128)(2,1)}, u32[]{:S(2)}, u32[]{:S(2)}) async-start(bf16[8,3,256,128]{3,2,1,0:T(8,128)(2,1)} %get-tuple-element.17.out_ref), calls=%async_computation.1 | async-start | bytes 3145728 | tf_op jit(solution)/shard_map/all_to_all | solution.py:256
  228.2 4.7 slice-start
  232.4 68.0 %copy-start.3 = (f32[768,1024]{1,0:T(8,128)}, f32[768,1024]{1,0:T(8,128)S(1)}, u32[]{:S(2)}) copy-start(f32[768,1024]{1,0:T(8,128)S(1)} %get-tuple-element.51) | copy-start | bytes 9437188
  246.2 6.1 copy-start.5
  246.2 6.1 copy-start.27
  287.1 13.2 %copy-start.4 = (bf16[768,4096]{1,0:T(8,128)(2,1)}, bf16[768,4096]{1,0:T(8,128)(2,1)S(1)}, u32[]{:S(2)}) copy-start(bf16[768,4096]{1,0:T(8,128)(2,1)S(1)} %get-tuple-element.52) | copy-start | bytes 18874372
  309.9 5.8 copy-start.30
  311.4 42.6 %all-to-all-start.2 = ((bf16[8,3,256,128]{3,2,1,0:T(8,128)(2,1)}), bf16[8,3,256,128]{3,2,1,0:T(8,128)(2,1)}, u32[]{:S(2)}, u32[]{:S(2)}) async-start(bf16[8,3,256,128]{3,2,1,0:T(8,128)(2,1)} %bitcast.117), calls=%async_computation.2 | async-start | bytes 3145728 | tf_op jit(solution)/shard_map/all_to_all | solution.py:256
  427.8 124.8 %all-to-all-start.3 = ((bf16[8,3,3,256,128]{4,3,2,1,0:T(8,128)(2,1)}), bf16[8,3,3,256,128]{4,3,2,1,0:T(8,128)(2,1)}, u32[]{:S(2)}, u32[]{:S(2)}) async-start(bf16[8,3,3,256,128]{4,3,2,1,0:T(8,128)(2,1)} %get-tuple-element.19), calls=%async_computation.3 | async-start | bytes 9437184 | tf_op jit(solution)/shard_map/all_to_all | solution.py:256
  432.4 235.9 %reduce-scatter.13.cloned.1.call-start = ((), (), s32[]{:S(2)}) async-start(), calls=%async_computation.13 | async-start | bytes 2359296 | tf_op jit(solution)/shard_map/reduce_scatter | solution.py:367
  437.6 230.7 %reduce-scatter.11.cloned.1.call-start = ((), (), s32[]{:S(2)}) async-start(), calls=%async_computation.12 | async-start | bytes 2359296 | tf_op jit(solution)/shard_map/reduce_scatter | solution.py:367
  562.6 157.2 %reduce-scatter.7.cloned.1.call-start = ((), (), s32[]{:S(2)}) async-start(), calls=%async_computation.10 | async-start | bytes 2359296 | tf_op jit(solution)/shard_map/reduce_scatter | solution.py:367
  569.7 221.0 %reduce-scatter.9.cloned.1.call-start = ((), (), s32[]{:S(2)}) async-start(), calls=%async_computation.11 | async-start | bytes 2359296 | tf_op jit(solution)/shard_map/reduce_scatter | solution.py:367
  576.7 365.7 %reduce-scatter.15.cloned.1.call-start = ((), (), s32[]{:S(2)}) async-start(), calls=%async_computation.14 | async-start | bytes 9437184 | tf_op jit(solution)/shard_map/reduce_scatter | solution.py:367
  589.3 505.0 %reduce-scatter.17.cloned.1.call-start = ((), (), s32[]{:S(2)}) async-start(), calls=%async_computation.15 | async-start | bytes 9437184 | tf_op jit(solution)/shard_map/reduce_scatter | solution.py:367
  600.7 565.0 %all-reduce.9.cloned.1.call-start = ((), (), s32[]{:S(2)}) async-start(), calls=%async_computation.16 | async-start | bytes 6291456 | tf_op jit(solution)/shard_map/psum | solution.py:369
  659.1 5.8 copy-start.10
  659.1 5.8 copy-start.35
  668.3 426.0 %copy-start.23 = (f32[768]{0:T(1024)S(1)}, f32[768]{0:T(1024)}, u32[]{:S(2)}) copy-start(f32[768]{0:T(1024)} %copy-done.22) | copy-start | bytes 9220
  668.3 426.0 %copy-start.25 = (f32[768]{0:T(1024)S(1)}, f32[768]{0:T(1024)}, u32[]{:S(2)}) copy-start(f32[768]{0:T(1024)} %copy-done.24) | copy-start | bytes 9220
  1165.6 5.3 copy-start.18
  (26 other events, 63.9 us)
Sparse Core Ops, SparseCore 0:
  437.7 140.3 reduce-scatter.12
  581.7 66.8 reduce-scatter.10
  652.7 67.0 reduce-scatter.6
  723.7 66.9 reduce-scatter.8
  794.2 148.0 reduce-scatter.14
  946.2 148.0 reduce-scatter.16
  1097.1 68.5 all-reduce.8

commit v2 on v1

v2 whole, which is shorter than its diff:
```python
import functools

import jax
import jax.numpy as jnp
from jax import lax
from jax.experimental import pallas as pl
from jax.experimental.pallas import tpu as pltpu
from jax.sharding import PartitionSpec as P

EPSILON = 1e-05
MASKED = -1e30
VMEM_BYTES = 50 * 1024 * 1024
COST_UNIT = 1.1e9
F32 = jnp.float32
BF16 = jnp.bfloat16
LAST = (((1,), (1,)), ((), ()))
FIRST = (((0,), (0,)), ((), ()))
SMEM = pl.BlockSpec(memory_space=pltpu.SMEM)
VMEM = pl.BlockSpec(memory_space=pltpu.VMEM)


def dot_last(left, right):
    return lax.dot_general(left, right, LAST, preferred_element_type=F32)


def dot_first(left, right):
    return lax.dot_general(left, right, FIRST, preferred_element_type=F32)


def dot(left, right):
    return jnp.dot(left, right, preferred_element_type=F32)


def kernel_params():
    return pltpu.CompilerParams(vmem_limit_bytes=VMEM_BYTES)


def cost(micros):
    return pl.CostEstimate(flops=int(micros * COST_UNIT), bytes_accessed=1024, transcendentals=0)


def exchange(parts):
    return lax.all_to_all(parts, "blk", 0, 0, tiled=True)


def norm_parts(rows_in):
    average = jnp.mean(rows_in, axis=-1, keepdims=True)
    centred = rows_in - average
    spread = lax.rsqrt(jnp.mean(centred * centred, axis=-1, keepdims=True) + EPSILON)
    return centred * spread, spread


def norm_back(hat, spread, gain, grad):
    weighted = grad * gain
    return spread * (
        weighted
        - jnp.mean(weighted, axis=-1, keepdims=True)
        - hat * jnp.mean(weighted * hat, axis=-1, keepdims=True)
    )


def project_kernel(x_ref, gain_ref, wq_ref, wk_ref, wv_ref, normed_ref, out_ref):
    group, _, _, width = out_ref.shape
    hat, _ = norm_parts(x_ref[...].astype(F32))
    normed = (hat * gain_ref[...]).astype(BF16)
    normed_ref[...] = normed
    for n, weight in enumerate((wq_ref, wk_ref, wv_ref)):
        product = dot(normed, weight[...]).astype(BF16)
        for s in range(group):
            out_ref[s, n] = product[:, s * width : (s + 1) * width]


def project(x_row, gain, w_query, w_key, w_value, group):
    span, model = x_row.shape
    return pl.pallas_call(
        project_kernel,
        out_shape=[
            jax.ShapeDtypeStruct((span, model), BF16),
            jax.ShapeDtypeStruct((group, 3, span, model // group), BF16),
        ],
        compiler_params=kernel_params(),
        cost_estimate=cost(5),
        name="project",
    )(x_row, gain, w_query, w_key, w_value)


def doc_start(offs_ref, row, pos):
    start = jnp.zeros_like(pos)
    for d in range(offs_ref.shape[1]):
        first = offs_ref[row, d]
        start = jnp.where(pos >= first, first, start)
    return start


def doc_end(offs_ref, row, pos, length):
    end = jnp.int32(length)
    for d in reversed(range(offs_ref.shape[1])):
        first = offs_ref[row, d]
        end = jnp.where(first > pos, first, end)
    return end


def head_lanes(shape, head, head_dim):
    lane = lax.broadcasted_iota(jnp.int32, shape, 1)
    return (lane >= head * head_dim) & (lane < (head + 1) * head_dim)


def attend_kernel(rows, heads, head_dim, offs_ref, scale_ref, *refs):
    count = len(rows)
    result_ref, lse_ref, score_ref = refs[count:]
    for n, row in enumerate(rows):
        attend_row(
            row,
            heads,
            head_dim,
            offs_ref,
            scale_ref,
            refs[n],
            result_ref.at[:, n],
            lse_ref.at[n],
            score_ref,
        )


def attend_row(
    row, heads, head_dim, offs_ref, scale_ref, held, result_ref, lse_ref, score_ref
):
    blocks, _, span, width = held.shape
    wide = score_ref.shape[-1]
    per = wide // span
    lanes = min(128, wide)
    score_scale = head_dim ** (-0.5)

    def query_block(i, carry):
        first_pos = i * span
        queries = held[i, 0] * jnp.asarray(score_scale, BF16)
        query_head = [
            jnp.where(head_lanes((span, width), h, head_dim), queries, 0).astype(BF16)
            for h in range(heads)
        ]
        query_pos = first_pos + lax.broadcasted_iota(jnp.int32, (span, 1), 0)
        query_start = doc_start(offs_ref, row, query_pos)
        low = doc_start(offs_ref, row, first_pos) // wide
        high = (first_pos + span - 1) // wide + 1

        def score_step(j, tops):
            keys = held[pl.ds(j * per, per), 1].reshape(wide, width)
            key_pos = j * wide + lax.broadcasted_iota(jnp.int32, (span, wide), 1)
            allowed = (key_pos >= query_start) & (key_pos <= query_pos)
            new = []
            for h in range(heads):
                scores = jnp.where(allowed, dot_last(query_head[h], keys), MASKED)
                score_ref[h, j] = scores
                top = tops[h]
                for c in range(0, wide, lanes):
                    top = jnp.maximum(top, scores[:, c : c + lanes])
                new.append(top)
            return tuple(new)

        tops = lax.fori_loop(
            low, high, score_step, tuple(jnp.full((span, lanes), MASKED, F32) for h in range(heads))
        )
        tops = [jnp.max(top, axis=1, keepdims=True) for top in tops]

        def value_step(j, state):
            values = held[pl.ds(j * per, per), 2].reshape(wide, width)
            new = []
            for h in range(heads):
                total, acc = state[h]
                probs = jnp.exp(score_ref[h, j] - tops[h])
                for c in range(0, wide, lanes):
                    total = total + probs[:, c : c + lanes]
                acc = acc + dot(probs.astype(BF16), values)
                new.append((total, acc))
            return tuple(new)

        state = lax.fori_loop(
            low,
            high,
            value_step,
            tuple(
                (jnp.zeros((span, lanes), F32), jnp.zeros((span, width), F32)) for h in range(heads)
            ),
        )
        result = jnp.zeros((span, width), F32)
        for h in range(heads):
            total = jnp.sum(state[h][0], axis=1, keepdims=True)
            result = jnp.where(head_lanes((span, width), h, head_dim), state[h][1] / total, result)
            log_total = tops[h] + jnp.log(total)
            lse_ref[i, h : h + 1, :] = jnp.transpose(jnp.broadcast_to(log_total, (span, 128)))[
                0:1, :
            ]
        result_ref[i] = (result * scale_ref[...]).astype(BF16)
        return carry

    lax.fori_loop(0, blocks, query_block, 0)


def attend(offsets, rows, qkv, scale_lanes, heads, head_dim):
    group, _, span, width = qkv[0].shape
    length = group * span
    wide = max(span, min(512, length))
    return pl.pallas_call(
        functools.partial(attend_kernel, rows, heads, head_dim),
        in_specs=[SMEM, VMEM] + [VMEM] * len(rows),
        out_shape=[
            jax.ShapeDtypeStruct((group, len(rows), span, width), BF16),
            jax.ShapeDtypeStruct((len(rows), group, heads, span), F32),
        ],
        scratch_shapes=[pltpu.VMEM((heads, length // wide, span, wide), F32)],
        compiler_params=kernel_params(),
        cost_estimate=cost(16),
        name="attend",
    )(offsets, scale_lanes, *qkv)


def attend_back_kernel(rows, heads, head_dim, offs_ref, inv_ref, grad_ref, *refs):
    count = len(rows)
    held, out_refs, lse_refs = refs[:count], refs[count : 2 * count], refs[2 * count : 3 * count]
    dqkv_ref, total_ref = refs[3 * count : 3 * count + 2]
    for n, row in enumerate(rows):
        attend_back_row(
            row,
            heads,
            head_dim,
            offs_ref,
            inv_ref,
            lse_refs[n],
            held[n],
            grad_ref.at[:, n],
            out_refs[n],
            dqkv_ref.at[:, n],
            total_ref.at[n],
            *refs[3 * count + 2 :],
        )


def attend_back_row(
    row,
    heads,
    head_dim,
    offs_ref,
    inv_ref,
    lse_ref,
    held,
    grad_ref,
    out_ref,
    dqkv_ref,
    total_ref,
    q_ref,
    k_ref,
    g_ref,
    delta_ref,
    dq_ref,
):
    blocks, _, span, width = held.shape
    score_scale = head_dim ** (-0.5)
    picks = lax.broadcasted_iota(jnp.int32, (8, width), 0)
    lane = lax.broadcasted_iota(jnp.int32, (8, width), 1)
    ones = jnp.where(lane // head_dim == picks, 1.0, 0.0).astype(F32)

    def prepare(i, carry):
        queries = held[i, 0] * jnp.asarray(score_scale, BF16)
        keys = held[i, 1]
        grads = grad_ref[i]
        for h in range(heads):
            mine = head_lanes((span, width), h, head_dim)
            q_ref[h, i] = jnp.where(mine, queries, 0).astype(BF16)
            k_ref[h, i] = jnp.where(mine, keys, 0).astype(BF16)
            g_ref[h, i] = jnp.where(mine, grads, 0).astype(BF16)
        product = grads.astype(F32) * out_ref[i].astype(F32) * inv_ref[...]
        delta_ref[i] = lax.dot_general(
            ones, product, LAST, precision=lax.Precision.HIGHEST, preferred_element_type=F32
        )
        dq_ref[i] = jnp.zeros((span, width), F32)
        return carry + delta_ref[i]

    total_ref[...] = lax.fori_loop(0, blocks, prepare, jnp.zeros((8, span), F32))

    def key_block(j, carry):
        keys = held[j, 1]
        values = held[j, 2]
        key_pos = j * span + lax.broadcasted_iota(jnp.int32, (span, 1), 0)
        last = (doc_end(offs_ref, row, (j + 1) * span - 1, blocks * span) - 1) // span + 1

        def query_step(i, state):
            dk, dv = state
            query_pos = i * span + lax.broadcasted_iota(jnp.int32, (1, span), 1)
            query_start = doc_start(offs_ref, row, query_pos)
            allowed = (key_pos >= query_start) & (key_pos <= query_pos)
            dq = dq_ref[i]
            for h in range(heads):
                scores = dot_last(keys, q_ref[h, i])
                scores = jnp.where(allowed, scores - lse_ref[i, h : h + 1, :], MASKED)
                probs = jnp.exp(scores)
                d_probs = dot_last(values, g_ref[h, i])
                d_scores = (probs * (d_probs - delta_ref[i, h : h + 1, :])).astype(BF16)
                dv = dv + dot(probs.astype(BF16), g_ref[h, i])
                dk = dk + dot(d_scores, q_ref[h, i])
                dq = dq + dot_first(d_scores, k_ref[h, j])
            dq_ref[i] = dq
            return (dk, dv)

        zero = jnp.zeros((span, width), F32)
        dk, dv = lax.fori_loop(j, last, query_step, (zero, zero))
        dqkv_ref[j, 1] = dk.astype(BF16)
        dqkv_ref[j, 2] = dv.astype(BF16)
        dqkv_ref[j, 0] = (dq_ref[j] * score_scale).astype(BF16)
        return carry

    lax.fori_loop(0, blocks, key_block, 0)


def attend_back(offsets, rows, qkv, grads, scaled, inverse_lanes, lse, heads, head_dim):
    group, _, span, width = qkv[0].shape
    count = len(rows)
    return pl.pallas_call(
        functools.partial(attend_back_kernel, rows, heads, head_dim),
        in_specs=[SMEM] + [VMEM] * (2 + 3 * count),
        out_shape=[
            jax.ShapeDtypeStruct((group, count, 3, span, width), BF16),
            jax.ShapeDtypeStruct((count, 8, span), F32),
        ],
        scratch_shapes=[pltpu.VMEM((heads, group, span, width), BF16)] * 3
        + [pltpu.VMEM((group, 8, span), F32), pltpu.VMEM((group, span, width), F32)],
        compiler_params=kernel_params(),
        cost_estimate=cost(26),
        name="attend_back",
    )(offsets, inverse_lanes, grads, *qkv, *scaled, *lse)


def join_grads_kernel(parts, in_ref, out_ref):
    group = in_ref.shape[0]
    for n in range(3):
        whole = jnp.concatenate([in_ref[s, 0, n] for s in range(group)], axis=1)
        piece = whole.shape[1] // parts
        for p in range(parts):
            to = (p * 3 + n) * piece
            out_ref[:, to : to + piece] = whole[:, p * piece : (p + 1) * piece]


def join_grads(block):
    group, _, _, span, width = block.shape
    return pl.pallas_call(
        functools.partial(join_grads_kernel, PARTS),
        out_shape=jax.ShapeDtypeStruct((span, 3 * group * width), BF16),
        compiler_params=kernel_params(),
        cost_estimate=cost(1.5),
        name="join_grads",
    )(block)


FF_STEP = 512


def layer_kernel(
    o_ref,
    x_ref,
    d_out_ref,
    post_ref,
    ffn_ref,
    mid_gain_ref,
    scale_ref,
    w_out_ref,
    d_mid_hbm,
    w_fc1_hbm,
    scaled_ref,
    ffn_in_ref,
    residual_ref,
    mid_ref,
    d_pre_ref,
    d_proj_ref,
    d_residual_ref,
    d_attn_ref,
    g_post_ref,
    g_ffn_ref,
    g_mid_ref,
    d_mid_ref,
    w_fc1_ref,
    act_ref,
    slope_ref,
    sems,
    *,
    row,
):
    group, _, span, width = o_ref.shape
    hidden = act_ref.shape[1]
    steps = [slice(c, c + FF_STEP) for c in range(0, hidden, FF_STEP)]
    weight_copies = [
        pltpu.make_async_copy(w_fc1_hbm.at[:, at], w_fc1_ref.at[:, at], sems.at[c])
        for c, at in enumerate(steps)
    ]
    mid_copy = pltpu.make_async_copy(
        d_mid_hbm.at[row * span : (row + 1) * span, :], d_mid_ref, sems.at[len(steps)]
    )
    for copy in weight_copies:
        copy.start()
    mid_copy.start()

    scaled = jnp.concatenate([o_ref[s, 0] for s in range(group)], axis=1)
    scaled_ref[...] = scaled
    proj_hat, proj_spread = norm_parts(dot(scaled, w_out_ref[...]))
    residual = x_ref[...].astype(F32) + proj_hat * post_ref[...]
    residual_ref[...] = residual
    res_hat, res_spread = norm_parts(residual)
    ffn_in = (res_hat * ffn_ref[...]).astype(BF16)
    ffn_in_ref[...] = ffn_in

    total = jnp.zeros((span, 1), F32)
    for c, at in enumerate(steps):
        weight_copies[c].wait()
        pre = dot(ffn_in, w_fc1_ref[:, at])
        phi = 0.5 + 0.5 * lax.erf(pre * (0.5**0.5))
        act = pre * phi
        act_ref[:, at] = act
        slope_ref[:, at] = phi + pre * jnp.exp(-0.5 * pre * pre) * 0.3989422804014327
        total += jnp.sum(act, axis=1, keepdims=True)
    average = total / hidden
    total = jnp.zeros((span, 1), F32)
    for at in steps:
        centred = act_ref[:, at] - average
        total += jnp.sum(centred * centred, axis=1, keepdims=True)
    spread = lax.rsqrt(total / hidden + EPSILON)

    mid_copy.wait()
    sum_weighted = jnp.zeros((span, 1), F32)
    sum_hat = jnp.zeros((span, 1), F32)
    for at in steps:
        hat = (act_ref[:, at] - average) * spread
        act_ref[:, at] = hat
        gain = mid_gain_ref[:, at]
        mid_ref[:, at] = (hat * gain).astype(BF16)
        grad = d_mid_ref[:, at]
        product = grad * hat
        g_mid_ref[:, at] = jnp.sum(product, axis=0, keepdims=True)
        sum_weighted += jnp.sum(grad * gain, axis=1, keepdims=True)
        sum_hat += jnp.sum(product * gain, axis=1, keepdims=True)
    sum_weighted = sum_weighted / hidden
    sum_hat = sum_hat / hidden
    d_ffn = jnp.zeros(x_ref.shape, F32)
    for at in steps:
        weighted = d_mid_ref[:, at] * mid_gain_ref[:, at]
        d_act = spread * (weighted - sum_weighted - act_ref[:, at] * sum_hat)
        d_pre = (d_act * slope_ref[:, at]).astype(BF16)
        d_pre_ref[:, at] = d_pre
        d_ffn += dot_last(d_pre, w_fc1_ref[:, at])

    g_ffn_ref[...] = jnp.sum(d_ffn * res_hat, axis=0, keepdims=True)
    d_residual = d_out_ref[...].astype(F32) + norm_back(res_hat, res_spread, ffn_ref[...], d_ffn)
    d_residual_ref[...] = d_residual
    g_post_ref[...] = jnp.sum(d_residual * proj_hat, axis=0, keepdims=True)
    d_proj = norm_back(proj_hat, proj_spread, post_ref[...], d_residual).astype(BF16)
    d_proj_ref[...] = d_proj
    d_attn = (dot_last(d_proj, w_out_ref[...]) * scale_ref[...]).astype(BF16)
    for s in range(group):
        d_attn_ref[s, 0] = d_attn[:, s * width : (s + 1) * width]


def layer(row, o_blocks, x_row, d_out_row, gains, w_out, d_mid, w_fc1):
    span, model = x_row.shape
    hidden = w_fc1.shape[1]
    shape = jax.ShapeDtypeStruct
    return pl.pallas_call(
        functools.partial(layer_kernel, row=row),
        in_specs=[VMEM] * 8 + [pl.BlockSpec(memory_space=pl.ANY)] * 2,
        out_shape=[
            shape((span, model), BF16),
            shape((span, model), BF16),
            shape((span, model), F32),
            shape((span, hidden), BF16),
            shape((span, hidden), BF16),
            shape((span, model), BF16),
            shape((span, model), F32),
            shape(o_blocks.shape, BF16),
            shape((1, model), F32),
            shape((1, model), F32),
            shape((1, hidden), F32),
        ],
        scratch_shapes=[
            pltpu.VMEM((span, hidden), F32),
            pltpu.VMEM(w_fc1.shape, BF16),
            pltpu.VMEM((span, hidden), F32),
            pltpu.VMEM((span, hidden), F32),
            pltpu.SemaphoreType.DMA((hidden // FF_STEP + 1,)),
        ],
        compiler_params=kernel_params(),
        cost_estimate=cost(16),
        name="layer",
    )(o_blocks, x_row, d_out_row, *gains, w_out, d_mid, w_fc1)


def layer_out_kernel(*refs):
    count = (len(refs) - 2) // 2
    weight, out_ref = refs[-2], refs[-1]
    for r in range(count):
        out_ref[r] = (refs[r][...] + dot(refs[count + r][...], weight[...])).astype(BF16)


def last_step(residuals, mids, w_fc2):
    return pl.pallas_call(
        layer_out_kernel,
        out_shape=jax.ShapeDtypeStruct((len(mids),) + residuals[0].shape, BF16),
        compiler_params=kernel_params(),
        cost_estimate=cost(13),
        name="layer_out",
    )(*residuals, *mids, w_fc2)


def flip(value, axis, bit):
    size = lax.axis_size(axis)
    return lax.ppermute(value, axis, [(i, i ^ (1 << bit)) for i in range(size)])


def bits(axis):
    return (lax.axis_size(axis) - 1).bit_length()


def add(left, right):
    return (left.astype(F32) + right.astype(F32)).astype(BF16)


def sum_small(value):
    for axis in ("batch", "blk"):
        for bit in range(bits(axis)):
            value = value + flip(value, axis, bit)
    return value


PARTS = 4


def weight_kernel(count, rows, added, part_ref, *refs):
    out_ref = refs[-1]
    extras = refs[2 * count * rows : 2 * count * rows + added]
    at = 0
    for n in range(count):
        lefts = refs[2 * n * rows : (2 * n + 1) * rows]
        rights = refs[(2 * n + 1) * rows : (2 * n + 2) * rows]
        width = rights[0].shape[1]
        total = sum(dot_first(left[...], right[...]) for left, right in zip(lefts, rights))
        for extra in extras:
            total = total + extra[0, :, at : at + width].astype(F32)
        out_ref[0, :, at : at + width] = total.astype(BF16)
        at += width


def weight_part_plain(pairs, part, extras, group):
    pieces = []
    for lefts, rights, kind in pairs:
        left, right = jnp.concatenate(lefts), jnp.concatenate(rights)
        if kind == "columns":
            wide = right.shape[1] // PARTS
            right = lax.dynamic_slice(right, (0, part * wide), (right.shape[0], wide))
            left = left.reshape(left.shape[0], group, -1)
        else:
            left = left.reshape(left.shape[0], group, PARTS, -1)
            left = lax.dynamic_index_in_dim(left, part, 2, keepdims=False)
        pieces.append(jnp.einsum("tsd,te->sde", left, right, preferred_element_type=F32))
    total = jnp.concatenate(pieces, axis=2)
    for extra in extras:
        total = total + extra.astype(F32)
    return total.astype(BF16)


def weight_part(pairs, part, extras, group):
    specs, width = [], 0
    for lefts, rights, kind in pairs:
        span, model = lefts[0].shape
        if kind == "columns":
            high, wide = model // group, rights[0].shape[1] // PARTS
            left_spec = pl.BlockSpec((span, high), lambda s, p: (0, s))
            right_spec = pl.BlockSpec((span, wide), lambda s, p: (0, p[0]))
        else:
            high, wide = model // group // PARTS, rights[0].shape[1]
            left_spec = pl.BlockSpec((span, high), lambda s, p: (0, s * PARTS + p[0]))
            right_spec = pl.BlockSpec((span, wide), lambda s, p: (0, 0))
        specs += [left_spec] * len(lefts) + [right_spec] * len(rights)
        width += wide
    if high % 128:
        return weight_part_plain(pairs, part, extras, group)
    block = pl.BlockSpec((1, high, width), lambda s, p: (s, 0, 0))
    arrays = [array for lefts, rights, _ in pairs for array in (*lefts, *rights)]
    return pl.pallas_call(
        functools.partial(weight_kernel, len(pairs), len(pairs[0][0]), len(extras)),
        grid_spec=pltpu.PrefetchScalarGridSpec(
            num_scalar_prefetch=1,
            grid=(group,),
            in_specs=specs + [block] * len(extras),
            out_specs=block,
        ),
        out_shape=jax.ShapeDtypeStruct((group, high, width), BF16),
        compiler_params=kernel_params(),
        cost_estimate=cost(7.5),
        name="weight_part",
    )(part.astype(jnp.int32).reshape(1), *arrays, *extras)


class WeightSum:
    def __init__(self, order, *pairs):
        self.order, self.pairs = order, pairs
        batch_at = lax.axis_index("batch")
        self.near, self.far = batch_at & 1, (batch_at >> 1) & 1

    def piece(self, near, far, *extras):
        def part_of(part):
            return weight_part(self.pairs, part, extras, lax.axis_size("blk"))

        return self.order(part_of, near * 2 + far)

    def away_far(self):
        self.first = flip(self.piece(1 - self.near, 1 - self.far), "batch", 0)

    def send_far(self):
        self.arrived = flip(self.piece(self.near, 1 - self.far, self.first), "batch", 1)

    def away_near(self):
        self.second = flip(self.piece(1 - self.near, self.far), "batch", 0)

    def keep(self):
        return self.piece(self.near, self.far, self.second, self.arrived)


class Order:
    def __init__(self):
        self.last = ()

    def __call__(self, step, *values):
        self.last = step(*tie(values, self.last))
        return self.last


def tie(values, *after):
    return lax.optimization_barrier((values, after))[0]


def halve(mine, bit):
    at = (lax.axis_index("blk") >> bit) & 1
    halves = mine.reshape((-1, 2) + mine.shape[1:])
    keep = lax.dynamic_index_in_dim(halves, at, 1, keepdims=False)
    send = lax.dynamic_index_in_dim(halves, 1 - at, 1, keepdims=False)
    return add(keep, flip(send, "blk", bit))


def halve_rest(mine, start):
    batch_at = lax.axis_index("batch")
    near, far = batch_at & 1, (batch_at >> 1) & 1
    for bit in range(start, bits("blk")):
        mine = halve(mine, bit)
    mine = mine[0]
    for bit in range(2, bits("batch")):
        mine = add(mine, flip(mine, "batch", bit))
    other = flip(mine, "batch", 1)
    pair = jnp.stack([jnp.where(far == 0, mine, other), jnp.where(far == 0, other, mine)])
    away = flip(pair, "batch", 0)
    first = jnp.where(near == 0, pair, away).astype(F32)
    second = jnp.where(near == 0, away, pair).astype(F32)
    return [first[0], first[1], second[0], second[1]]


def input_grad_kernel(parts, rows, x_ref, gain_ref, wq_ref, wk_ref, wv_ref, *refs):
    out_ref, sum_ref = refs[2 * rows :]
    model = wq_ref.shape[0]
    piece = model // parts
    total = jnp.zeros(sum_ref.shape, F32)
    for r in range(rows):
        d_ref, res_ref = refs[r], refs[rows + r]
        grad = jnp.zeros(res_ref.shape, F32)
        for p in range(parts):
            for n, weight in enumerate((wq_ref, wk_ref, wv_ref)):
                at = (p * 3 + n) * piece
                grad += dot_last(d_ref[:, at : at + piece], weight[:, p * piece : (p + 1) * piece])
        hat, spread = norm_parts(x_ref[r].astype(F32))
        out_ref[r] = res_ref[...] + norm_back(hat, spread, gain_ref[...], grad)
        total += jnp.sum(grad * hat, axis=0, keepdims=True)
    sum_ref[...] = total


def input_grad(x, gain, w_query, w_key, w_value, d_rows, d_residuals):
    return pl.pallas_call(
        functools.partial(input_grad_kernel, PARTS, len(d_rows)),
        out_shape=[
            jax.ShapeDtypeStruct(x.shape, F32),
            jax.ShapeDtypeStruct((1, x.shape[2]), F32),
        ],
        compiler_params=kernel_params(),
        cost_estimate=cost(13),
        name="input_grad",
    )(x, gain, w_query, w_key, w_value, *d_rows, *d_residuals)


def on_device(
    inputs,
    ln_attn,
    w_query,
    w_key,
    w_value,
    w_out,
    head_scale,
    ln_post,
    ln_ffn,
    w_fc1,
    ln_mid,
    w_fc2,
    offsets,
    cotangent,
):
    row_count, span, model = inputs.shape
    head_count = head_scale.shape[0]
    head_dim = model // head_count
    tokens = row_count * span
    group = lax.axis_size("blk")
    heads = head_count // group
    width = heads * head_dim
    my_index = lax.axis_index("blk")
    rows = range(row_count)

    order = Order()
    gain = ln_attn.reshape(1, model)
    normed, qkv = [], []
    for r in rows:

        def project_row(x_row):
            return project(x_row, gain, w_query, w_key, w_value, group)

        normed_row, sent = order(project_row, inputs[r])
        normed.append(normed_row)
        qkv.append(exchange(tie(sent, qkv[-1:])))

    def middle_grad(grad, _):
        return jnp.einsum("td,fd->tf", grad, w_fc2, preferred_element_type=F32)

    d_mid = order(middle_grad, cotangent.reshape(tokens, model), qkv[0])

    my_scale = lax.dynamic_slice(head_scale, (my_index * heads,), (heads,))
    scale_lanes = jnp.repeat(my_scale, head_dim).reshape(1, width)
    scaled_mine, lse = [], []
    for r in rows:

        def attend_one(held):
            return attend(offsets, [r], [held], scale_lanes, heads, head_dim)

        out, log_total = order(attend_one, qkv[r])
        scaled_mine.append(out)
        lse.append(log_total)
    early = exchange(tie(jnp.concatenate(scaled_mine[:-1], axis=1), qkv[-1]))
    late = exchange(tie(scaled_mine[-1], early))

    layer_gains = [
        ln_post.reshape(1, model),
        ln_ffn.reshape(1, model),
        ln_mid.reshape(1, -1),
        jnp.repeat(head_scale, head_dim).reshape(1, model),
    ]
    layers = []
    for r in rows:

        def layer_row(o_blocks):
            return layer(
                r, o_blocks, inputs[r], cotangent[r], layer_gains, w_out, d_mid, w_fc1
            )

        layers.append(order(layer_row, early[:, r : r + 1] if r < row_count - 1 else late))
    (
        scaled,
        ffn_in,
        residual,
        mid,
        d_pre,
        d_proj,
        d_residual,
        d_attn,
        g_post,
        g_ffn,
        g_mid,
    ) = zip(*layers)
    first_heads = exchange(tie(d_attn[0], late))
    rest_heads = exchange(tie(jnp.concatenate(d_attn[1:], axis=1), first_heads))
    d_out = [cotangent[r] for r in rows]

    totals, sent = [], []

    def back(r, row_heads):
        def back_row(held, grads):
            return attend_back(
                offsets,
                [r],
                [held],
                grads,
                [scaled_mine[r].reshape(group, span, width)],
                1.0 / scale_lanes,
                [lse[r].reshape(lse[r].shape[1:])],
                heads,
                head_dim,
            )

        out, total = order(back_row, qkv[r], row_heads)
        totals.append(total)
        sent.append(out)

    sum_fc2 = WeightSum(order, (mid, d_out, "rows"))
    sum_rest = WeightSum(order, (ffn_in, d_pre, "columns"), (scaled, d_proj, "columns"))
    back(0, first_heads)
    grads = [exchange(tie(sent[0], rest_heads))]
    sum_fc2.away_far()
    sum_rest.away_far()
    sum_fc2.send_far()
    sum_rest.send_far()
    for r in rows[1:]:
        back(r, rest_heads[:, r - 1 : r])
        grads.append(exchange(tie(sent[r], grads)))
    sum_fc2.away_near()
    sum_rest.away_near()
    mine_fc2 = halve(sum_fc2.keep(), 0)
    mine_rest = halve(sum_rest.keep(), 0)
    d_rows = [order(join_grads, part) for part in grads]
    sum_qkv = WeightSum(order, (normed, d_rows, "columns"))
    sum_qkv.away_far()
    sum_qkv.away_near()
    sum_qkv.send_far()

    def input_step(x):
        return input_grad(x, gain, w_query, w_key, w_value, d_rows, d_residual)

    grad_inputs, grad_ln_attn = order(input_step, inputs)

    def output_step(weight):
        return last_step(residual, mid, weight)

    layer_out = order(output_step, w_fc2)
    mine_qkv = sum_qkv.keep()
    grads_ffn = halve_rest(tie(jnp.concatenate([mine_fc2, mine_rest], axis=2), d_rows), 1)
    grads_qkv = halve_rest(mine_qkv, 0)
    delta_sum = sum(jnp.sum(total, axis=(0, 2)) for total in totals)
    my_grad = delta_sum[:heads] / my_scale
    scale_part = lax.dynamic_update_slice(
        jnp.zeros((head_count,), F32), my_grad, (my_index * heads,)
    )
    gains = sum_small(
        jnp.concatenate(
            [grad_ln_attn[0], sum(g_post)[0], sum(g_ffn)[0], sum(g_mid)[0], scale_part]
        )
    )
    ends = [0, model, 2 * model, 3 * model, 3 * model + ln_mid.shape[0]]
    ends.append(ends[-1] + head_count)
    gains = [gains[low:high] for low, high in zip(ends[:-1], ends[1:])]

    def shard_of(vector):
        part = vector.shape[0] // group
        return lax.dynamic_slice(vector, (my_index * part,), (part,))

    def whole(parts, start, width, axis=1):
        return jnp.concatenate([part[:, start : start + width] for part in parts], axis=axis)

    piece = model // PARTS
    ff_piece = w_fc1.shape[1] // PARTS
    return (
        layer_out,
        grad_inputs,
        shard_of(gains[0]),
        whole(grads_qkv, 0, piece),
        whole(grads_qkv, piece, piece),
        whole(grads_qkv, 2 * piece, piece),
        whole(grads_ffn, model + ff_piece, piece),
        gains[4],
        shard_of(gains[1]),
        shard_of(gains[2]),
        whole(grads_ffn, model, ff_piece),
        shard_of(gains[3]),
        whole(grads_ffn, 0, model, 0),
    )


def solution(mesh):
    rows = P("batch", "blk", None)
    shard = P("blk", None)
    return jax.shard_map(
        on_device,
        mesh=mesh,
        in_specs=(rows,) + (P(),) * 11 + (P("batch", None), rows),
        out_specs=(
            rows,
            rows,
            P("blk"),
            shard,
            shard,
            shard,
            shard,
            P(),
            P("blk"),
            P("blk"),
            shard,
            P("blk"),
            shard,
        ),
        check_vma=False,
    )
```

time: 1190 us -> 709 us (0.60)
  waiting for transfers between devices: 731 us -> 225 us
  Pallas kernels: 121 us -> 319 us
  matrix products: 120 us -> 12.6 us
  blocking collectives: 84.3 us -> 0 us
  starting transfers between devices: 21.5 us -> 78.2 us
  other arithmetic: 59.9 us -> 16.9 us
  between operations: 16.4 us -> 2.28 us
  local copies, waits for them, and re-layouts: 27.3 us -> 41.1 us
    reduce_scatter x6 -> x0, waiting for transfers between devices: 426 us -> none  [reduced(): lax.psum_scatter(part.astype(BF16), 'blk', scatter_dimension=0, tiled=True)]
    all_to_all x4 -> x10, waiting for transfers between devices: 291 us -> 67.8 us  [exchange(): return lax.all_to_all(parts, 'blk', 0, 0, tiled=True)]
    pallas_call x2 -> x29, Pallas kernels: 121 us -> 319 us  [the longest x3 85.5 us: attend_back(): pl.pallas_call(functools.partial(attend_back_kernel, rows, heads, head_di...]
    ppermute x0 -> x25, waiting for transfers between devices: none -> 157 us  [flip(): return lax.ppermute(value, axis, [(i, i ^ 1 << bit) for i in range(size)])]
    dot_general x18 -> x1, matrix products: 120 us -> 12.6 us  [middle_grad(): return jnp.einsum('td,fd->tf', grad, w_fc2, preferred_element_type=F32)]
    psum x2 -> x0, blocking collectives: 49.1 us -> none  [the longest x1 42.9 us: on_device(): grad_scale = lax.psum(grad_scale, ('batch', 'blk'))]
    unnamed x1 -> x0, blocking collectives: 35.2 us -> none
    convert_element_type x14 -> x7, other arithmetic: 34.4 us -> 4.89 us  [the longest x5 4.47 us: add(): return (left.astype(F32) + right.astype(F32)).astype(BF16)]
  transfers between devices with their start and end apart: 11 -> 35, of which waited for: 9 -> 19; matrix products, arithmetic and copies ran while one was open for 8% -> 5% of each run, Pallas kernels for 0% -> 40%
where the time goes in v2:
time: 709 us; the launch traced here: 695 us
  Pallas kernels  319 us (45%)
  waiting for transfers between devices  225 us (32%)
  starting transfers between devices  78.2 us (11%)
  local copies, waits for them, and re-layouts  41.1 us (6%)
  other arithmetic  16.9 us (2%)
  matrix products  12.6 us (2%)
    ppermute x25, waiting for transfers between devices, flip(): return lax.ppermute(value, axis, [(i, i ^ 1 << bit) for i in range(size)])  157 us
    pallas_call x3, Pallas kernels, attend_back(): pl.pallas_call(functools.partial(attend_back_kernel, rows, heads, head_di...  85.5 us
    pallas_call x12, Pallas kernels, weight_part(): pl.pallas_call(functools.partial(weight_kernel, len(pairs), len(pairs[0][...  83.9 us
    all_to_all x10, waiting for transfers between devices, exchange(): return lax.all_to_all(parts, 'blk', 0, 0, tiled=True)  67.8 us
    pallas_call x3, Pallas kernels, attend(): pl.pallas_call(functools.partial(attend_kernel, rows, heads, head_dim), i...  52.4 us
    pallas_call x3, Pallas kernels, layer(): pl.pallas_call(functools.partial(layer_kernel, row=row), in_specs=[VMEM]...  50.9 us
    all_to_all x10, starting transfers between devices, exchange(): return lax.all_to_all(parts, 'blk', 0, 0, tiled=True)  49 us
    ppermute x25, starting transfers between devices, flip(): return lax.ppermute(value, axis, [(i, i ^ 1 << bit) for i in range(size)])  29.1 us
  transfers between devices with their start and end apart: 35, of which 19 were waited for; matrix products, arithmetic and copies ran while one was open for 5% of the time, Pallas kernels for 40%

profile of v2, /device:TPU:0, one launch (start us, length us, event | category | flops | bytes accessed | tf_op | source)
XLA Modules:
  0.0 695.3 jit_solution(16368068036827521098)
XLA Ops:
  24.3 30.1 %all-to-all-done.refs_0_ = bf16[8,3,256,128]{3,2,1,0:T(8,128)(2,1)S(1)} async-done(((bf16[8,3,256,128]{3,2,1,0:T(8,128)(2,1)}), bf16[8,3,256,128]{3,2,1,0:T(8,128)(2,1)S(1)}, u32[]{:S(2)}, u32[]{:S(2)}) %all-to-all-start) | async-done | bytes 1572896 | tf_op jit(solution)/shard_map/all_to_all | solution.py:43
  68.2 12.6 %fusion.18.d_mid_hbm = f32[768,4096]{1,0:T(8,128)} fusion(bf16[768,1024]{1,0:T(8,128)(2,1)S(1)} %bitcast.134, bf16[4096,1024]{1,0:T(8,128)(2,1)} %refs_6_), kind=kOutput, calls=%fused_computation.76 | convolution fusion | flops 6442450944 | bytes 22544384 | tf_op jit(solution)/shard_map/td,fd->tf/dot_general | solution.py:730
  80.8 14.6 %all-to-all-done.1.refs_0_ = bf16[8,3,256,128]{3,2,1,0:T(8,128)(2,1)S(1)} async-done(((bf16[8,3,256,128]{3,2,1,0:T(8,128)(2,1)}), bf16[8,3,256,128]{3,2,1,0:T(8,128)(2,1)S(1)}, u32[]{:S(2)}, u32[]{:S(2)}) %all-to-all-start.1) | async-done | bytes 1572896 | tf_op jit(solution)/shard_map/all_to_all | solution.py:43
  99.7 18.6 %attend.3 = (bf16[8,1,256,128]{3,2,1,0:T(8,128)(2,1)S(1)}, f32[1,8,2,256]{3,2,1,0:T(2,128)S(1)}) custom-call(s32[3,4]{1,0:T(4,128)S(1)} %copy-done.28, f32[1,128]{1,0:T(1,128)S(1)} %reshape_reshape.6.scale_ref, bf16[8,3,256,128]{3,2,1,0:T(8,128)(2,1)S(1)} %all-to-all-done.refs_0_), custom_call_target="tpu_custom_call" | custom-call | flops 17600000000 | bytes 1024 | tf_op jit(solution)/shard_map/attend/pallas_call | solution.py:203
  118.3 13.7 %attend.4 = (bf16[8,1,256,128]{3,2,1,0:T(8,128)(2,1)S(1)}, f32[1,8,2,256]{3,2,1,0:T(2,128)S(1)}) custom-call(s32[3,4]{1,0:T(4,128)S(1)} %copy-done.28, f32[1,128]{1,0:T(1,128)S(1)} %reshape_reshape.6.scale_ref, bf16[8,3,256,128]{3,2,1,0:T(8,128)(2,1)S(1)} %all-to-all-done.1.refs_0_), custom_call_target="tpu_custom_call" | custom-call | flops 17600000000 | bytes 1024 | tf_op jit(solution)/shard_map/attend/pallas_call | solution.py:203
  140.0 20.2 %attend.5 = (bf16[8,1,256,128]{3,2,1,0:T(8,128)(2,1)}, f32[1,8,2,256]{3,2,1,0:T(2,128)S(1)}) custom-call(s32[3,4]{1,0:T(4,128)S(1)} %copy-done.28, f32[1,128]{1,0:T(1,128)S(1)} %reshape_reshape.6.scale_ref, bf16[8,3,256,128]{3,2,1,0:T(8,128)(2,1)} %all-to-all-done.2.refs_0_), custom_call_target="tpu_custom_call" | custom-call | flops 17600000000 | bytes 1024 | tf_op jit(solution)/shard_map/attend/pallas_call | solution.py:203
  172.0 17.9 %layer.3 = (bf16[256,1024]{1,0:T(8,128)(2,1)S(1)}, bf16[256,1024]{1,0:T(8,128)(2,1)S(1)}, f32[256,1024]{1,0:T(8,128)}, bf16[256,4096]{1,0:T(8,128)(2,1)}, bf16[2...) custom-call(bf16[8,1,256,128]{3,2,1,0:T(8,128)(2,1)S(1)} %get-tuple-, ...), custom_call_target="tpu_custom_call" | custom-call | flops 17600000000 | bytes 1024 | tf_op jit(solution)/shard_map/layer/pallas_call | solution.py:463
  192.4 16.5 %layer.4 = (bf16[256,1024]{1,0:T(8,128)(2,1)S(1)}, bf16[256,1024]{1,0:T(8,128)(2,1)S(1)}, f32[256,1024]{1,0:T(8,128)}, bf16[256,4096]{1,0:T(8,128)(2,1)}, bf16[2...) custom-call(bf16[8,1,256,128]{3,2,1,0:T(8,128)(2,1)S(1)} %get-tuple-, ...), custom_call_target="tpu_custom_call" | custom-call | flops 17600000000 | bytes 1024 | tf_op jit(solution)/shard_map/layer/pallas_call | solution.py:463
  218.6 16.5 %layer.5 = (bf16[256,1024]{1,0:T(8,128)(2,1)S(1)}, bf16[256,1024]{1,0:T(8,128)(2,1)S(1)}, f32[256,1024]{1,0:T(8,128)}, bf16[256,4096]{1,0:T(8,128)(2,1)}, bf16[2...) custom-call(bf16[8,1,256,128]{3,2,1,0:T(8,128)(2,1)S(1)} %all-to-all, ...), custom_call_target="tpu_custom_call" | custom-call | flops 17600000000 | bytes 1024 | tf_op jit(solution)/shard_map/layer/pallas_call | solution.py:463
  238.7 29.4 %attend_back.3 = (bf16[8,1,3,256,128]{4,3,2,1,0:T(8,128)(2,1)}, f32[1,8,256]{2,1,0:T(8,128)S(1)}) custom-call(s32[3,4]{1,0:T(4,128)S(1)} %copy-done.28, f32[1,128]{1,0:T(1,128)S(1)} %broadcast_divide_fusion.inv_ref, bf16[8,1,256,128]{3,2,1,0:T(8,128)(2,1)S(1)} %all-to-all-done.5.grad_ref, bf16[8,3,256,128]{3,2,1,0:T(8,128)(2,1)} %copy-done.4, ...), custom_call_target="tpu_custom_call" | custom-call | flops 28600000512 | bytes 1024 | tf_op jit(solution)/shard_map/attend_back/pallas_call | solution.py:317
  296.4 14.8 %all-to-all-done.6 = bf16[8,2,256,128]{3,2,1,0:T(8,128)(2,1)} async-done(((bf16[8,2,256,128]{3,2,1,0:T(8,128)(2,1)}), bf16[8,2,256,128]{3,2,1,0:T(8,128)(2,1)}, u32[]{:S(2)}, u32[]{:S(2)}) %all-to-all-start.6) | async-done | bytes 1048608 | tf_op jit(solution)/shard_map/all_to_all | solution.py:43
  323.9 8.5 %weight_part.15 = bf16[8,128,1280]{2,1,0:T(8,128)(2,1)} custom-call(s32[1]{0:T(128)} %bitcast.16.part_ref, bf16[256,1024]{1,0:T(8,128)(2,1)S(1)} %copy-done.38, bf16[256,1024]{1,0:T(8,128)(2,1)S(1)} %copy-done.50, bf16[256,1024]{1,0:T(8,128)(2,1)S(1)} %copy-done.59, bf16[256,4096]{1,0:T(8,128)(2,1)} %get-tuple-element.134.refs_3_, ...), custom_call_target="tpu_custom_call" | custom-call | flops 8249999872 | bytes 1024 | tf_op jit(solution)/shard_map/weight_part/pallas_call | solution.py:583
  332.4 23.0 %attend_back.4 = (bf16[8,1,3,256,128]{4,3,2,1,0:T(8,128)(2,1)}, f32[1,8,256]{2,1,0:T(8,128)S(1)}) custom-call(s32[3,4]{1,0:T(4,128)S(1)} %copy-done.28, f32[1,128]{1,0:T(1,128)S(1)} %broadcast_divide_fusion.inv_ref, bf16[8,1,256,128]{3,2,1,0:T(8,128)(2,1)S(1)} %get-tuple-element.176.grad_ref, bf16[8,3,256,128]{3,2,1,0:T(8,128)(2,1)} %copy-done, ...), custom_call_target="tpu_custom_call" | custom-call | flops 28600000512 | bytes 1024 | tf_op jit(solution)/shard_map/attend_back/pallas_call | solution.py:317
  355.4 33.1 %attend_back.5 = (bf16[8,1,3,256,128]{4,3,2,1,0:T(8,128)(2,1)S(1)}, f32[1,8,256]{2,1,0:T(8,128)S(1)}) custom-call(s32[3,4]{1,0:T(4,128)S(1)} %copy-done.28, f32[1,128]{1,0:T(1,128)S(1)} %broadcast_divide_fusion.inv_ref, bf16[8,1,256,128]{3,2,1,0:T(8,128)(2,1)S(1)} %get-tuple-element.180.grad_ref, bf16[8,3,256,128]{3,2,1,0:T(8,128)(2,1)} %all-to-all-done.2.refs_0_, ...), custom_call_target="tpu_custom_call" | custom-call | flops 28600000512 | bytes 1024 | tf_op jit(solution)/shard_map/attend_back/pallas_call | solution.py:317
  422.6 41.2 %collective-permute-done.5.refs_13_ = bf16[8,128,1280]{2,1,0:T(8,128)(2,1)} collective-permute-done((bf16[8,128,1280]{2,1,0:T(8,128)(2,1)}, bf16[8,128,1280]{2,1,0:T(8,128)(2,1)}, u32[]{:S(2)}, u32[]{:S(2)}) %collective-permute-start.5) | collective-permute-done | bytes 2621472 | tf_op jit(solution)/shard_map/ppermute | solution.py:511
  463.9 9.0 %weight_part.19 = bf16[8,128,1280]{2,1,0:T(8,128)(2,1)} custom-call(s32[1]{0:T(128)} %bitcast.24.part_ref, bf16[256,1024]{1,0:T(8,128)(2,1)S(1)} %copy-done.39, bf16[256,1024]{1,0:T(8,128)(2,1)S(1)} %copy-done.51, bf16[256,1024]{1,0:T(8,128)(2,1)S(1)} %copy-done.60, bf16[256,4096]{1,0:T(8,128)(2,1)} %get-tuple-element.134.refs_3_, ...), custom_call_target="tpu_custom_call" | custom-call | flops 8249999872 | bytes 1024 | tf_op jit(solution)/shard_map/weight_part/pallas_call | solution.py:583
  486.4 33.5 %collective-permute-done.20 = bf16[4,128,1280]{2,1,0:T(8,128)(2,1)} collective-permute-done((bf16[4,128,1280]{2,1,0:T(8,128)(2,1)}, bf16[4,128,1280]{2,1,0:T(8,128)(2,1)}, u32[]{:S(2)}, u32[]{:S(2)}) %collective-permute-start.20) | collective-permute-done | bytes 1310752 | tf_op jit(solution)/shard_map/ppermute | solution.py:511
  538.9 13.8 %collective-permute-done.21 = bf16[2,128,2304]{2,1,0:T(8,128)(2,1)S(1)} collective-permute-done((bf16[2,128,2304]{2,1,0:T(8,128)(2,1)S(1)}, bf16[2,128,2304]{2,1,0:T(8,128)(2,1)S(1)}, u32[]{:S(2)}, u32[]{:S(2)}) %collective-permute-start.21) | collective-permute-done | bytes 1179680 | tf_op jit(solution)/shard_map/ppermute | solution.py:511
  564.2 12.9 %input_grad.1 = (f32[3,256,1024]{2,1,0:T(8,128)}, f32[1,1024]{1,0:T(1,128)S(1)}) custom-call(bf16[3,256,1024]{2,1,0:T(8,128)(2,1)} %x_ref, f32[1,1024]{1,0:T(1,128)S(1)} %bitcast.124, bf16[1024,1024]{1,0:T(8,128)(2,1)} %wq_ref.7, bf16[1024,1024]{1,0:T(8,128)(2,1)} %wk_ref.7, bf16[1024,1024]{1,0:T(8,128)(2,1)} %wv_ref.7, bf16[256,3072]{1,0:T(8,128)(2,1)} %copy-done.29, ...), custom_call_target="tpu_custom_call" | custom-call | flops 14300000256 | bytes 1024 | tf_op jit(solution)/shard_map/input_grad/pallas_call | solution.py:679
  582.9 11.6 %collective-permute-done.8 = f32[7184]{0:T(1024)S(1)} collective-permute-done((f32[7184]{0:T(1024)S(1)}, f32[7184]{0:T(1024)S(1)}, u32[]{:S(2)}, u32[]{:S(2)}) %collective-permute-start.8) | collective-permute-done | bytes 28768 | tf_op jit(solution)/shard_map/ppermute | solution.py:511
  607.9 13.0 %layer_out.1 = bf16[3,256,1024]{2,1,0:T(8,128)(2,1)} custom-call(f32[256,1024]{1,0:T(8,128)S(1)} %copy-done.71, f32[256,1024]{1,0:T(8,128)S(1)} %copy-done.72, f32[256,1024]{1,0:T(8,128)S(1)} %copy-done.73, bf16[256,4096]{1,0:T(8,128)(2,1)} %get-tuple-element.133.refs_0_.refs_3_, bf16[256,4096]{1,0:T(8,128)(2,1)} %get-tuple-element.146.refs_1_.refs_4_, ...), custom_call_target="tpu_custom_call" | custom-call | flops 14300000256 | bytes 1024 | tf_op jit(solution)/shard_map/layer_out/pallas_call | solution.py:500
  624.2 12.3 %collective-permute-done.13.refs_7_ = bf16[8,128,768]{2,1,0:T(8,128)(2,1)} collective-permute-done((bf16[8,128,768]{2,1,0:T(8,128)(2,1)S(1)}, bf16[8,128,768]{2,1,0:T(8,128)(2,1)}, u32[]{:S(2)}, u32[]{:S(2)}) %collective-permute-start.13) | collective-permute-done | bytes 1572896 | tf_op jit(solution)/shard_map/ppermute | solution.py:511
  645.9 16.8 %collective-permute-done.14 = bf16[4,128,768]{2,1,0:T(8,128)(2,1)S(1)} collective-permute-done((bf16[4,128,768]{2,1,0:T(8,128)(2,1)S(1)}, bf16[4,128,768]{2,1,0:T(8,128)(2,1)S(1)}, u32[]{:S(2)}, u32[]{:S(2)}) %collective-permute-start.14) | collective-permute-done | bytes 786464 | tf_op jit(solution)/shard_map/ppermute | solution.py:511
  664.3 8.6 %collective-permute-done.15 = bf16[2,128,768]{2,1,0:T(8,128)(2,1)S(1)} collective-permute-done((bf16[2,128,768]{2,1,0:T(8,128)(2,1)S(1)}, bf16[2,128,768]{2,1,0:T(8,128)(2,1)S(1)}, u32[]{:S(2)}, u32[]{:S(2)}) %collective-permute-start.15) | collective-permute-done | bytes 393248 | tf_op jit(solution)/shard_map/ppermute | solution.py:511
  (326 shorter events, 250.9 us)
Async XLA Ops:
  10.2 44.3 %all-to-all-start = ((bf16[8,3,256,128]{3,2,1,0:T(8,128)(2,1)}), bf16[8,3,256,128]{3,2,1,0:T(8,128)(2,1)S(1)}, u32[]{:S(2)}, u32[]{:S(2)}) async-start(bf16[8,3,256,128]{3,2,1,0:T(8,128)(2,1)} %get-tuple-element.108), calls=%async_computation | async-start | bytes 3145728 | tf_op jit(solution)/shard_map/all_to_all | solution.py:43
  54.5 41.0 %all-to-all-start.1 = ((bf16[8,3,256,128]{3,2,1,0:T(8,128)(2,1)}), bf16[8,3,256,128]{3,2,1,0:T(8,128)(2,1)S(1)}, u32[]{:S(2)}, u32[]{:S(2)}) async-start(bf16[8,3,256,128]{3,2,1,0:T(8,128)(2,1)} %copy-done.5), calls=%async_computation.1 | async-start | bytes 3145728 | tf_op jit(solution)/shard_map/all_to_all | solution.py:43
  95.4 40.9 %all-to-all-start.2 = ((bf16[8,3,256,128]{3,2,1,0:T(8,128)(2,1)}), bf16[8,3,256,128]{3,2,1,0:T(8,128)(2,1)}, u32[]{:S(2)}, u32[]{:S(2)}) async-start(bf16[8,3,256,128]{3,2,1,0:T(8,128)(2,1)} %copy-done.6), calls=%async_computation.2 | async-start | bytes 3145728 | tf_op jit(solution)/shard_map/all_to_all | solution.py:43
  136.4 29.6 %all-to-all-start.3 = ((bf16[8,2,256,128]{3,2,1,0:T(8,128)(2,1)}), bf16[8,2,256,128]{3,2,1,0:T(8,128)(2,1)S(1)}, u32[]{:S(2)}, u32[]{:S(2)}) async-start(bf16[8,2,256,128]{3,2,1,0:T(8,128)(2,1)} %pad_maximum_fusion.4), calls=%async_computation.3 | async-start | bytes 2097152 | tf_op jit(solution)/shard_map/all_to_all | solution.py:43
  166.9 45.2 %all-to-all-start.4 = ((bf16[8,1,256,128]{3,2,1,0:T(8,128)(2,1)}), bf16[8,1,256,128]{3,2,1,0:T(8,128)(2,1)S(1)}, u32[]{:S(2)}, u32[]{:S(2)}) async-start(bf16[8,1,256,128]{3,2,1,0:T(8,128)(2,1)} %get-tuple-element.143), calls=%async_computation.4 | async-start | bytes 1048576 | tf_op jit(solution)/shard_map/all_to_all | solution.py:43
  212.1 26.4 %all-to-all-start.5 = ((bf16[8,1,256,128]{3,2,1,0:T(8,128)(2,1)}), bf16[8,1,256,128]{3,2,1,0:T(8,128)(2,1)S(1)}, u32[]{:S(2)}, u32[]{:S(2)}) async-start(bf16[8,1,256,128]{3,2,1,0:T(8,128)(2,1)} %get-tuple-element.158), calls=%async_computation.5 | async-start | bytes 1048576 | tf_op jit(solution)/shard_map/all_to_all | solution.py:43
  275.2 40.9 %collective-permute-start = (bf16[8,128,1024]{2,1,0:T(8,128)(2,1)}, bf16[8,128,1024]{2,1,0:T(8,128)(2,1)}, u32[]{:S(2)}, u32[]{:S(2)}) collective-permute-start(bf16[8,128,1024]{2,1,0:T(8,128)(2,1)} %weight_part.12), channel_id=1, source_target_pairs={{0,8},{8,0},{16,24},{24,16},{1,9},{9,1},{17,25},{25,17},{2,10},{10... | collective-permute-start | bytes 6291464 | tf_op jit(solution)/shard_map/ppermute | solution.py:511
  279.2 31.9 %all-to-all-start.6 = ((bf16[8,2,256,128]{3,2,1,0:T(8,128)(2,1)}), bf16[8,2,256,128]{3,2,1,0:T(8,128)(2,1)}, u32[]{:S(2)}, u32[]{:S(2)}) async-start(bf16[8,2,256,128]{3,2,1,0:T(8,128)(2,1)} %pad_maximum_fusion.5), calls=%async_computation.6 | async-start | bytes 2097152 | tf_op jit(solution)/shard_map/all_to_all | solution.py:43
  296.4 27.5 %collective-permute-start.1 = (bf16[8,128,1280]{2,1,0:T(8,128)(2,1)}, bf16[8,128,1280]{2,1,0:T(8,128)(2,1)}, u32[]{:S(2)}, u32[]{:S(2)}) collective-permute-start(bf16[8,128,1280]{2,1,0:T(8,128)(2,1)} %weight_part.13), channel_id=1, source_target_pairs={{0,8},{8,0},{16,24},{24,16},{1,9},{9,1},{17,25},{25,17},{2,10},{10... | collective-permute-start | bytes 7864328 | tf_op jit(solution)/shard_map/ppermute | solution.py:511
  311.1 95.3 %all-to-all-start.7 = ((bf16[8,1,3,256,128]{4,3,2,1,0:T(8,128)(2,1)}), bf16[8,1,3,256,128]{4,3,2,1,0:T(8,128)(2,1)S(1)}, u32[]{:S(2)}, u32[]{:S(2)}) async-start(bf16[8,1,3,256,128]{4,3,2,1,0:T(8,128)(2,1)} %get-tuple-element.183), calls=%async_computation.7 | async-start | bytes 3145728 | tf_op jit(solution)/shard_map/all_to_all | solution.py:43
  323.8 88.6 %collective-permute-start.3 = (bf16[8,128,1024]{2,1,0:T(8,128)(2,1)}, bf16[8,128,1024]{2,1,0:T(8,128)(2,1)}, u32[]{:S(2)}, u32[]{:S(2)}) collective-permute-start(bf16[8,128,1024]{2,1,0:T(8,128)(2,1)} %weight_part.14), channel_id=1, source_target_pairs={{0,16},{8,24},{16,0},{24,8},{1,17},{9,25},{17,1},{25,9},{2,18},{10... | collective-permute-start | bytes 6291464 | tf_op jit(solution)/shard_map/ppermute | solution.py:511
  404.4 59.4 %collective-permute-start.5 = (bf16[8,128,1280]{2,1,0:T(8,128)(2,1)}, bf16[8,128,1280]{2,1,0:T(8,128)(2,1)}, u32[]{:S(2)}, u32[]{:S(2)}) collective-permute-start(bf16[8,128,1280]{2,1,0:T(8,128)(2,1)} %weight_part.15), channel_id=1, source_target_pairs={{0,16},{8,24},{16,0},{24,8},{1,17},{9,25},{17,1},{25,9},{2,18},{10... | collective-permute-start | bytes 7864328 | tf_op jit(solution)/shard_map/ppermute | solution.py:511
  406.4 70.9 %all-to-all-start.8 = ((bf16[8,1,3,256,128]{4,3,2,1,0:T(8,128)(2,1)}), bf16[8,1,3,256,128]{4,3,2,1,0:T(8,128)(2,1)}, u32[]{:S(2)}, u32[]{:S(2)}) async-start(bf16[8,1,3,256,128]{4,3,2,1,0:T(8,128)(2,1)} %get-tuple-element.184), calls=%async_computation.8 | async-start | bytes 3145728 | tf_op jit(solution)/shard_map/all_to_all | solution.py:43
  420.6 63.6 %collective-permute-start.19 = (bf16[4,128,1024]{2,1,0:T(8,128)(2,1)S(1)}, bf16[4,128,1024]{2,1,0:T(8,128)(2,1)}, u32[]{:S(2)}, u32[]{:S(2)}) collective-permute-start(bf16[4,128,1024]{2,1,0:T(8,128)(2,1)S(1)} %dynamic-slice_bitcast_fusion.2), channel_id=1, source_target_pairs={{0,1},{1,0},{2,3},{3,2},{4,5},{5,4},{6,7},{7,6},{8,9},{9,8},{10,11... | collective-permute-start | bytes 3145736 | tf_op jit(solution)/shard_map/ppermute | solution.py:511
  475.3 44.6 %collective-permute-start.20 = (bf16[4,128,1280]{2,1,0:T(8,128)(2,1)}, bf16[4,128,1280]{2,1,0:T(8,128)(2,1)}, u32[]{:S(2)}, u32[]{:S(2)}) collective-permute-start(bf16[4,128,1280]{2,1,0:T(8,128)(2,1)} %dynamic-slice_bitcast_fusion), channel_id=1, source_target_pairs={{0,1},{1,0},{2,3},{3,2},{4,5},{5,4},{6,7},{7,6},{8,9},{9,8},{10,11... | collective-permute-start | bytes 3932168 | tf_op jit(solution)/shard_map/ppermute | solution.py:511
  477.3 48.1 %all-to-all-start.9 = ((bf16[8,1,3,256,128]{4,3,2,1,0:T(8,128)(2,1)}), bf16[8,1,3,256,128]{4,3,2,1,0:T(8,128)(2,1)}, u32[]{:S(2)}, u32[]{:S(2)}) async-start(bf16[8,1,3,256,128]{4,3,2,1,0:T(8,128)(2,1)} %copy-done.3), calls=%async_computation.9 | async-start | bytes 3145728 | tf_op jit(solution)/shard_map/all_to_all | solution.py:43
  527.2 25.6 %collective-permute-start.21 = (bf16[2,128,2304]{2,1,0:T(8,128)(2,1)S(1)}, bf16[2,128,2304]{2,1,0:T(8,128)(2,1)S(1)}, u32[]{:S(2)}, u32[]{:S(2)}) collective-permute-start(bf16[2,128,2304]{2,1,0:T(8,128)(2,1)S(1)} %dynamic-slice_bitcast_fusion.1), channel_id=1, source_target_pairs={{0,2},{1,3},{2,0},{3,1},{4,6},{5,7},{6,4},{7,5},{8,10},{9,11},{10,... | collective-permute-start | bytes 3538952 | tf_op jit(solution)/shard_map/ppermute | solution.py:511
  534.0 22.2 %collective-permute-start.6 = (bf16[8,128,768]{2,1,0:T(8,128)(2,1)S(1)}, bf16[8,128,768]{2,1,0:T(8,128)(2,1)S(1)}, u32[]{:S(2)}, u32[]{:S(2)}) collective-permute-start(bf16[8,128,768]{2,1,0:T(8,128)(2,1)S(1)} %weight_part.20), channel_id=1, source_target_pairs={{0,8},{8,0},{16,24},{24,16},{1,9},{9,1},{17,25},{25,17},{2,10},{10... | collective-permute-start | bytes 4718600 | tf_op jit(solution)/shard_map/ppermute | solution.py:511
  553.1 25.5 %collective-permute-start.22 = (bf16[1,128,2304]{2,1,0:T(8,128)(2,1)S(1)}, bf16[1,128,2304]{2,1,0:T(8,128)(2,1)S(1)}, u32[]{:S(2)}, u32[]{:S(2)}) collective-permute-start(bf16[1,128,2304]{2,1,0:T(8,128)(2,1)S(1)} %constant_dynamic-slice_fusion), channel_id=1, source_target_pairs={{0,4},{1,5},{2,6},{3,7},{4,0},{5,1},{6,2},{7,3},{8,12},{9,13},{10,... | collective-permute-start | bytes 1769480 | tf_op jit(solution)/shard_map/ppermute | solution.py:511
  579.6 25.4 %collective-permute-start.23 = (bf16[128,2304]{1,0:T(8,128)(2,1)}, bf16[128,2304]{1,0:T(8,128)(2,1)}, u32[]{:S(2)}, u32[]{:S(2)}) collective-permute-start(bf16[128,2304]{1,0:T(8,128)(2,1)} %fusion.5), channel_id=1, source_target_pairs={{0,16},{8,24},{16,0},{24,8},{1,17},{9,25},{17,1},{25,9},{2,18},{10... | collective-permute-start | bytes 1769480 | tf_op jit(solution)/shard_map/ppermute | solution.py:511
  599.5 24.4 %collective-permute-start.12 = (bf16[8,128,768]{2,1,0:T(8,128)(2,1)S(1)}, bf16[8,128,768]{2,1,0:T(8,128)(2,1)S(1)}, u32[]{:S(2)}, u32[]{:S(2)}) collective-permute-start(bf16[8,128,768]{2,1,0:T(8,128)(2,1)S(1)} %weight_part.21), channel_id=1, source_target_pairs={{0,8},{8,0},{16,24},{24,16},{1,9},{9,1},{17,25},{25,17},{2,10},{10... | collective-permute-start | bytes 4718600 | tf_op jit(solution)/shard_map/ppermute | solution.py:511
  599.5 36.9 %collective-permute-start.13 = (bf16[8,128,768]{2,1,0:T(8,128)(2,1)S(1)}, bf16[8,128,768]{2,1,0:T(8,128)(2,1)}, u32[]{:S(2)}, u32[]{:S(2)}) collective-permute-start(bf16[8,128,768]{2,1,0:T(8,128)(2,1)S(1)} %weight_part.22), channel_id=1, source_target_pairs={{0,16},{8,24},{16,0},{24,8},{1,17},{9,25},{17,1},{25,9},{2,18},{10... | collective-permute-start | bytes 4718600 | tf_op jit(solution)/shard_map/ppermute | solution.py:511
  606.5 38.5 %collective-permute-start.24 = (bf16[2,128,2304]{2,1,0:T(8,128)(2,1)S(1)}, bf16[2,128,2304]{2,1,0:T(8,128)(2,1)S(1)}, u32[]{:S(2)}, u32[]{:S(2)}) collective-permute-start(bf16[2,128,2304]{2,1,0:T(8,128)(2,1)S(1)} %pad_maximum_fusion.3), channel_id=1, source_target_pairs={{0,8},{8,0},{16,24},{24,16},{1,9},{9,1},{17,25},{25,17},{2,10},{10... | collective-permute-start | bytes 3538952 | tf_op jit(solution)/shard_map/ppermute | solution.py:511
  643.5 19.2 %collective-permute-start.14 = (bf16[4,128,768]{2,1,0:T(8,128)(2,1)S(1)}, bf16[4,128,768]{2,1,0:T(8,128)(2,1)S(1)}, u32[]{:S(2)}, u32[]{:S(2)}) collective-permute-start(bf16[4,128,768]{2,1,0:T(8,128)(2,1)S(1)} %dynamic-slice_bitcast_fusion.3), channel_id=1, source_target_pairs={{0,1},{1,0},{2,3},{3,2},{4,5},{5,4},{6,7},{7,6},{8,9},{9,8},{10,11... | collective-permute-start | bytes 2359304 | tf_op jit(solution)/shard_map/ppermute | solution.py:511
  (97 other events, 1044.1 us)

commit v3 on v2

--- a/solution.py
+++ b/solution.py
@@ -10,7 +10,6 @@
 EPSILON = 1e-05
 MASKED = -1e30
 VMEM_BYTES = 50 * 1024 * 1024
-COST_UNIT = 1.1e9
 F32 = jnp.float32
 BF16 = jnp.bfloat16
 LAST = (((1,), (1,)), ((), ()))
@@ -35,8 +34,8 @@
     return pltpu.CompilerParams(vmem_limit_bytes=VMEM_BYTES)
 
 
-def cost(micros):
-    return pl.CostEstimate(flops=int(micros * COST_UNIT), bytes_accessed=1024, transcendentals=0)
+def cost(flops, size):
+    return pl.CostEstimate(flops=int(flops), bytes_accessed=int(size), transcendentals=0)
 
 
 def exchange(parts):
@@ -59,29 +58,49 @@
     )
 
 
-def project_kernel(x_ref, gain_ref, wq_ref, wk_ref, wv_ref, normed_ref, out_ref):
+def project_kernel(
+    order_ref, x_ref, gain_ref, wq_hbm, wk_hbm, wv_hbm, normed_ref, out_ref, weight_ref, sems
+):
     group, _, _, width = out_ref.shape
+    copies = [
+        pltpu.make_async_copy(weight, weight_ref.at[n], sems.at[n])
+        for n, weight in enumerate((wq_hbm, wk_hbm, wv_hbm))
+    ]
+    for copy in copies:
+        copy.start()
     hat, _ = norm_parts(x_ref[...].astype(F32))
     normed = (hat * gain_ref[...]).astype(BF16)
     normed_ref[...] = normed
-    for n, weight in enumerate((wq_ref, wk_ref, wv_ref)):
-        product = dot(normed, weight[...]).astype(BF16)
+    for n in range(3):
+        copies[n].wait()
+        product = dot(normed, weight_ref[n]).astype(BF16)
         for s in range(group):
             out_ref[s, n] = product[:, s * width : (s + 1) * width]
 
 
-def project(x_row, gain, w_query, w_key, w_value, group):
-    span, model = x_row.shape
+def project(order, slot, x, gain, w_query, w_key, w_value, group):
+    _, span, model = x.shape
     return pl.pallas_call(
         project_kernel,
+        grid_spec=pltpu.PrefetchScalarGridSpec(
+            num_scalar_prefetch=1,
+            grid=(1,),
+            in_specs=[pl.BlockSpec((None, span, model), lambda i, o: (o[slot], 0, 0)), VMEM]
+            + [pl.BlockSpec(memory_space=pl.ANY)] * 3,
+            out_specs=[VMEM] * 2,
+            scratch_shapes=[
+                pltpu.VMEM((3, model, model), BF16),
+                pltpu.SemaphoreType.DMA((3,)),
+            ],
+        ),
         out_shape=[
             jax.ShapeDtypeStruct((span, model), BF16),
             jax.ShapeDtypeStruct((group, 3, span, model // group), BF16),
         ],
         compiler_params=kernel_params(),
-        cost_estimate=cost(5),
+        cost_estimate=cost(0, 1024),
         name="project",
-    )(x_row, gain, w_query, w_key, w_value)
+    )(order, x, gain, w_query, w_key, w_value)
 
 
 def doc_start(offs_ref, row, pos):
@@ -105,12 +124,12 @@
     return (lane >= head * head_dim) & (lane < (head + 1) * head_dim)
 
 
-def attend_kernel(rows, heads, head_dim, offs_ref, scale_ref, *refs):
+def attend_kernel(rows, heads, head_dim, order_ref, offs_ref, scale_ref, *refs):
     count = len(rows)
     result_ref, lse_ref, score_ref = refs[count:]
     for n, row in enumerate(rows):
         attend_row(
-            row,
+            order_ref[row],
             heads,
             head_dim,
             offs_ref,
@@ -196,31 +215,31 @@
     lax.fori_loop(0, blocks, query_block, 0)
 
 
-def attend(offsets, rows, qkv, scale_lanes, heads, head_dim):
+def attend(order, offsets, rows, qkv, scale_lanes, heads, head_dim):
     group, _, span, width = qkv[0].shape
     length = group * span
     wide = max(span, min(512, length))
     return pl.pallas_call(
         functools.partial(attend_kernel, rows, heads, head_dim),
-        in_specs=[SMEM, VMEM] + [VMEM] * len(rows),
+        in_specs=[SMEM, SMEM, VMEM] + [VMEM] * len(rows),
         out_shape=[
             jax.ShapeDtypeStruct((group, len(rows), span, width), BF16),
             jax.ShapeDtypeStruct((len(rows), group, heads, span), F32),
         ],
         scratch_shapes=[pltpu.VMEM((heads, length // wide, span, wide), F32)],
         compiler_params=kernel_params(),
-        cost_estimate=cost(16),
+        cost_estimate=cost(0, 1024),
         name="attend",
-    )(offsets, scale_lanes, *qkv)
-
-
-def attend_back_kernel(rows, heads, head_dim, offs_ref, inv_ref, grad_ref, *refs):
+    )(order, offsets, scale_lanes, *qkv)
+
+
+def attend_back_kernel(rows, heads, head_dim, order_ref, offs_ref, inv_ref, grad_ref, *refs):
     count = len(rows)
     held, out_refs, lse_refs = refs[:count], refs[count : 2 * count], refs[2 * count : 3 * count]
     dqkv_ref, total_ref = refs[3 * count : 3 * count + 2]
     for n, row in enumerate(rows):
         attend_back_row(
-            row,
+            order_ref[row],
             heads,
             head_dim,
             offs_ref,
@@ -311,12 +330,18 @@
     lax.fori_loop(0, blocks, key_block, 0)
 
 
-def attend_back(offsets, rows, qkv, grads, scaled, inverse_lanes, lse, heads, head_dim):
+def attend_back(
+    order, offsets, rows, qkv, grads, at, scaled, inverse_lanes, lse, heads, head_dim
+):
     group, _, span, width = qkv[0].shape
     count = len(rows)
     return pl.pallas_call(
         functools.partial(attend_back_kernel, rows, heads, head_dim),
-        in_specs=[SMEM] + [VMEM] * (2 + 3 * count),
+        grid=(1,),
+        in_specs=[SMEM, SMEM, VMEM]
+        + [pl.BlockSpec((group, count, span, width), lambda i: (0, at, 0, 0))]
+        + [VMEM] * (3 * count),
+        out_specs=[VMEM] * 2,
         out_shape=[
             jax.ShapeDtypeStruct((group, count, 3, span, width), BF16),
             jax.ShapeDtypeStruct((count, 8, span), F32),
@@ -324,9 +349,9 @@
         scratch_shapes=[pltpu.VMEM((heads, group, span, width), BF16)] * 3
         + [pltpu.VMEM((group, 8, span), F32), pltpu.VMEM((group, span, width), F32)],
         compiler_params=kernel_params(),
-        cost_estimate=cost(26),
+        cost_estimate=cost(0, 1024),
         name="attend_back",
-    )(offsets, inverse_lanes, grads, *qkv, *scaled, *lse)
+    )(order, offsets, inverse_lanes, grads, *qkv, *scaled, *lse)
 
 
 def join_grads_kernel(parts, in_ref, out_ref):
@@ -345,7 +370,7 @@
         functools.partial(join_grads_kernel, PARTS),
         out_shape=jax.ShapeDtypeStruct((span, 3 * group * width), BF16),
         compiler_params=kernel_params(),
-        cost_estimate=cost(1.5),
+        cost_estimate=cost(0, 1024),
         name="join_grads",
     )(block)
 
@@ -354,6 +379,7 @@
 
 
 def layer_kernel(
+    order_ref,
     o_ref,
     x_ref,
     d_out_ref,
@@ -381,7 +407,7 @@
     slope_ref,
     sems,
     *,
-    row,
+    slot,
 ):
     group, _, span, width = o_ref.shape
     hidden = act_ref.shape[1]
@@ -391,7 +417,9 @@
         for c, at in enumerate(steps)
     ]
     mid_copy = pltpu.make_async_copy(
-        d_mid_hbm.at[row * span : (row + 1) * span, :], d_mid_ref, sems.at[len(steps)]
+        d_mid_hbm.at[pl.ds(pl.multiple_of(order_ref[slot] * span, span), span), :],
+        d_mid_ref,
+        sems.at[len(steps)],
     )
     for copy in weight_copies:
         copy.start()
@@ -456,13 +484,29 @@
         d_attn_ref[s, 0] = d_attn[:, s * width : (s + 1) * width]
 
 
-def layer(row, o_blocks, x_row, d_out_row, gains, w_out, d_mid, w_fc1):
-    span, model = x_row.shape
+def layer(order, slot, o_blocks, at, x, d_out, gains, w_out, d_mid, w_fc1):
+    group, _, span, width = o_blocks.shape
+    model = x.shape[2]
     hidden = w_fc1.shape[1]
     shape = jax.ShapeDtypeStruct
     return pl.pallas_call(
-        functools.partial(layer_kernel, row=row),
-        in_specs=[VMEM] * 8 + [pl.BlockSpec(memory_space=pl.ANY)] * 2,
+        functools.partial(layer_kernel, slot=slot),
+        grid_spec=pltpu.PrefetchScalarGridSpec(
+            num_scalar_prefetch=1,
+            grid=(1,),
+            in_specs=[pl.BlockSpec((group, 1, span, width), lambda i, o: (0, at, 0, 0))]
+            + [pl.BlockSpec((None, span, model), lambda i, o: (o[slot], 0, 0))] * 2
+            + [VMEM] * 5
+            + [pl.BlockSpec(memory_space=pl.ANY)] * 2,
+            out_specs=[VMEM] * 11,
+            scratch_shapes=[
+                pltpu.VMEM((span, hidden), F32),
+                pltpu.VMEM(w_fc1.shape, BF16),
+                pltpu.VMEM((span, hidden), F32),
+                pltpu.VMEM((span, hidden), F32),
+                pltpu.SemaphoreType.DMA((hidden // FF_STEP + 1,)),
+            ],
+        ),
         out_shape=[
             shape((span, model), BF16),
             shape((span, model), BF16),
@@ -471,39 +515,33 @@
             shape((span, hidden), BF16),
             shape((span, model), BF16),
             shape((span, model), F32),
-            shape(o_blocks.shape, BF16),
+            shape((group, 1, span, width), BF16),
             shape((1, model), F32),
             shape((1, model), F32),
             shape((1, hidden), F32),
         ],
-        scratch_shapes=[
-            pltpu.VMEM((span, hidden), F32),
-            pltpu.VMEM(w_fc1.shape, BF16),
-            pltpu.VMEM((span, hidden), F32),
-            pltpu.VMEM((span, hidden), F32),
-            pltpu.SemaphoreType.DMA((hidden // FF_STEP + 1,)),
-        ],
         compiler_params=kernel_params(),
-        cost_estimate=cost(16),
+        cost_estimate=cost(0, 1024),
         name="layer",
-    )(o_blocks, x_row, d_out_row, *gains, w_out, d_mid, w_fc1)
-
-
-def layer_out_kernel(*refs):
+    )(order, o_blocks, x, d_out, *gains, w_out, d_mid, w_fc1)
+
+
+def layer_out_kernel(order_ref, *refs):
     count = (len(refs) - 2) // 2
     weight, out_ref = refs[-2], refs[-1]
     for r in range(count):
-        out_ref[r] = (refs[r][...] + dot(refs[count + r][...], weight[...])).astype(BF16)
-
-
-def last_step(residuals, mids, w_fc2):
+        out_ref[order_ref[r]] = (refs[r][...] + dot(refs[count + r][...], weight[...])).astype(BF16)
+
+
+def last_step(order, residuals, mids, w_fc2):
     return pl.pallas_call(
         layer_out_kernel,
+        in_specs=[SMEM] + [VMEM] * (2 * len(mids) + 1),
         out_shape=jax.ShapeDtypeStruct((len(mids),) + residuals[0].shape, BF16),
         compiler_params=kernel_params(),
-        cost_estimate=cost(13),
+        cost_estimate=cost(0, 1024),
         name="layer_out",
-    )(*residuals, *mids, w_fc2)
+    )(order, *residuals, *mids, w_fc2)
 
 
 def flip(value, axis, bit):
@@ -515,32 +553,29 @@
     return (lax.axis_size(axis) - 1).bit_length()
 
 
-def add(left, right):
-    return (left.astype(F32) + right.astype(F32)).astype(BF16)
-
-
-def sum_small(value):
-    for axis in ("batch", "blk"):
-        for bit in range(bits(axis)):
-            value = value + flip(value, axis, bit)
-    return value
-
-
 PARTS = 4
 
 
-def weight_kernel(count, rows, added, part_ref, *refs):
+def weight_kernel(count, rows, added, shards, part_ref, *refs):
     out_ref = refs[-1]
-    extras = refs[2 * count * rows : 2 * count * rows + added]
+    high = out_ref.shape[1]
+    per = rows * (shards + 1)
+    extras = refs[per * count : per * count + added]
     at = 0
     for n in range(count):
-        lefts = refs[2 * n * rows : (2 * n + 1) * rows]
-        rights = refs[(2 * n + 1) * rows : (2 * n + 2) * rows]
+        mine = refs[n * per : (n + 1) * per]
+        rights = mine[rows * shards :]
         width = rights[0].shape[1]
-        total = sum(dot_first(left[...], right[...]) for left, right in zip(lefts, rights))
-        for extra in extras:
-            total = total + extra[0, :, at : at + width].astype(F32)
-        out_ref[0, :, at : at + width] = total.astype(BF16)
+        total = 0.0
+        for r in range(rows):
+            left = [ref[...] for ref in mine[r * shards : (r + 1) * shards]]
+            left = jnp.concatenate(left, axis=1) if shards > 1 else left[0]
+            total += dot_first(left, rights[r][...])
+        for i in range(shards):
+            piece = total[i * high : (i + 1) * high]
+            for extra in extras:
+                piece = piece + extra[i, :, at : at + width].astype(F32)
+            out_ref[i, :, at : at + width] = piece.astype(BF16)
         at += width
 
 
@@ -563,61 +598,78 @@
 
 
 def weight_part(pairs, part, extras, group):
-    specs, width = [], 0
+    shards = 2
+    specs, arrays, width = [], [], 0
     for lefts, rights, kind in pairs:
         span, model = lefts[0].shape
-        if kind == "columns":
-            high, wide = model // group, rights[0].shape[1] // PARTS
-            left_spec = pl.BlockSpec((span, high), lambda s, p: (0, s))
-            right_spec = pl.BlockSpec((span, wide), lambda s, p: (0, p[0]))
-        else:
-            high, wide = model // group // PARTS, rights[0].shape[1]
-            left_spec = pl.BlockSpec((span, high), lambda s, p: (0, s * PARTS + p[0]))
-            right_spec = pl.BlockSpec((span, wide), lambda s, p: (0, 0))
-        specs += [left_spec] * len(lefts) + [right_spec] * len(rights)
+        stride = 1 if kind == "columns" else PARTS
+        high = model // group // stride
+        wide = rights[0].shape[1] // (PARTS if kind == "columns" else 1)
+        for left in lefts:
+            for i in range(shards):
+
+                def left_at(g, p, i=i, stride=stride):
+                    return (0, (g * shards + i) * stride + (p[0] if stride > 1 else 0))
+
+                specs.append(pl.BlockSpec((span, high), left_at))
+                arrays.append(left)
+        for right in rights:
+
+            def right_at(g, p, stride=stride):
+                return (0, p[0] if stride == 1 else 0)
+
+            specs.append(pl.BlockSpec((span, wide), right_at))
+            arrays.append(right)
         width += wide
     if high % 128:
         return weight_part_plain(pairs, part, extras, group)
-    block = pl.BlockSpec((1, high, width), lambda s, p: (s, 0, 0))
-    arrays = [array for lefts, rights, _ in pairs for array in (*lefts, *rights)]
+    block = pl.BlockSpec((shards, high, width), lambda g, p: (g, 0, 0))
     return pl.pallas_call(
-        functools.partial(weight_kernel, len(pairs), len(pairs[0][0]), len(extras)),
+        functools.partial(weight_kernel, len(pairs), len(pairs[0][0]), len(extras), shards),
         grid_spec=pltpu.PrefetchScalarGridSpec(
             num_scalar_prefetch=1,
-            grid=(group,),
+            grid=(group // shards,),
             in_specs=specs + [block] * len(extras),
             out_specs=block,
         ),
         out_shape=jax.ShapeDtypeStruct((group, high, width), BF16),
         compiler_params=kernel_params(),
-        cost_estimate=cost(7.5),
+        cost_estimate=cost(0, 1024),
         name="weight_part",
     )(part.astype(jnp.int32).reshape(1), *arrays, *extras)
 
 
 class WeightSum:
-    def __init__(self, order, *pairs):
-        self.order, self.pairs = order, pairs
+    def __init__(self, *pairs):
+        self.pairs = pairs
         batch_at = lax.axis_index("batch")
         self.near, self.far = batch_at & 1, (batch_at >> 1) & 1
 
-    def piece(self, near, far, *extras):
+    def piece(self, order, near, far, *extras):
         def part_of(part):
             return weight_part(self.pairs, part, extras, lax.axis_size("blk"))
 
-        return self.order(part_of, near * 2 + far)
-
-    def away_far(self):
-        self.first = flip(self.piece(1 - self.near, 1 - self.far), "batch", 0)
-
-    def send_far(self):
-        self.arrived = flip(self.piece(self.near, 1 - self.far, self.first), "batch", 1)
-
-    def away_near(self):
-        self.second = flip(self.piece(1 - self.near, self.far), "batch", 0)
-
-    def keep(self):
-        return self.piece(self.near, self.far, self.second, self.arrived)
+        return order(part_of, near * 2 + far)
+
+    def away_far(self, order):
+        return self.piece(order, 1 - self.near, 1 - self.far)
+
+    def send_far(self, order, away):
+        return self.piece(order, self.near, 1 - self.far, away)
+
+    def away_near(self, order):
+        return self.piece(order, 1 - self.near, self.far)
+
+    def keep(self, order, away, arrived):
+        return self.piece(order, self.near, self.far, away, arrived)
+
+
+def over_near(sent):
+    return flip(sent, "batch", 0)
+
+
+def over_far(sent):
+    return flip(sent, "batch", 1)
 
 
 class Order:
@@ -629,35 +681,141 @@
         return self.last
 
 
+def window(always, step):
+    def nothing():
+        return jax.tree.map(lambda leaf: jnp.zeros(leaf.shape, leaf.dtype), jax.eval_shape(step))
+
+    return lax.cond(always, step, nothing)
+
+
 def tie(values, *after):
     return lax.optimization_barrier((values, after))[0]
 
 
-def halve(mine, bit):
-    at = (lax.axis_index("blk") >> bit) & 1
-    halves = mine.reshape((-1, 2) + mine.shape[1:])
-    keep = lax.dynamic_index_in_dim(halves, at, 1, keepdims=False)
-    send = lax.dynamic_index_in_dim(halves, 1 - at, 1, keepdims=False)
-    return add(keep, flip(send, "blk", bit))
-
-
-def halve_rest(mine, start):
+def combine_kernel(plan, at_ref, *refs):
+    ins = sum(2 if added else 1 for added, _ in plan)
+    into, out_of = list(refs[:ins]), list(refs[ins:])
+    for n, (added, cut) in enumerate(plan):
+        terms = [into.pop(0) for _ in range(2 if added else 1)]
+
+        def total(i):
+            if len(terms) == 1:
+                return terms[0][i]
+            return (terms[0][i].astype(F32) + terms[1][i].astype(F32)).astype(BF16)
+
+        if cut:
+            keep, send = out_of.pop(0), out_of.pop(0)
+            for j in range(keep.shape[0]):
+                keep[j] = total(2 * j + at_ref[n])
+                send[j] = total(2 * j + 1 - at_ref[n])
+        else:
+            whole = out_of.pop(0)
+            for j in range(whole.shape[0]):
+                whole[j] = total(j)
+
+
+class Tree:
+    def __init__(self, mine):
+        self.steps = [("blk", bit) for bit in range(bits("blk"))]
+        self.steps += [("batch", bit) for bit in range(2, bits("batch"))]
+        self.steps += [("far", 1), ("near", 0)]
+        self.kept, self.sends, self.arrived = mine, None, None
+
+    def start(self):
+        kind, bit = self.steps[0]
+        return [flip(send, "blk" if kind == "blk" else "batch", bit) for send in self.sends]
+
+    def end(self, arrived):
+        self.last = self.steps.pop(0)[0]
+        self.arrived = arrived
+
+
+def combine(trees):
+    me = lax.axis_index("blk")
+    plan, ins, shapes, at, cutting = [], [], [], [], []
+    for tree in trees:
+        if tree.sends is not None and tree.last == "far":
+            tree.sends = [tree.kept, tree.arrived[0]]
+            continue
+        added = tree.sends is not None
+        kind, bit = tree.steps[0]
+        cut = kind == "blk"
+        plan.append((added, cut))
+        ins += [tree.kept] + (list(tree.arrived) if added else [])
+        count, *rest = tree.kept.shape
+        shape = jax.ShapeDtypeStruct((count // 2 if cut else count, *rest), BF16)
+        shapes += [shape] * (2 if cut else 1)
+        at.append((me >> bit) & 1 if cut else me * 0)
+        cutting.append(tree)
+    if not plan:
+        return
+    outs = list(
+        pl.pallas_call(
+            functools.partial(combine_kernel, plan),
+            in_specs=[SMEM] + [VMEM] * len(ins),
+            out_shape=shapes,
+            compiler_params=kernel_params(),
+            cost_estimate=cost(0, 1024),
+            name="combine",
+        )(jnp.stack(at).astype(jnp.int32), *ins)
+    )
+    for tree, (_, cut) in zip(cutting, plan):
+        tree.kept = outs.pop(0)
+        tree.sends = [outs.pop(0)] if cut else [tree.kept]
+
+
+def place_kernel(layout, part_ref, *refs):
+    ins, outs = list(refs[: 4 * len(layout)]), list(refs[4 * len(layout) :])
+    near, far = part_ref[0], part_ref[1]
+    order = [near * 2 + far, near * 2 + 1 - far, (1 - near) * 2 + far, (1 - near) * 2 + 1 - far]
+    for spans in layout:
+        pieces = [ins.pop(0) for _ in range(4)]
+        for start, width, kind in spans:
+            out = outs.pop(0)
+            for part, piece in zip(order, pieces):
+                value = piece[0, :, start : start + width].astype(F32)
+                if kind == "columns":
+                    out[:, pl.ds(pl.multiple_of(part * width, 128), width)] = value
+                else:
+                    high = value.shape[0]
+                    out[pl.ds(pl.multiple_of(part * high, 8), high), :] = value
+
+
+def place(trees, layout):
     batch_at = lax.axis_index("batch")
-    near, far = batch_at & 1, (batch_at >> 1) & 1
-    for bit in range(start, bits("blk")):
-        mine = halve(mine, bit)
-    mine = mine[0]
-    for bit in range(2, bits("batch")):
-        mine = add(mine, flip(mine, "batch", bit))
-    other = flip(mine, "batch", 1)
-    pair = jnp.stack([jnp.where(far == 0, mine, other), jnp.where(far == 0, other, mine)])
-    away = flip(pair, "batch", 0)
-    first = jnp.where(near == 0, pair, away).astype(F32)
-    second = jnp.where(near == 0, away, pair).astype(F32)
-    return [first[0], first[1], second[0], second[1]]
-
-
-def input_grad_kernel(parts, rows, x_ref, gain_ref, wq_ref, wk_ref, wv_ref, *refs):
+    parts = jnp.stack([batch_at & 1, (batch_at >> 1) & 1]).astype(jnp.int32)
+    ins, shapes = [], []
+    for tree, spans in zip(trees, layout):
+        ins += [*tree.sends, *tree.arrived]
+        high = tree.kept.shape[1]
+        for _, width, kind in spans:
+            shape = (high, PARTS * width) if kind == "columns" else (PARTS * high, width)
+            shapes.append(jax.ShapeDtypeStruct(shape, F32))
+    return pl.pallas_call(
+        functools.partial(place_kernel, layout),
+        in_specs=[SMEM] + [VMEM] * len(ins),
+        out_shape=shapes,
+        compiler_params=kernel_params(),
+        cost_estimate=cost(0, 1024),
+        name="place",
+    )(parts, *ins)
+
+
+class SmallSum:
+    def __init__(self, mine):
+        self.mine = mine
+        self.steps = [("batch", bit) for bit in range(bits("batch"))]
+        self.steps += [("blk", bit) for bit in range(bits("blk"))]
+
+    def start(self):
+        return flip(self.mine, *self.steps[0])
+
+    def end(self, arrived):
+        self.steps.pop(0)
+        self.mine = self.mine + arrived
+
+
+def input_grad_kernel(parts, rows, order_ref, x_ref, gain_ref, wq_ref, wk_ref, wv_ref, *refs):
     out_ref, sum_ref = refs[2 * rows :]
     model = wq_ref.shape[0]
     piece = model // parts
@@ -669,23 +827,25 @@
             for n, weight in enumerate((wq_ref, wk_ref, wv_ref)):
                 at = (p * 3 + n) * piece
                 grad += dot_last(d_ref[:, at : at + piece], weight[:, p * piece : (p + 1) * piece])
-        hat, spread = norm_parts(x_ref[r].astype(F32))
-        out_ref[r] = res_ref[...] + norm_back(hat, spread, gain_ref[...], grad)
+        row = order_ref[r]
+        hat, spread = norm_parts(x_ref[row].astype(F32))
+        out_ref[row] = res_ref[...] + norm_back(hat, spread, gain_ref[...], grad)
         total += jnp.sum(grad * hat, axis=0, keepdims=True)
     sum_ref[...] = total
 
 
-def input_grad(x, gain, w_query, w_key, w_value, d_rows, d_residuals):
+def input_grad(order, x, gain, w_query, w_key, w_value, d_rows, d_residuals):
     return pl.pallas_call(
         functools.partial(input_grad_kernel, PARTS, len(d_rows)),
+        in_specs=[SMEM] + [VMEM] * (5 + 2 * len(d_rows)),
         out_shape=[
             jax.ShapeDtypeStruct(x.shape, F32),
             jax.ShapeDtypeStruct((1, x.shape[2]), F32),
         ],
         compiler_params=kernel_params(),
-        cost_estimate=cost(13),
+        cost_estimate=cost(0, 1024),
         name="input_grad",
-    )(x, gain, w_query, w_key, w_value, *d_rows, *d_residuals)
+    )(order, x, gain, w_query, w_key, w_value, *d_rows, *d_residuals)
 
 
 def on_device(
@@ -714,52 +874,115 @@
     my_index = lax.axis_index("blk")
     rows = range(row_count)
 
-    order = Order()
+    always = offsets[0, 0] == 0
+    ends = jnp.concatenate(
+        [offsets[:, 1:], jnp.full((row_count, 1), span * group, offsets.dtype)], axis=1
+    )
+    work = jnp.sum((ends - offsets) ** 2, axis=1)
+    index = jnp.arange(row_count, dtype=jnp.int32)
+    before = (work[None, :] > work[:, None]) | (
+        (work[None, :] == work[:, None]) & (index[None, :] < index[:, None])
+    )
+    rank = jnp.sum(before.astype(jnp.int32), axis=1)
+    by_work = jnp.sum(jnp.where(rank[None, :] == index[:, None], index[None, :], 0), axis=1)
     gain = ln_attn.reshape(1, model)
-    normed, qkv = [], []
-    for r in rows:
-
-        def project_row(x_row):
-            return project(x_row, gain, w_query, w_key, w_value, group)
-
-        normed_row, sent = order(project_row, inputs[r])
-        normed.append(normed_row)
-        qkv.append(exchange(tie(sent, qkv[-1:])))
-
-    def middle_grad(grad, _):
-        return jnp.einsum("td,fd->tf", grad, w_fc2, preferred_element_type=F32)
-
-    d_mid = order(middle_grad, cotangent.reshape(tokens, model), qkv[0])
-
+    last = row_count - 1
     my_scale = lax.dynamic_slice(head_scale, (my_index * heads,), (heads,))
     scale_lanes = jnp.repeat(my_scale, head_dim).reshape(1, width)
-    scaled_mine, lse = [], []
-    for r in rows:
-
-        def attend_one(held):
-            return attend(offsets, [r], [held], scale_lanes, heads, head_dim)
-
-        out, log_total = order(attend_one, qkv[r])
-        scaled_mine.append(out)
-        lse.append(log_total)
-    early = exchange(tie(jnp.concatenate(scaled_mine[:-1], axis=1), qkv[-1]))
-    late = exchange(tie(scaled_mine[-1], early))
-
     layer_gains = [
         ln_post.reshape(1, model),
         ln_ffn.reshape(1, model),
         ln_mid.reshape(1, -1),
         jnp.repeat(head_scale, head_dim).reshape(1, model),
     ]
-    layers = []
-    for r in rows:
-
-        def layer_row(o_blocks):
-            return layer(
-                r, o_blocks, inputs[r], cotangent[r], layer_gains, w_out, d_mid, w_fc1
+
+    def project_row(r, x):
+        return project(by_work, r, x, gain, w_query, w_key, w_value, group)
+
+    def attend_one(r, held):
+        return attend(by_work, offsets, [r], [held], scale_lanes, heads, head_dim)
+
+    def layer_row(r, o_blocks):
+        at = r if r < last else 0
+        return layer(by_work, r, o_blocks, at, inputs, cotangent, layer_gains, w_out, d_mid, w_fc1)
+
+    def back(order, r, row_heads, at=0):
+        def back_row(held):
+            return attend_back(
+                by_work,
+                offsets,
+                [r],
+                [held],
+                row_heads,
+                at,
+                [scaled_mine[r].reshape(group, span, width)],
+                1.0 / scale_lanes,
+                [lse[r].reshape(lse[r].shape[1:])],
+                heads,
+                head_dim,
             )
 
-        layers.append(order(layer_row, early[:, r : r + 1] if r < row_count - 1 else late))
+        return order(back_row, qkv[r])
+
+    def first_window():
+        order = Order()
+        return exchange(sent), [
+            order(functools.partial(project_row, r), inputs) for r in rows[1:]
+        ]
+
+    normed_first, sent = project_row(0, inputs)
+    held, projected = window(always, first_window)
+    qkv = [held]
+    normed = [normed_first] + [part[0] for part in projected]
+    scaled_mine, lse = [], []
+    for r in rows[1:]:
+
+        def next_window():
+            order = Order()
+            extra = ()
+            if r == 1:
+                extra = jnp.einsum(
+                    "td,fd->tf",
+                    cotangent.reshape(tokens, model),
+                    w_fc2,
+                    preferred_element_type=F32,
+                )
+            return exchange(projected[r - 1][1]), attend_one(r - 1, qkv[r - 1]), extra
+
+        held, (out, log_total), extra = window(always, next_window)
+        d_mid = extra if r == 1 else d_mid
+        qkv.append(held)
+        scaled_mine.append(out)
+        lse.append(log_total)
+
+    def early_window():
+        return (
+            exchange(jnp.concatenate(scaled_mine, axis=1)),
+            attend_one(last, qkv[last]),
+        )
+
+    early, (out, log_total) = window(always, early_window)
+    scaled_mine.append(out)
+    lse.append(log_total)
+
+    def late_window():
+        return exchange(scaled_mine[last]), layer_row(0, early)
+
+    late, layer_first = window(always, late_window)
+
+    def layer_window():
+        order = Order()
+        first = exchange(layer_first[7])
+        rest = []
+        for r in rows[1:]:
+
+            def one(o_blocks):
+                return layer_row(r, o_blocks)
+
+            rest.append(order(one, early if r < last else late))
+        return first, rest
+
+    first_heads, rest = window(always, layer_window)
     (
         scaled,
         ffn_in,
@@ -772,74 +995,148 @@
         g_post,
         g_ffn,
         g_mid,
-    ) = zip(*layers)
-    first_heads = exchange(tie(d_attn[0], late))
-    rest_heads = exchange(tie(jnp.concatenate(d_attn[1:], axis=1), first_heads))
-    d_out = [cotangent[r] for r in rows]
-
-    totals, sent = [], []
-
-    def back(r, row_heads):
-        def back_row(held, grads):
-            return attend_back(
-                offsets,
-                [r],
-                [held],
-                grads,
-                [scaled_mine[r].reshape(group, span, width)],
-                1.0 / scale_lanes,
-                [lse[r].reshape(lse[r].shape[1:])],
-                heads,
-                head_dim,
-            )
-
-        out, total = order(back_row, qkv[r], row_heads)
+    ) = zip(layer_first, *rest)
+    d_out = [lax.dynamic_index_in_dim(cotangent, by_work[r], keepdims=False) for r in rows]
+    sum_one = WeightSum((mid, d_out, "rows"))
+    sum_two = WeightSum((ffn_in, d_pre, "columns"))
+    sum_three = WeightSum((scaled, d_proj, "columns"))
+    order = Order()
+    away = over_near(sum_one.away_far(order))
+    away_two = sum_two.away_far(order)
+    sent_one = sum_one.send_far(order, away)
+
+    def back_first():
+        order = Order()
+        arrived = over_far(sent_one)
+        heads_in = exchange(jnp.concatenate(d_attn[1:], axis=1))
+        away = over_near(away_two)
+        near = sum_one.away_near(order)
+        out = back(order, 0, first_heads)
+        return arrived, heads_in, out, near, sum_two.send_far(order, away)
+
+    far_one, rest_heads, (sent, total), near_one, sent_two = window(always, back_first)
+    totals = [total]
+
+    def back_second():
+        order = Order()
+        arrived = over_far(sent_two), over_near(near_one)
+        grad = exchange(sent)
+        out = back(order, 1, rest_heads, 0)
+        return grad, out, arrived, sum_two.away_near(order), sum_three.away_far(order)
+
+    grad, (sent, total), arrived, near_two, away_three = window(always, back_second)
+    far_two, near_one = arrived
+    totals.append(total)
+    grads = [grad]
+    order = Order()
+    away_three = over_near(away_three)
+    tree_one = Tree(sum_one.keep(order, near_one, far_one))
+    combine([tree_one])
+    sent_three = sum_three.send_far(order, away_three)
+    for r in rows[2:]:
+
+        def back_next():
+            order = Order()
+            moved, near = (), ()
+            if r == 2:
+                moved = tree_one.start(), over_far(sent_three), over_near(near_two)
+            grad = exchange(sent)
+            out = back(order, r, rest_heads, r - 1)
+            if r == 2:
+                near = sum_three.away_near(order)
+            return grad, moved, near, out
+
+        grad, moved, near, (sent, total) = window(always, back_next)
         totals.append(total)
-        sent.append(out)
-
-    sum_fc2 = WeightSum(order, (mid, d_out, "rows"))
-    sum_rest = WeightSum(order, (ffn_in, d_pre, "columns"), (scaled, d_proj, "columns"))
-    back(0, first_heads)
-    grads = [exchange(tie(sent[0], rest_heads))]
-    sum_fc2.away_far()
-    sum_rest.away_far()
-    sum_fc2.send_far()
-    sum_rest.send_far()
-    for r in rows[1:]:
-        back(r, rest_heads[:, r - 1 : r])
-        grads.append(exchange(tie(sent[r], grads)))
-    sum_fc2.away_near()
-    sum_rest.away_near()
-    mine_fc2 = halve(sum_fc2.keep(), 0)
-    mine_rest = halve(sum_rest.keep(), 0)
-    d_rows = [order(join_grads, part) for part in grads]
-    sum_qkv = WeightSum(order, (normed, d_rows, "columns"))
-    sum_qkv.away_far()
-    sum_qkv.away_near()
-    sum_qkv.send_far()
-
-    def input_step(x):
-        return input_grad(x, gain, w_query, w_key, w_value, d_rows, d_residual)
-
-    grad_inputs, grad_ln_attn = order(input_step, inputs)
-
-    def output_step(weight):
-        return last_step(residual, mid, weight)
-
-    layer_out = order(output_step, w_fc2)
-    mine_qkv = sum_qkv.keep()
-    grads_ffn = halve_rest(tie(jnp.concatenate([mine_fc2, mine_rest], axis=2), d_rows), 1)
-    grads_qkv = halve_rest(mine_qkv, 0)
+        grads.append(grad)
+        if r == 2:
+            moved, far_three, near_two = moved
+            tree_one.end(moved)
+            near_three = near
+    tree_two = Tree(sum_two.keep(Order(), near_two, far_two))
+    combine([tree_one, tree_two])
+
+    def back_last():
+        order = Order()
+        moved = tree_one.start(), tree_two.start(), over_near(near_three)
+        grad = exchange(sent)
+        joined = [order(join_grads, part) for part in grads]
+
+        def output_step(weight):
+            return last_step(by_work, residual, mid, weight)
+
+        return grad, moved, joined, order(output_step, w_fc2)
+
+    grad, moved, d_rows, layer_out = window(always, back_last)
+    tree_one.end(moved[0])
+    tree_two.end(moved[1])
+    near_three = moved[2]
+    order = Order()
+    d_rows = d_rows + [order(join_grads, grad)]
+    sum_qkv = WeightSum((normed, d_rows, "columns"))
+    away_qkv = over_near(sum_qkv.away_far(order))
+    near_qkv = sum_qkv.away_near(order)
+    tree_three = Tree(sum_three.keep(order, near_three, far_three))
+    combine([tree_one, tree_two, tree_three])
+    sent_qkv = sum_qkv.send_far(order, away_qkv)
+
+    def advance(trees, extra=lambda: ()):
+        def step():
+            return [tree.start() for tree in trees], extra()
+
+        moved, out = window(always, step)
+        for tree, arrived in zip(trees, moved):
+            tree.end(arrived)
+        return out
+
+    def beside():
+        order = Order()
+        arrived = over_far(sent_qkv)
+        near = over_near(near_qkv)
+
+        def input_step(x):
+            return input_grad(by_work, x, gain, w_query, w_key, w_value, d_rows, d_residual)
+
+        return arrived, near, order(input_step, inputs)
+
+    far_qkv, near_qkv, (grad_inputs, grad_ln_attn) = advance(
+        [tree_one, tree_two, tree_three], beside
+    )
+    tree_qkv = Tree(sum_qkv.keep(order, near_qkv, far_qkv))
     delta_sum = sum(jnp.sum(total, axis=(0, 2)) for total in totals)
     my_grad = delta_sum[:heads] / my_scale
     scale_part = lax.dynamic_update_slice(
         jnp.zeros((head_count,), F32), my_grad, (my_index * heads,)
     )
-    gains = sum_small(
+    small = SmallSum(
         jnp.concatenate(
             [grad_ln_attn[0], sum(g_post)[0], sum(g_ffn)[0], sum(g_mid)[0], scale_part]
         )
     )
+    piece = model // PARTS
+    ff_piece = w_fc1.shape[1] // PARTS
+    trees = [tree_qkv, tree_three, tree_two, tree_one]
+    placed = None
+    while any(tree.steps for tree in trees + [small]):
+        combine([tree for tree in trees if tree.steps])
+
+        def place_early():
+            if tree_two.steps or tree_one.steps or placed is not None:
+                return ()
+            return place(
+                [tree_one, tree_two], [[(0, model, "rows")], [(0, ff_piece, "columns")]]
+            )
+
+        early_out = advance([tree for tree in trees + [small] if tree.steps], place_early)
+        placed = early_out or placed
+    if placed is None:
+        placed = place([tree_one, tree_two], [[(0, model, "rows")], [(0, ff_piece, "columns")]])
+    grad_fc2, grad_fc1 = placed
+    *grads_qkv, grad_out = place(
+        [tree_qkv, tree_three],
+        [[(n * piece, piece, "columns") for n in range(3)], [(0, piece, "columns")]],
+    )
+    gains = small.mine
     ends = [0, model, 2 * model, 3 * model, 3 * model + ln_mid.shape[0]]
     ends.append(ends[-1] + head_count)
     gains = [gains[low:high] for low, high in zip(ends[:-1], ends[1:])]
@@ -848,25 +1145,20 @@
         part = vector.shape[0] // group
         return lax.dynamic_slice(vector, (my_index * part,), (part,))
 
-    def whole(parts, start, width, axis=1):
-        return jnp.concatenate([part[:, start : start + width] for part in parts], axis=axis)
-
-    piece = model // PARTS
-    ff_piece = w_fc1.shape[1] // PARTS
     return (
         layer_out,
         grad_inputs,
         shard_of(gains[0]),
-        whole(grads_qkv, 0, piece),
-        whole(grads_qkv, piece, piece),
-        whole(grads_qkv, 2 * piece, piece),
-        whole(grads_ffn, model + ff_piece, piece),
+        grads_qkv[0],
+        grads_qkv[1],
+        grads_qkv[2],
+        grad_out,
         gains[4],
         shard_of(gains[1]),
         shard_of(gains[2]),
-        whole(grads_ffn, model, ff_piece),
+        grad_fc1,
         shard_of(gains[3]),
-        whole(grads_ffn, 0, model, 0),
+        grad_fc2,
     )
 
 

time: 709 us -> 639 us (0.901)
  waiting for transfers between devices: 225 us -> 167 us
  local copies, waits for them, and re-layouts: 41.1 us -> 13.4 us
  Pallas kernels: 319 us -> 334 us
  other arithmetic: 16.9 us -> 9.09 us
    ppermute x25 -> x41, waiting for transfers between devices: 157 us -> 105 us  [flip(): return lax.ppermute(value, axis, [(i, i ^ 1 << bit) for i in range(size)])]
    unnamed x176 -> x92, local copies, waits for them, and re-layouts: 26.3 us -> 2.71 us
    pallas_call x7 -> x16, Pallas kernels: 80.4 us -> 104 us  [the longest x3 56.2 us: layer(): pl.pallas_call(functools.partial(layer_kernel, slot=slot), grid_spec=pltp...]
    pallas_call x12 -> x16, Pallas kernels: 83.9 us -> 77.9 us  [weight_part(): pl.pallas_call(functools.partial(weight_kernel, len(pairs), len(pairs[0][...]
    ppermute x25 -> x41, starting transfers between devices: 29.1 us -> 30.6 us  [flip(): return lax.ppermute(value, axis, [(i, i ^ 1 << bit) for i in range(size)])]
  transfers between devices with their start and end apart: 35 -> 51, of which waited for: 19 -> 22; matrix products, arithmetic and copies ran while one was open for 5% -> 2% of each run, Pallas kernels for 40% -> 45%
where the time goes in v3:
time: 639 us; the launch traced here: 630 us
  Pallas kernels  334 us (52%)
  waiting for transfers between devices  167 us (26%)
  starting transfers between devices  83.9 us (13%)
  local copies, waits for them, and re-layouts  13.4 us (2%)
  matrix products  12.3 us (2%)
  other arithmetic  9.09 us (1%)
  between operations  8.47 us (1%)
    ppermute x41, waiting for transfers between devices, flip(): return lax.ppermute(value, axis, [(i, i ^ 1 << bit) for i in range(size)])  105 us
    pallas_call x3, Pallas kernels, attend_back(): pl.pallas_call(functools.partial(attend_back_kernel, rows, heads, head_di...  82.5 us
    pallas_call x16, Pallas kernels, weight_part(): pl.pallas_call(functools.partial(weight_kernel, len(pairs), len(pairs[0][...  77.9 us
    all_to_all x10, waiting for transfers between devices, exchange(): return lax.all_to_all(parts, 'blk', 0, 0, tiled=True)  61.9 us
    pallas_call x3, Pallas kernels, layer(): pl.pallas_call(functools.partial(layer_kernel, slot=slot), grid_spec=pltp...  56.2 us
    all_to_all x10, starting transfers between devices, exchange(): return lax.all_to_all(parts, 'blk', 0, 0, tiled=True)  53.3 us
    pallas_call x3, Pallas kernels, attend(): pl.pallas_call(functools.partial(attend_kernel, rows, heads, head_dim), i...  51.3 us
    ppermute x41, starting transfers between devices, flip(): return lax.ppermute(value, axis, [(i, i ^ 1 << bit) for i in range(size)])  30.6 us
  transfers between devices with their start and end apart: 51, of which 22 were waited for; matrix products, arithmetic and copies ran while one was open for 2% of the time, Pallas kernels for 45%

profile of v3, /device:TPU:0, one launch (start us, length us, event | category | flops | bytes accessed | tf_op | source)
XLA Modules:
  0.0 630.0 jit_solution(11458731622823367760)
XLA Ops:
  16.0 44.4 %conditional.16 = (bf16[8,3,256,128]{3,2,1,0:T(8,128)(2,1)}, bf16[256,1024]{1,0:T(8,128)(2,1)}, bf16[8,3,256,128]{3,2,1,0:T(8,128)(2,1)}, bf16[256,1024]{1,0:T(8,128)(2,1)}, bf16[8,3,256,128]{3,2,1,0:T(8,128)(2,1)}) conditional(s32[]{:T(128)} %bitcast.18, () %tuple.168, (bf16[8,3,256,128]{3,2,1,0:T(8,128)(2,1)}, bf16[3,256,1024]{2,1,0:T(8,128)(2,1)S(1)}, ...), branch_computations={%region_3.4_spmd, %region_4.5_spmd} | conditional | bytes 29886620 | solution.py:688
  33.7 26.7 %all-to-all-done = bf16[8,3,256,128]{3,2,1,0:T(8,128)(2,1)} async-done(((bf16[8,3,256,128]{3,2,1,0:T(8,128)(2,1)}), bf16[8,3,256,128]{3,2,1,0:T(8,128)(2,1)}, u32[]{:S(2)}, u32[]{:S(2)}) %all-to-all-start) | async-done | bytes 1572896 | tf_op jit(solution)/shard_map/cond/branch_1_fun/all_to_all | solution.py:42
  60.4 41.7 %conditional.17 = (bf16[8,3,256,128]{3,2,1,0:T(8,128)(2,1)}, bf16[8,1,256,128]{3,2,1,0:T(8,128)(2,1)S(1)}, f32[1,8,2,256]{3,2,1,0:T(2,128)S(1)}, f32[768,4096]{1,0:T(8,128)}) conditional(s32[]{:T(128)} %bitcast.18, () %tuple.167, (bf16[8,3,256,128]{3,2,1,0:T(8,128)(2,1)}, s32[3]{0:T(128)S(1)}, s32[3,4]{1,0:T(4,128)S(1)}, f32[1,128]{1,0:T(1,128)S(1)}, ...), branch_computations={%region_5.6_spmd, %region_6.7_spmd} | conditional | flops 6442450944 | bytes 27264064 | solution.py:688
  65.0 19.4 %attend.3 = (bf16[8,1,256,128]{3,2,1,0:T(8,128)(2,1)S(1)}, f32[1,8,2,256]{3,2,1,0:T(2,128)S(1)}) custom-call(s32[3]{0:T(128)S(1)} %get-tuple-element.381.order_ref, s32[3,4]{1,0:T(4,128)S(1)} %get-tuple-element.382.offs_ref, f32[1,128]{1,0:T(1,128)S(1)} %get-tuple-element.383.scale_ref, bf16[8,3,256,128]{3,2,1,0:T(8,128)(2,1)} %get-tuple-element.384.refs_0_), custom_call_target="tpu_custom_call" | custom-call | bytes 1024 | tf_op jit(solution)/shard_map/cond/branch_1_fun/attend/pallas_call | solution.py:222
  102.1 41.0 %conditional.18 = (bf16[8,3,256,128]{3,2,1,0:T(8,128)(2,1)}, bf16[8,1,256,128]{3,2,1,0:T(8,128)(2,1)}, f32[1,8,2,256]{3,2,1,0:T(2,128)S(1)}) conditional(s32[]{:T(128)} %bitcast.18, () %tuple.171, (bf16[8,3,256,128]{3,2,1,0:T(8,128)(2,1)}, s32[3]{0:T(128)S(1)}, s32[3,4]{1,0:T(4,128)S(1)}, f32[1,128]{1,0:T(1,128)S(1)}, ...), branch_computations={%region_7.8_spmd, %region_8.9_spmd} | conditional | bytes 4719672 | solution.py:688
  106.4 16.7 %attend.4 = (bf16[8,1,256,128]{3,2,1,0:T(8,128)(2,1)}, f32[1,8,2,256]{3,2,1,0:T(2,128)S(1)}) custom-call(s32[3]{0:T(128)S(1)} %get-tuple-element.390.order_ref, s32[3,4]{1,0:T(4,128)S(1)} %get-tuple-element.391.offs_ref, f32[1,128]{1,0:T(1,128)S(1)} %get-tuple-element.392.scale_ref, bf16[8,3,256,128]{3,2,1,0:T(8,128)(2,1)} %get-tuple-element.393.refs_0_), custom_call_target="tpu_custom_call" | custom-call | bytes 1024 | tf_op jit(solution)/shard_map/cond/branch_1_fun/attend/pallas_call | solution.py:222
  123.1 20.0 %all-to-all-done.1 = bf16[8,3,256,128]{3,2,1,0:T(8,128)(2,1)} async-done(((bf16[8,3,256,128]{3,2,1,0:T(8,128)(2,1)}), bf16[8,3,256,128]{3,2,1,0:T(8,128)(2,1)}, u32[]{:S(2)}, u32[]{:S(2)}) %all-to-all-start.1) | async-done | bytes 1572896 | tf_op jit(solution)/shard_map/cond/branch_1_fun/all_to_all | solution.py:42
  143.1 32.0 %conditional.19 = (bf16[8,2,256,128]{3,2,1,0:T(8,128)(2,1)}, bf16[8,1,256,128]{3,2,1,0:T(8,128)(2,1)}, f32[1,8,2,256]{3,2,1,0:T(2,128)S(1)}) conditional(s32[]{:T(128)} %bitcast.18, () %tuple.166, (bf16[8,1,256,128]{3,2,1,0:T(8,128)(2,1)S(1)}, bf16[8,1,256,128]{3,2,1,0:T(8,128)(2,1)}, s32[3]{0:T(128)S(1)}, s32[3,4]{1,0:T(4,128)S(1)}, ...), branch_computations={%region_9.10_spmd, %region_10.11_spmd} | conditional | flops 524288 | bytes 5243960 | solution.py:688
  175.1 22.1 %conditional.20 = (bf16[8,1,256,128]{3,2,1,0:T(8,128)(2,1)}, bf16[256,1024]{1,0:T(8,128)(2,1)}, bf16[256,1024]{1,0:T(8,128)(2,1)}, f32[256,1024]{1,0:T(8,128)}, ...) conditional(s32[]{:T(128)} %bitcast.18, () %tuple.165, ...), branch_computations={%region_11.12_spmd, %region_12.13_spmd} | conditional | bytes 8937602 | solution.py:688
  179.5 17.5 %layer.3 = (bf16[256,1024]{1,0:T(8,128)(2,1)}, bf16[256,1024]{1,0:T(8,128)(2,1)}, f32[256,1024]{1,0:T(8,128)}, bf16[256,4096]{1,0:T(8,128)(2,1)}, bf16[256,4096]...) custom-call(s32[3]{0:T(128)S(1)} %get-tuple-element.405.order_ref, ...), custom_call_target="tpu_custom_call" | custom-call | bytes 1024 | tf_op jit(solution)/shard_map/cond/branch_1_fun/layer/pallas_call | solution.py:492
  197.2 45.0 %conditional.21 = (bf16[8,1,256,128]{3,2,1,0:T(8,128)(2,1)}, bf16[256,1024]{1,0:T(8,128)(2,1)S(1)}, bf16[256,1024]{1,0:T(8,128)(2,1)}, f32[256,1024]{1,0:T(8,128...) conditional(s32[]{:T(128)} %bitcast.18, () %tuple.175, ...), branch_computations={%region_13.14_spmd, %region_14.15_spmd} | conditional | bytes 33032484 | solution.py:688
  203.2 18.7 %layer.4 = (bf16[256,1024]{1,0:T(8,128)(2,1)S(1)}, bf16[256,1024]{1,0:T(8,128)(2,1)}, f32[256,1024]{1,0:T(8,128)}, bf16[256,4096]{1,0:T(8,128)(2,1)}, bf16[256,4...) custom-call(s32[3]{0:T(128)S(1)} %get-tuple-element.428.order_ref, ...), custom_call_target="tpu_custom_call" | custom-call | bytes 1024 | tf_op jit(solution)/shard_map/cond/branch_1_fun/layer/pallas_call | solution.py:492
  222.0 20.0 %layer.5 = (bf16[256,1024]{1,0:T(8,128)(2,1)}, bf16[256,1024]{1,0:T(8,128)(2,1)}, f32[256,1024]{1,0:T(8,128)}, bf16[256,4096]{1,0:T(8,128)(2,1)}, bf16[256,4096]...) custom-call(s32[3]{0:T(128)S(1)} %get-tuple-element.428.order_ref, ...), custom_call_target="tpu_custom_call" | custom-call | bytes 1024 | tf_op jit(solution)/shard_map/cond/branch_1_fun/layer/pallas_call | solution.py:492
  262.5 57.9 %conditional.22 = (bf16[8,128,1024]{2,1,0:T(8,128)(2,1)}, bf16[8,2,256,128]{3,2,1,0:T(8,128)(2,1)}, bf16[8,1,3,256,128]{4,3,2,1,0:T(8,128)(2,1)}, bf16[8,128,102...) conditional(s32[]{:T(128)} %bitcast.18, () %tuple.164, (bf16[8,128,1024]{2,1,0:T(8,128)(2,1)}, ...), branch_computations={%region_15.16_spmd, %region_16.18_spmd} | conditional | flops 526462 | bytes 53490100 | solution.py:688
  280.2 34.4 %attend_back.3 = (bf16[8,1,3,256,128]{4,3,2,1,0:T(8,128)(2,1)}, f32[1,8,256]{2,1,0:T(8,128)S(1)}) custom-call(s32[3]{0:T(128)S(1)} %get-tuple-element.466.order_ref, s32[3,4]{1,0:T(4,128)S(1)} %get-tuple-element.467.offs_ref, f32[1,128]{1,0:T(1,128)S(1)} %broadcast_divide_fusion.inv_ref, bf16[8,1,256,128]{3,2,1,0:T(8,128)(2,1)} %get-tuple-element.469.grad_ref, ...), custom_call_target="tpu_custom_call" | custom-call | bytes 1024 | tf_op jit(solution)/shard_map/cond/branch_1_fun/attend_back/pallas_call | solution.py:338
  320.4 53.5 %conditional.23 = (bf16[8,1,3,256,128]{4,3,2,1,0:T(8,128)(2,1)}, bf16[8,1,3,256,128]{4,3,2,1,0:T(8,128)(2,1)}, bf16[8,128,1024]{2,1,0:T(8,128)(2,1)}, bf16[8,128...) conditional(s32[]{:T(128)} %bitcast.18, () %tuple.163, ...), branch_computations={%region_18.19_spmd, %region_19.21_spmd} | conditional | flops 2173 | bytes 27799900 | solution.py:688
  327.1 26.5 %attend_back.4 = (bf16[8,1,3,256,128]{4,3,2,1,0:T(8,128)(2,1)}, f32[1,8,256]{2,1,0:T(8,128)S(1)}) custom-call(s32[3]{0:T(128)S(1)} %get-tuple-element.493.order_ref, s32[3,4]{1,0:T(4,128)S(1)} %get-tuple-element.494.offs_ref, f32[1,128]{1,0:T(1,128)S(1)} %broadcast_divide_fusion.1.inv_ref, bf16[8,2,256,128]{3,2,1,0:T(8,128)(2,1)} %get-tuple-element.496.grad_ref, ...), custom_call_target="tpu_custom_call" | custom-call | bytes 1024 | tf_op jit(solution)/shard_map/cond/branch_1_fun/attend_back/pallas_call | solution.py:338
  384.8 48.5 %conditional.24 = (bf16[8,1,3,256,128]{4,3,2,1,0:T(8,128)(2,1)}, bf16[4,128,1024]{2,1,0:T(8,128)(2,1)}, bf16[8,128,256]{2,1,0:T(8,128)(2,1)}, bf16[8,128,1024]{2...) conditional(s32[]{:T(128)} %bitcast.18, () %tuple.162, ...), branch_computations={%region_21.22_spmd, %region_22.24_spmd} | conditional | flops 2171 | bytes 19410200 | solution.py:688
  393.3 21.6 %attend_back.5 = (bf16[8,1,3,256,128]{4,3,2,1,0:T(8,128)(2,1)}, f32[1,8,256]{2,1,0:T(8,128)S(1)}) custom-call(s32[3]{0:T(128)S(1)} %get-tuple-element.526.order_ref, s32[3,4]{1,0:T(4,128)S(1)} %get-tuple-element.527.offs_ref, f32[1,128]{1,0:T(1,128)S(1)} %broadcast_divide_fusion.2.inv_ref, bf16[8,2,256,128]{3,2,1,0:T(8,128)(2,1)} %get-tuple-element.529.grad_ref, ...), custom_call_target="tpu_custom_call" | custom-call | bytes 1024 | tf_op jit(solution)/shard_map/cond/branch_1_fun/attend_back/pallas_call | solution.py:338
  444.2 46.3 %conditional.25 = (bf16[8,1,3,256,128]{4,3,2,1,0:T(8,128)(2,1)}, bf16[2,128,1024]{2,1,0:T(8,128)(2,1)}, bf16[4,128,1024]{2,1,0:T(8,128)(2,1)}, bf16[8,128,256]{2...) conditional(s32[]{:T(128)} %bitcast.18, () %tuple.161, ...), branch_computations={%region_24.25_spmd, %region_25.26_spmd} | conditional | bytes 38276388 | solution.py:688
  469.1 18.6 %collective-permute-done = bf16[2,128,1024]{2,1,0:T(8,128)(2,1)} collective-permute-done((bf16[2,128,1024]{2,1,0:T(8,128)(2,1)}, bf16[2,128,1024]{2,1,0:T(8,128)(2,1)}, u32[]{:S(2)}, u32[]{:S(2)}) %collective-permute-start) | collective-permute-done | bytes 524320 | tf_op jit(solution)/shard_map/cond/branch_1_fun/ppermute | solution.py:549
  513.7 37.4 %conditional.26 = (bf16[1,128,1024]{2,1,0:T(8,128)(2,1)}, bf16[2,128,1024]{2,1,0:T(8,128)(2,1)}, bf16[4,128,256]{2,1,0:T(8,128)(2,1)}, bf16[8,128,768]{2,1,0:T(8...) conditional(s32[]{:T(128)} %bitcast.18, () %tuple.184, ...), branch_computations={%region_26.27_spmd, %region_27.28_spmd} | conditional | bytes 16778496 | solution.py:688
  534.7 16.4 %collective-permute-done.6 = bf16[8,128,768]{2,1,0:T(8,128)(2,1)} collective-permute-done((bf16[8,128,768]{2,1,0:T(8,128)(2,1)}, bf16[8,128,768]{2,1,0:T(8,128)(2,1)}, u32[]{:S(2)}, u32[]{:S(2)}) %collective-permute-start.6) | collective-permute-done | bytes 1572896 | tf_op jit(solution)/shard_map/cond/branch_1_fun/ppermute | solution.py:549
  557.5 19.4 %conditional.27 = (bf16[4,128,768]{2,1,0:T(8,128)(2,1)}, bf16[2,128,256]{2,1,0:T(8,128)(2,1)}, bf16[1,128,1024]{2,1,0:T(8,128)(2,1)}, bf16[1,128,1024]{2,1,0:T(8,128)(2,1)}, f32[7184]{0:T(1024)}) conditional(s32[]{:T(128)} %bitcast.18, () %tuple.190, (bf16[4,128,768]{2,1,0:T(8,128)(2,1)S(1)}, bf16[2,128,256]{2,1,0:T(8,128)(2,1)S(1)}, ...), branch_computations={%region_28.29_spmd, %region_29.30_spmd} | conditional | bytes 5882352 | solution.py:688
  (309 shorter events, 402.9 us)
Async XLA Ops:
  16.0 44.4 %all-to-all-start = ((bf16[8,3,256,128]{3,2,1,0:T(8,128)(2,1)}), bf16[8,3,256,128]{3,2,1,0:T(8,128)(2,1)}, u32[]{:S(2)}, u32[]{:S(2)}) async-start(bf16[8,3,256,128]{3,2,1,0:T(8,128)(2,1)} %get-tuple-element.368), calls=%async_computation | async-start | bytes 3145728 | tf_op jit(solution)/shard_map/cond/branch_1_fun/all_to_all | solution.py:42
  60.4 41.2 %all-to-all-start.9 = ((bf16[8,3,256,128]{3,2,1,0:T(8,128)(2,1)}), bf16[8,3,256,128]{3,2,1,0:T(8,128)(2,1)}, u32[]{:S(2)}, u32[]{:S(2)}) async-start(bf16[8,3,256,128]{3,2,1,0:T(8,128)(2,1)} %get-tuple-element.380), calls=%async_computation.9 | async-start | bytes 3145728 | tf_op jit(solution)/shard_map/cond/branch_1_fun/all_to_all | solution.py:42
  102.1 40.9 %all-to-all-start.1 = ((bf16[8,3,256,128]{3,2,1,0:T(8,128)(2,1)}), bf16[8,3,256,128]{3,2,1,0:T(8,128)(2,1)}, u32[]{:S(2)}, u32[]{:S(2)}) async-start(bf16[8,3,256,128]{3,2,1,0:T(8,128)(2,1)} %get-tuple-element.389), calls=%async_computation.1 | async-start | bytes 3145728 | tf_op jit(solution)/shard_map/cond/branch_1_fun/all_to_all | solution.py:42
  145.2 29.9 %all-to-all-start.5 = ((bf16[8,2,256,128]{3,2,1,0:T(8,128)(2,1)}), bf16[8,2,256,128]{3,2,1,0:T(8,128)(2,1)}, u32[]{:S(2)}, u32[]{:S(2)}) async-start(bf16[8,2,256,128]{3,2,1,0:T(8,128)(2,1)} %pad_maximum_fusion), calls=%async_computation.5 | async-start | bytes 2097152 | tf_op jit(solution)/shard_map/cond/branch_1_fun/all_to_all | solution.py:42
  175.1 21.8 %all-to-all-start.2 = ((bf16[8,1,256,128]{3,2,1,0:T(8,128)(2,1)}), bf16[8,1,256,128]{3,2,1,0:T(8,128)(2,1)}, u32[]{:S(2)}, u32[]{:S(2)}) async-start(bf16[8,1,256,128]{3,2,1,0:T(8,128)(2,1)} %get-tuple-element.404), calls=%async_computation.2 | async-start | bytes 1048576 | tf_op jit(solution)/shard_map/cond/branch_1_fun/all_to_all | solution.py:42
  197.2 44.8 %all-to-all-start.3 = ((bf16[8,1,256,128]{3,2,1,0:T(8,128)(2,1)}), bf16[8,1,256,128]{3,2,1,0:T(8,128)(2,1)}, u32[]{:S(2)}, u32[]{:S(2)}) async-start(bf16[8,1,256,128]{3,2,1,0:T(8,128)(2,1)} %get-tuple-element.427), calls=%async_computation.3 | async-start | bytes 1048576 | tf_op jit(solution)/shard_map/cond/branch_1_fun/all_to_all | solution.py:42
  265.2 49.6 %collective-permute-start.28 = (bf16[8,128,1024]{2,1,0:T(8,128)(2,1)}, bf16[8,128,1024]{2,1,0:T(8,128)(2,1)S(1)}, u32[]{:S(2)}, u32[]{:S(2)}) collective-permute-start(bf16[8,128,1024]{2,1,0:T(8,128)(2,1)} %get-tuple-element.491), channel_id=1, source_target_pairs={{0,8},{8,0},{16,24},{24,16},{1,9},{9,1},{17,25},{25,17},{2,10},{10... | collective-permute-start | bytes 6291464 | tf_op jit(solution)/shard_map/cond/branch_1_fun/ppermute | solution.py:549
  266.0 54.3 %collective-permute-start.27 = (bf16[8,128,1024]{2,1,0:T(8,128)(2,1)}, bf16[8,128,1024]{2,1,0:T(8,128)(2,1)}, u32[]{:S(2)}, u32[]{:S(2)}) collective-permute-start(bf16[8,128,1024]{2,1,0:T(8,128)(2,1)} %get-tuple-element.463), channel_id=1, source_target_pairs={{0,16},{8,24},{16,0},{24,8},{1,17},{9,25},{17,1},{25,9},{2,18},{10... | collective-permute-start | bytes 6291464 | tf_op jit(solution)/shard_map/cond/branch_1_fun/ppermute | solution.py:549
  268.6 51.7 %all-to-all-start.6 = ((bf16[8,2,256,128]{3,2,1,0:T(8,128)(2,1)}), bf16[8,2,256,128]{3,2,1,0:T(8,128)(2,1)}, u32[]{:S(2)}, u32[]{:S(2)}) async-start(bf16[8,2,256,128]{3,2,1,0:T(8,128)(2,1)} %pad_maximum_fusion.1), calls=%async_computation.6 | async-start | bytes 2097152 | tf_op jit(solution)/shard_map/cond/branch_1_fun/all_to_all | solution.py:42
  320.4 53.5 %all-to-all-start.7 = ((bf16[8,1,3,256,128]{4,3,2,1,0:T(8,128)(2,1)}), bf16[8,1,3,256,128]{4,3,2,1,0:T(8,128)(2,1)}, u32[]{:S(2)}, u32[]{:S(2)}) async-start(bf16[8,1,3,256,128]{4,3,2,1,0:T(8,128)(2,1)} %get-tuple-element.492), calls=%async_computation.7 | async-start | bytes 3145728 | tf_op jit(solution)/shard_map/cond/branch_1_fun/all_to_all | solution.py:42
  326.5 47.3 %collective-permute-start.29 = (bf16[8,128,1024]{2,1,0:T(8,128)(2,1)}, bf16[8,128,1024]{2,1,0:T(8,128)(2,1)}, u32[]{:S(2)}, u32[]{:S(2)}) collective-permute-start(bf16[8,128,1024]{2,1,0:T(8,128)(2,1)} %get-tuple-element.501), channel_id=1, source_target_pairs={{0,16},{8,24},{16,0},{24,8},{1,17},{9,25},{17,1},{25,9},{2,18},{10... | collective-permute-start | bytes 6291464 | tf_op jit(solution)/shard_map/cond/branch_1_fun/ppermute | solution.py:549
  327.1 46.7 %collective-permute-start.30 = (bf16[8,128,1024]{2,1,0:T(8,128)(2,1)}, bf16[8,128,1024]{2,1,0:T(8,128)(2,1)}, u32[]{:S(2)}, u32[]{:S(2)}) collective-permute-start(bf16[8,128,1024]{2,1,0:T(8,128)(2,1)} %get-tuple-element.502), channel_id=1, source_target_pairs={{0,8},{8,0},{16,24},{24,16},{1,9},{9,1},{17,25},{25,17},{2,10},{10... | collective-permute-start | bytes 6291464 | tf_op jit(solution)/shard_map/cond/branch_1_fun/ppermute | solution.py:549
  384.8 48.3 %all-to-all-start.8 = ((bf16[8,1,3,256,128]{4,3,2,1,0:T(8,128)(2,1)}), bf16[8,1,3,256,128]{4,3,2,1,0:T(8,128)(2,1)}, u32[]{:S(2)}, u32[]{:S(2)}) async-start(bf16[8,1,3,256,128]{4,3,2,1,0:T(8,128)(2,1)} %get-tuple-element.520), calls=%async_computation.8 | async-start | bytes 3145728 | tf_op jit(solution)/shard_map/cond/branch_1_fun/all_to_all | solution.py:42
  390.7 42.4 %collective-permute-start.33 = (bf16[8,128,1024]{2,1,0:T(8,128)(2,1)}, bf16[8,128,1024]{2,1,0:T(8,128)(2,1)}, u32[]{:S(2)}, u32[]{:S(2)}) collective-permute-start(bf16[8,128,1024]{2,1,0:T(8,128)(2,1)} %get-tuple-element.523), channel_id=1, source_target_pairs={{0,8},{8,0},{16,24},{24,16},{1,9},{9,1},{17,25},{25,17},{2,10},{10... | collective-permute-start | bytes 6291464 | tf_op jit(solution)/shard_map/cond/branch_1_fun/ppermute | solution.py:549
  390.9 42.2 %collective-permute-start.31 = (bf16[4,128,1024]{2,1,0:T(8,128)(2,1)}, bf16[4,128,1024]{2,1,0:T(8,128)(2,1)}, u32[]{:S(2)}, u32[]{:S(2)}) collective-permute-start(bf16[4,128,1024]{2,1,0:T(8,128)(2,1)} %get-tuple-element.521), channel_id=1, source_target_pairs={{0,1},{1,0},{2,3},{3,2},{4,5},{5,4},{6,7},{7,6},{8,9},{9,8},{10,11... | collective-permute-start | bytes 3145736 | tf_op jit(solution)/shard_map/cond/branch_1_fun/ppermute | solution.py:549
  392.7 26.5 %collective-permute-start.32 = (bf16[8,128,256]{2,1,0:T(8,128)(2,1)}, bf16[8,128,256]{2,1,0:T(8,128)(2,1)}, u32[]{:S(2)}, u32[]{:S(2)}) collective-permute-start(bf16[8,128,256]{2,1,0:T(8,128)(2,1)} %get-tuple-element.522), channel_id=1, source_target_pairs={{0,16},{8,24},{16,0},{24,8},{1,17},{9,25},{17,1},{25,9},{2,18},{10... | collective-permute-start | bytes 1572872 | tf_op jit(solution)/shard_map/cond/branch_1_fun/ppermute | solution.py:549
  444.2 46.3 %all-to-all-start.4 = ((bf16[8,1,3,256,128]{4,3,2,1,0:T(8,128)(2,1)}), bf16[8,1,3,256,128]{4,3,2,1,0:T(8,128)(2,1)}, u32[]{:S(2)}, u32[]{:S(2)}) async-start(bf16[8,1,3,256,128]{4,3,2,1,0:T(8,128)(2,1)} %get-tuple-element.542), calls=%async_computation.4 | async-start | bytes 3145728 | tf_op jit(solution)/shard_map/cond/branch_1_fun/all_to_all | solution.py:42
  448.8 41.7 %collective-permute-start.1 = (bf16[4,128,1024]{2,1,0:T(8,128)(2,1)}, bf16[4,128,1024]{2,1,0:T(8,128)(2,1)}, u32[]{:S(2)}, u32[]{:S(2)}) collective-permute-start(bf16[4,128,1024]{2,1,0:T(8,128)(2,1)} %get-tuple-element.544), channel_id=1, source_target_pairs={{0,1},{1,0},{2,3},{3,2},{4,5},{5,4},{6,7},{7,6},{8,9},{9,8},{10,11... | collective-permute-start | bytes 3145736 | tf_op jit(solution)/shard_map/cond/branch_1_fun/ppermute | solution.py:549
  450.8 36.9 %collective-permute-start = (bf16[2,128,1024]{2,1,0:T(8,128)(2,1)}, bf16[2,128,1024]{2,1,0:T(8,128)(2,1)}, u32[]{:S(2)}, u32[]{:S(2)}) collective-permute-start(bf16[2,128,1024]{2,1,0:T(8,128)(2,1)} %get-tuple-element.543), channel_id=1, source_target_pairs={{0,2},{1,3},{2,0},{3,1},{4,6},{5,7},{6,4},{7,5},{8,10},{9,11},{10,... | collective-permute-start | bytes 1572872 | tf_op jit(solution)/shard_map/cond/branch_1_fun/ppermute | solution.py:549
  452.3 35.5 %collective-permute-start.2 = (bf16[8,128,256]{2,1,0:T(8,128)(2,1)}, bf16[8,128,256]{2,1,0:T(8,128)(2,1)}, u32[]{:S(2)}, u32[]{:S(2)}) collective-permute-start(bf16[8,128,256]{2,1,0:T(8,128)(2,1)} %get-tuple-element.545), channel_id=1, source_target_pairs={{0,8},{8,0},{16,24},{24,16},{1,9},{9,1},{17,25},{25,17},{2,10},{10... | collective-permute-start | bytes 1572872 | tf_op jit(solution)/shard_map/cond/branch_1_fun/ppermute | solution.py:549
  514.0 37.2 %collective-permute-start.6 = (bf16[8,128,768]{2,1,0:T(8,128)(2,1)}, bf16[8,128,768]{2,1,0:T(8,128)(2,1)}, u32[]{:S(2)}, u32[]{:S(2)}) collective-permute-start(bf16[8,128,768]{2,1,0:T(8,128)(2,1)} %get-tuple-element.561), channel_id=1, source_target_pairs={{0,16},{8,24},{16,0},{24,8},{1,17},{9,25},{17,1},{25,9},{2,18},{10... | collective-permute-start | bytes 4718600 | tf_op jit(solution)/shard_map/cond/branch_1_fun/ppermute | solution.py:549
  514.7 36.5 %collective-permute-start.7 = (bf16[8,128,768]{2,1,0:T(8,128)(2,1)}, bf16[8,128,768]{2,1,0:T(8,128)(2,1)}, u32[]{:S(2)}, u32[]{:S(2)}) collective-permute-start(bf16[8,128,768]{2,1,0:T(8,128)(2,1)} %get-tuple-element.562), channel_id=1, source_target_pairs={{0,8},{8,0},{16,24},{24,16},{1,9},{9,1},{17,25},{25,17},{2,10},{10... | collective-permute-start | bytes 4718600 | tf_op jit(solution)/shard_map/cond/branch_1_fun/ppermute | solution.py:549
  514.9 19.9 %collective-permute-start.4 = (bf16[2,128,1024]{2,1,0:T(8,128)(2,1)S(1)}, bf16[2,128,1024]{2,1,0:T(8,128)(2,1)}, u32[]{:S(2)}, u32[]{:S(2)}) collective-permute-start(bf16[2,128,1024]{2,1,0:T(8,128)(2,1)S(1)} %get-tuple-element.559), channel_id=1, source_target_pairs={{0,2},{1,3},{2,0},{3,1},{4,6},{5,7},{6,4},{7,5},{8,10},{9,11},{10,... | collective-permute-start | bytes 1572872 | tf_op jit(solution)/shard_map/cond/branch_1_fun/ppermute | solution.py:549
  557.6 19.3 %collective-permute-start.8 = (bf16[4,128,768]{2,1,0:T(8,128)(2,1)S(1)}, bf16[4,128,768]{2,1,0:T(8,128)(2,1)}, u32[]{:S(2)}, u32[]{:S(2)}) collective-permute-start(bf16[4,128,768]{2,1,0:T(8,128)(2,1)S(1)} %get-tuple-element.577), channel_id=1, source_target_pairs={{0,1},{1,0},{2,3},{3,2},{4,5},{5,4},{6,7},{7,6},{8,9},{9,8},{10,11... | collective-permute-start | bytes 2359304 | tf_op jit(solution)/shard_map/cond/branch_1_fun/ppermute | solution.py:549
  (89 other events, 1114.8 us)
